TPU v7x, 32 devices: a whole 2x2x4 slice. The times are simulated.
32 devices in a mesh: fsdp: 16 (over z, y, x), tensor: 2 (over core).
Axes of the slice: x: 2, y: 2, z: 4, core: 2. Of those that a mesh axis runs over, the one named last changes fastest.
Arguments:
- tokens: bfloat16 [16384, 768], P(('fsdp', 'tensor'))
- cotangent: bfloat16 [16384, 768], P(('fsdp', 'tensor')), may hold values from -6 to 6
- prefix_len: int32 [16], P('fsdp'), may hold values from 102 to 512
- expert_ids: int32 [16384, 1], P('fsdp'), may hold values from 0 to 3
- norm_gains: bfloat16 [2, 768], P(None, 'fsdp'), may hold values from 0.5 to 1.5
- qkv_weight: bfloat16 [3, 768, 768], P(None, 'fsdp', 'tensor'), may hold values from -0.21875 to 0.21875
- out_weight: bfloat16 [768, 768], P('fsdp', 'tensor'), may hold values from -1.75 to 1.75
- router_weight: bfloat16 [4, 768], P(None, 'fsdp'), may hold values from -0.15625 to 0.15625
- up_weight: bfloat16 [4, 768, 3072], P(None, 'fsdp', 'tensor'), may hold values from -0.21875 to 0.21875
- down_weight: bfloat16 [4, 768, 3072], P(None, 'fsdp', 'tensor'), may hold values from -0.21875 to 0.21875
Outputs:
- block_out: bfloat16 [16384, 768], P(('fsdp', 'tensor'))
- tokens_grad: float32 [16384, 768], P(('fsdp', 'tensor'))
- gains_grad: float32 [2, 768], P(None, 'fsdp')
- qkv_grad: float32 [3, 768, 768], P(None, 'fsdp', 'tensor')
- out_grad: float32 [768, 768], P('fsdp', 'tensor')
- router_grad: float32 [4, 768], P(None, 'fsdp')
- up_grad: float32 [4, 768, 3072], P(None, 'fsdp', 'tensor')
- down_grad: float32 [4, 768, 3072], P(None, 'fsdp', 'tensor')
- balance_loss: float32 [], replicated
All inputs are finite; a program needn't handle non-finite values.
Results may differ from a plain program's by a relative error of at most 0.011.
Values may be sent and summed in bfloat16 or wider, within the bound.
A program may use at most 256 MiB of HBM per device.

v0:
```python
import math

import jax
import jax.numpy as jnp
from jax import lax
from jax.sharding import PartitionSpec as P

HEAD = 64
EXPERTS = 4
SEQ = 1024
CAP = 256


highest = lax.Precision.HIGHEST
norm_eps = 1e-05
balance_weight = 0.01
masked_score = -1e30


def softmax_rows(scores):
    row_max = jnp.max(scores, axis=-1, keepdims=True)
    shifted = jnp.exp(scores - row_max)
    return shifted / jnp.sum(shifted, axis=-1, keepdims=True)


def slot_index(group_ids):
    onehot = (group_ids[:, None] == jnp.arange(EXPERTS, dtype=jnp.int32)[None, :]).astype(jnp.int32)
    running = jnp.cumsum(onehot, axis=0)
    placed = jnp.sum(running * onehot, axis=1) - 1
    return jnp.where(placed < CAP, group_ids * CAP + placed, EXPERTS * CAP)


def rms_factor(values):
    return lax.rsqrt(jnp.mean(values * values, axis=-1, keepdims=True) + norm_eps)


def norm_back(grad_out, inputs, factor, gain):
    scaled = grad_out * gain
    row_inner = jnp.mean(scaled * inputs, axis=-1, keepdims=True)
    grad_in = factor * (scaled - inputs * factor * factor * row_inner)
    grad_gain = jnp.sum(grad_out * inputs * factor, axis=0)
    return (grad_in, grad_gain)


def gelu_slope(values):
    cumulative = 0.5 * (1.0 + lax.erf(values / math.sqrt(2.0)))
    density = jnp.exp(-0.5 * values * values) / math.sqrt(2.0 * math.pi)
    return cumulative + values * density


def block_scores(query_block, key_seq, offset, prefix, score_scale):
    scores = (
        jnp.einsum("qhd,khd->hqk", query_block, key_seq, preferred_element_type=jnp.float32)
        * score_scale
    )
    shape_pair = (query_block.shape[0], key_seq.shape[0])
    row_pos = offset + lax.broadcasted_iota(jnp.int32, shape_pair, 0)
    col_pos = lax.broadcasted_iota(jnp.int32, shape_pair, 1)
    allowed = (col_pos <= row_pos) | (col_pos < prefix)
    return jnp.where(allowed[None], scores, masked_score)


def attend(project, prefix_len, score_scale):
    group_rows = project.shape[0]
    full_width = project.shape[2]
    heads_here = full_width // HEAD
    block_rows = min(512, SEQ)
    shaped = project.reshape(group_rows, 3, heads_here, HEAD)
    query_all = shaped[:, 0]
    key_all = shaped[:, 1]
    value_all = shaped[:, 2]

    def one_block(number):
        row_start = number * block_rows
        seq_number = row_start // SEQ
        seq_start = seq_number * SEQ
        query_block = lax.dynamic_slice_in_dim(query_all, row_start, block_rows, 0)
        scores = block_scores(
            query_block, key_all, row_start - seq_start, prefix_len[seq_number], score_scale
        )
        row_max = jnp.max(scores, axis=-1, keepdims=True)
        shifted = jnp.exp(scores - row_max)
        row_total = jnp.sum(shifted, axis=-1, keepdims=True)
        prob_low = (shifted / row_total).astype(jnp.bfloat16)
        result = jnp.einsum("hqk,khd->qhd", prob_low, value_all, preferred_element_type=jnp.float32)
        return (
            result.reshape(block_rows, full_width).astype(jnp.bfloat16),
            (row_max + jnp.log(row_total))[..., 0],
        )

    outputs, log_total = lax.map(one_block, jnp.arange(group_rows // block_rows, dtype=jnp.int32))
    return (outputs.reshape(group_rows, full_width), log_total)


def attend_back(project, grad_att, log_total, prefix_len, score_scale):
    group_rows = project.shape[0]
    full_width = project.shape[2]
    heads_here = full_width // HEAD
    block_rows = min(512, SEQ)
    shaped = project.reshape(group_rows, 3, heads_here, HEAD)
    query_all = shaped[:, 0]
    key_all = shaped[:, 1]
    value_all = shaped[:, 2]
    grad_shaped = grad_att.reshape(group_rows, heads_here, HEAD)

    def one_block(carried, number):
        grad_keys, grad_values = carried
        row_start = number * block_rows
        seq_number = row_start // SEQ
        seq_start = seq_number * SEQ
        query_block = lax.dynamic_slice_in_dim(query_all, row_start, block_rows, 0)
        grad_block = lax.dynamic_slice_in_dim(grad_shaped, row_start, block_rows, 0)
        scores = block_scores(
            query_block, key_all, row_start - seq_start, prefix_len[seq_number], score_scale
        )
        prob_block = jnp.exp(scores - log_total[number][..., None])
        prob_low = prob_block.astype(jnp.bfloat16)
        grad_prob = jnp.einsum(
            "qhd,khd->hqk", grad_block, value_all, preferred_element_type=jnp.float32
        )
        value_part = jnp.einsum(
            "hqk,qhd->khd", prob_low, grad_block, preferred_element_type=jnp.float32
        )
        row_inner = jnp.sum(prob_block * grad_prob, axis=-1, keepdims=True)
        grad_scores = (prob_block * (grad_prob - row_inner)).astype(jnp.bfloat16)
        query_grad = (
            jnp.einsum("hqk,khd->qhd", grad_scores, key_all, preferred_element_type=jnp.float32)
            * score_scale
        )
        key_part = (
            jnp.einsum("hqk,qhd->khd", grad_scores, query_block, preferred_element_type=jnp.float32)
            * score_scale
        )
        old_keys = grad_keys
        grad_keys = old_keys + key_part
        old_values = grad_values
        grad_values = old_values + value_part
        return ((grad_keys, grad_values), query_grad)

    zero_rows = jnp.zeros((group_rows, heads_here, HEAD), jnp.float32)
    final, grad_query = lax.scan(
        one_block, (zero_rows, zero_rows), jnp.arange(group_rows // block_rows, dtype=jnp.int32)
    )
    grad_keys, grad_values = final
    stacked = jnp.stack(
        [
            grad_query.reshape(group_rows, full_width),
            grad_keys.reshape(group_rows, full_width),
            grad_values.reshape(group_rows, full_width),
        ],
        axis=1,
    )
    return stacked.astype(jnp.bfloat16)


def per_device(
    tokens,
    cotangent,
    prefix_len,
    expert_ids,
    norm_gains,
    qkv_weight,
    out_weight,
    router_weight,
    up_weight,
    down_weight,
):
    tensor_size = lax.axis_size("tensor")
    fsdp_size = lax.axis_size("fsdp")
    own_rows = tokens.shape[0]
    group_rows = own_rows * tensor_size
    all_tokens = group_rows * fsdp_size
    own_start = lax.axis_index("tensor") * own_rows
    score_scale = 1.0 / math.sqrt(HEAD)
    gains_full, qkv_full, out_stack = (
        lax.all_gather(norm_gains, "fsdp", axis=1, tiled=True),
        lax.all_gather(qkv_weight, "fsdp", axis=1, tiled=True),
        lax.all_gather(out_weight[None], "fsdp", axis=1, tiled=True),
    )
    out_full = out_stack[0]
    router_full, up_full, down_full = (
        lax.all_gather(router_weight, "fsdp", axis=1, tiled=True),
        lax.all_gather(up_weight, "fsdp", axis=1, tiled=True),
        lax.all_gather(down_weight, "fsdp", axis=1, tiled=True),
    )
    inputs = lax.all_gather(tokens, "tensor", axis=0, tiled=True)
    input_float = inputs.astype(jnp.float32)
    factor_one = rms_factor(input_float)
    gain_one = gains_full[0].astype(jnp.float32)
    normed_one = (input_float * factor_one * gain_one).astype(jnp.bfloat16)
    project = jnp.einsum(
        "td,sdw->tsw", normed_one, qkv_full, preferred_element_type=jnp.float32
    ).astype(jnp.bfloat16)
    attended, log_total = attend(project, prefix_len, score_scale)
    branch = lax.psum_scatter(
        lax.dot_general(
            attended, out_full, (((1,), (1,)), ((), ())), preferred_element_type=jnp.float32
        ),
        "tensor",
        scatter_dimension=0,
        tiled=True,
    )
    hidden_own = tokens.astype(jnp.float32) + branch
    hidden_group = lax.all_gather(hidden_own, "tensor", axis=0, tiled=True)
    factor_two = rms_factor(hidden_group)
    gain_two = gains_full[1].astype(jnp.float32)
    moe_input = (hidden_group * factor_two * gain_two).astype(jnp.bfloat16)
    logits = lax.dot_general(
        moe_input, router_full, (((1,), (1,)), ((), ())), preferred_element_type=jnp.float32
    )
    group_ids = expert_ids[:, 0]
    onehot = (group_ids[:, None] == jnp.arange(EXPERTS, dtype=jnp.int32)[None, :]).astype(
        jnp.float32
    )
    gate_value = jax.nn.sigmoid(jnp.sum(logits * onehot, axis=-1))
    router_prob = softmax_rows(logits)
    counts, prob_sums = lax.psum((jnp.sum(onehot, axis=0), jnp.sum(router_prob, axis=0)), "fsdp")
    route_share = counts / all_tokens
    balance_loss = EXPERTS * jnp.sum(route_share * prob_sums) / all_tokens
    slot_rows = slot_index(group_ids)
    model_width = moe_input.shape[1]
    dispatched = (
        jnp.zeros((EXPERTS * CAP, model_width), jnp.bfloat16)
        .at[slot_rows]
        .set(moe_input, mode="drop")
        .reshape(EXPERTS, CAP, model_width)
    )
    before = jnp.einsum("ecd,edf->ecf", dispatched, up_full, preferred_element_type=jnp.float32)
    activated = jax.nn.gelu(before, approximate=False).astype(jnp.bfloat16)
    expert_out = jnp.einsum(
        "ecf,edf->ecd", activated, down_full, preferred_element_type=jnp.float32
    ).reshape(EXPERTS * CAP, model_width)
    combined_part = jnp.concatenate([expert_out, jnp.zeros((1, model_width), jnp.float32)], axis=0)[
        slot_rows
    ]
    combined = lax.psum_scatter(combined_part, "tensor", scatter_dimension=0, tiled=True)
    gate_own = lax.dynamic_slice_in_dim(gate_value, own_start, own_rows, 0)
    block_out = (hidden_own + gate_own[:, None] * combined).astype(jnp.bfloat16)
    gains_back, qkv_back, out_again, router_back, up_back, down_back = (
        lax.all_gather(norm_gains, "fsdp", axis=1, tiled=True),
        lax.all_gather(qkv_weight, "fsdp", axis=1, tiled=True),
        lax.all_gather(out_weight[None], "fsdp", axis=1, tiled=True),
        lax.all_gather(router_weight, "fsdp", axis=1, tiled=True),
        lax.all_gather(up_weight, "fsdp", axis=1, tiled=True),
        lax.all_gather(down_weight, "fsdp", axis=1, tiled=True),
    )
    out_back = out_again[0]
    cot_group = lax.all_gather(cotangent, "tensor", axis=0, tiled=True).astype(jnp.float32)
    grad_combined = (gate_value[:, None] * cot_group).astype(jnp.bfloat16)
    gate_grad_own = jnp.sum(cotangent.astype(jnp.float32) * combined, axis=-1)
    gate_grad_placed = lax.dynamic_update_slice_in_dim(
        jnp.zeros((group_rows,), jnp.float32), gate_grad_own, own_start, 0
    )
    grad_slots = (
        jnp.zeros((EXPERTS * CAP, model_width), jnp.bfloat16)
        .at[slot_rows]
        .set(grad_combined, mode="drop")
        .reshape(EXPERTS, CAP, model_width)
    )
    grad_activated = jnp.einsum(
        "ecd,edf->ecf", grad_slots, down_back, preferred_element_type=jnp.float32
    )
    down_grad = jnp.einsum(
        "ecd,ecf->edf", grad_slots, activated, preferred_element_type=jnp.float32
    )
    grad_before = (grad_activated * gelu_slope(before)).astype(jnp.bfloat16)
    up_grad = jnp.einsum(
        "ecd,ecf->edf", dispatched, grad_before, preferred_element_type=jnp.float32
    )
    grad_dispatched = jnp.einsum(
        "ecf,edf->ecd", grad_before, up_back, preferred_element_type=jnp.float32
    ).reshape(EXPERTS * CAP, model_width)
    grad_input_part = jnp.concatenate(
        [grad_dispatched, jnp.zeros((1, model_width), jnp.float32)], axis=0
    )[slot_rows]
    grad_moe, gate_grad = lax.psum((grad_input_part, gate_grad_placed), "tensor")
    gate_slope = gate_value * (1.0 - gate_value)
    mixed_share = jnp.sum(router_prob * route_share[None, :], axis=-1, keepdims=True)
    logit_grad = onehot * (gate_grad * gate_slope)[
        :, None
    ] + balance_weight * EXPERTS / all_tokens * router_prob * (route_share[None, :] - mixed_share)
    grad_norm_two = grad_moe + jnp.dot(
        logit_grad, router_back.astype(jnp.float32), precision=highest
    )
    router_grad = jnp.dot(logit_grad.T, moe_input.astype(jnp.float32), precision=highest)
    grad_hidden, gain_two_grad = norm_back(
        grad_norm_two, hidden_group, factor_two, gains_back[1].astype(jnp.float32)
    )
    grad_hidden = grad_hidden + cot_group
    grad_branch = grad_hidden.astype(jnp.bfloat16)
    grad_att = jnp.dot(grad_branch, out_back, preferred_element_type=jnp.float32).astype(
        jnp.bfloat16
    )
    out_grad = lax.dot_general(
        grad_branch, attended, (((0,), (0,)), ((), ())), preferred_element_type=jnp.float32
    )
    grad_project = attend_back(project, grad_att, log_total, prefix_len, score_scale)
    qkv_grad = jnp.einsum(
        "td,tsw->sdw", normed_one, grad_project, preferred_element_type=jnp.float32
    )
    grad_normed_part = jnp.einsum(
        "tsw,sdw->td", grad_project, qkv_back, preferred_element_type=jnp.float32
    )
    grad_normed = lax.psum(grad_normed_part, "tensor")
    grad_tokens, gain_one_grad = norm_back(
        grad_normed, input_float, factor_one, gains_back[0].astype(jnp.float32)
    )
    grad_tokens = grad_tokens + grad_hidden
    tokens_grad = lax.dynamic_slice_in_dim(grad_tokens, own_start, own_rows, 0)
    gains_own, qkv_own, out_own, router_own, up_own, down_own = (
        lax.psum_scatter(
            jnp.stack([gain_one_grad, gain_two_grad], axis=0),
            "fsdp",
            scatter_dimension=1,
            tiled=True,
        ),
        lax.psum_scatter(qkv_grad, "fsdp", scatter_dimension=1, tiled=True),
        lax.psum_scatter(out_grad[None], "fsdp", scatter_dimension=1, tiled=True),
        lax.psum_scatter(router_grad, "fsdp", scatter_dimension=1, tiled=True),
        lax.psum_scatter(up_grad, "fsdp", scatter_dimension=1, tiled=True),
        lax.psum_scatter(down_grad, "fsdp", scatter_dimension=1, tiled=True),
    )
    return (
        block_out,
        tokens_grad,
        gains_own,
        qkv_own,
        out_own[0],
        router_own,
        up_own,
        down_own,
        balance_loss,
    )


def solution(mesh):
    placed = (
        P(("fsdp", "tensor"), None),
        P(("fsdp", "tensor"), None),
        P("fsdp"),
        P("fsdp", None),
        P(None, "fsdp"),
        P(None, "fsdp", "tensor"),
        P("fsdp", "tensor"),
        P(None, "fsdp"),
        P(None, "fsdp", "tensor"),
        P(None, "fsdp", "tensor"),
    )
    return jax.shard_map(
        per_device,
        mesh=mesh,
        in_specs=placed,
        out_specs=(
            P(("fsdp", "tensor"), None),
            P(("fsdp", "tensor"), None),
            P(None, "fsdp"),
            P(None, "fsdp", "tensor"),
            P("fsdp", "tensor"),
            P(None, "fsdp"),
            P(None, "fsdp", "tensor"),
            P(None, "fsdp", "tensor"),
            P(),
        ),
        check_vma=False,
    )
```

profile of v0, /device:TPU:0, one launch (start us, length us, event | category | flops | bytes accessed | tf_op | source)
XLA Modules:
  0.0 1811.8 jit_solution(11943425897177358683)
XLA Ops:
  8.7 42.4 %all-gather.1 = bf16[16,48,2]{1,2,0:T(2,128)(2,1)S(1)} all-gather(bf16[1,48,2]{1,2,0:T(2,128)(2,1)} %bitcast.179), channel_id=1, replica_groups=mesh['fsdp'=16,'tensor'=2] {'fsdp'}, dimensions={0}, use_global_device_ids=true | all-gather | bytes 3264 | tf_op jit(solution)/shard_map/all_gather | solution.py:176
  51.2 43.0 %all-gather = bf16[768,384]{1,0:T(8,128)(2,1)} all-gather(bf16[48,384]{1,0:T(8,128)(2,1)} %param.20), channel_id=2, replica_groups=mesh['fsdp'=16,'tensor'=2] {'fsdp'}, dimensions={0}, use_global_device_ids=true | all-gather | bytes 626688 | tf_op jit(solution)/shard_map/all_gather | solution.py:178
  96.0 4.1 convolution_convert_fusion
  100.5 27.6 %while.31 = (s32[]{:T(128)}, bf16[2,512,384]{2,1,0:T(8,128)(2,1)}, f32[2,6,512]{2,1,0:T(8,128)S(1)}, s32[2]{0:T(128)S(1)}, s32[1]{0:T(128)}, /*index=5*/bf16[102...) while((s32[]{:T(128)}, bf16[2,512,384]{2,1,0:T(8,128)(2,1)}, ...), condition=%wide.region_4.5_spmd, body=%wide.region_1.4_spmd.sunk | while | flops 844298752 | bytes 43895676 | solution.py:91
  102.9 2.4 fusion.134
  105.3 3.6 fusion.135
  108.9 4.3 fusion.136
  116.6 2.4 fusion.134
  119.0 3.6 fusion.135
  122.7 4.3 fusion.136
  128.1 4.8 fusion.79
  133.0 9.1 reduce-scatter.12.cloned.1.call-done
  142.1 2.9 convert_add_fusion.1
  149.2 9.2 all-gather.14.cloned.1.call-done
  158.4 2.3 multiply_reduce_fusion.3
  161.3 6.9 scatter_custom_fusion
  168.1 116.8 %all-gather.16.cloned.1.call-done = bf16[4,768,1536]{2,1,0:T(8,128)(2,1)} async-done(((bf16[4,48,1536]{2,1,0:T(8,128)(2,1)}), bf16[4,768,1536]{2,1,0:T(8,128)(2,1)}) %all-gather.16.cloned.1.call-update) | async-done | bytes 9437200 | tf_op jit(solution)/shard_map/all_gather | solution.py:183
  284.9 7.4 fusion.58
  292.3 2.6 copy-done.16
  294.9 14.1 fusion.33
  309.1 99.4 %all-gather.18.cloned.1.call-done = bf16[4,768,1536]{2,1,0:T(8,128)(2,1)} async-done(((bf16[4,48,1536]{2,1,0:T(8,128)(2,1)}), bf16[4,768,1536]{2,1,0:T(8,128)(2,1)}) %all-gather.18.cloned.1.call-update) | async-done | bytes 9437200 | tf_op jit(solution)/shard_map/all_gather | solution.py:184
  408.4 5.2 fusion.80
  413.9 5.3 gather_fusion
  419.8 38.1 %all-gather.2 = bf16[16,48,4]{1,2,0:T(4,128)(2,1)S(1)} all-gather(bf16[1,48,4]{1,2,0:T(4,128)(2,1)S(1)} %bitcast.178), channel_id=1, replica_groups=mesh['fsdp'=16,'tensor'=2] {'fsdp'}, dimensions={0}, use_global_device_ids=true | all-gather | bytes 6528 | tf_op jit(solution)/shard_map/all_gather | solution.py:182
  460.2 6.5 scatter_custom_fusion.1
  466.8 8.0 fusion.39
  474.8 6.4 fusion.81
  481.4 5.3 gather_fusion.1
  486.8 36.8 %psum.37 = f32[4]{0:T(128)S(1)} all-reduce(f32[4]{0:T(128)S(1)} %get-tuple-element.330), channel_id=1, replica_groups=mesh['fsdp'=16,'tensor'=2] {'fsdp'}, use_global_device_ids=true, to_apply=%region_20.21 | all-reduce | flops 4 | bytes 32 | tf_op jit(solution)/shard_map/psum | solution.py:217
  524.4 3.3 multiply_reduce_fusion.4
  527.9 2.4 psum.36
  530.4 5.1 multiply_reduce_fusion.1
  539.8 81.5 %while.32 = (s32[]{:T(128)}, f32[1024,6,64]{0,2,1:T(8,128)}, f32[1024,6,64]{0,2,1:T(8,128)}, bf16[2,512,6,64]{1,3,2,0:T(8,128)(2,1)}, s32[2]{0:T(128)S(1)}, /*in...) while((s32[]{:T(128)}, f32[1024,6,64]{0,2,1:T(8,128)}, ...), condition=%wide.region_25.26_spmd.clone, body=%wide.region_23.25_spmd.clone.sunk | while | flops 2063661568 | bytes 179927728 | solution.py:141
  542.3 6.4 fusion.146
  550.5 7.7 multiply_reduce_fusion.8
  559.1 5.1 multiply_convert_fusion.5
  564.2 5.4 bitcast_add_fusion.4
  569.5 2.0 fusion.148
  572.4 7.6 bitcast_add_fusion.5
  582.3 6.4 fusion.146
  590.5 7.7 multiply_reduce_fusion.8
  599.1 5.1 multiply_convert_fusion.5
  604.2 5.8 bitcast_add_fusion.4
  610.0 2.0 fusion.148
  612.9 8.1 bitcast_add_fusion.5
  621.4 2.1 copy.40
  628.8 5.4 convolution_bitcast_fusion.1
  635.6 2.5 convolution_bitcast_fusion.3
  638.2 17.2 all-reduce.9.cloned.1.call-done
  655.4 5.4 fusion.50
  661.8 5.1 convolution_bitcast_fusion
  667.0 6.3 copy.45
  673.3 1.8 copy-done.10
  675.2 3.2 convolution_bitcast_fusion.2
  678.6 11.5 fusion.83
  690.2 11.5 fusion.82
  703.7 41.9 %psum.39 = f32[4]{0:T(128)S(1)} all-reduce(f32[4]{0:T(128)S(1)} %copy-done.45), channel_id=1, replica_groups=mesh['fsdp'=16,'tensor'=2] {'fsdp'}, use_global_device_ids=true, to_apply=%region_37.38 | all-reduce | flops 4 | bytes 32 | tf_op jit(solution)/shard_map/psum | solution.py:217
  746.9 36.0 %reduce-scatter.24.cloned.1.call-done = f32[48,4]{1,0:T(8,128)} async-done(((f32[768,4]{1,0:T(8,128)}), f32[48,4]{1,0:T(8,128)}) %reduce-scatter.24.cloned.1.call-update) | async-done | bytes 784
  784.4 3.4 dynamic-slice_add_fusion
  787.7 121.1 %reduce-scatter.22.cloned.1.call-done = f32[48,2]{1,0:T(8,128)} async-done(((f32[768,2]{1,0:T(8,128)}), f32[48,2]{1,0:T(8,128)}) %reduce-scatter.22.cloned.1.call-update) | async-done | bytes 400
  910.2 183.2 %all-reduce.11.cloned.1.call-done = f32[3,768,384]{2,0,1:T(4,128)} async-done(((f32[3,768,384]{2,0,1:T(4,128)}), f32[3,768,384]{2,0,1:T(4,128)}) %all-reduce.11.cloned.1.call-update) | async-done | bytes 3538960
  1095.1 126.7 %reduce-scatter.16.cloned.1.call-done = f32[1,48,384]{2,1,0:T(8,128)} async-done(((f32[1,768,384]{2,1,0:T(8,128)}), f32[1,48,384]{2,1,0:T(8,128)}) %reduce-scatter.16.cloned.1.call-update) | async-done | bytes 73744 | tf_op jit(solution)/shard_map/reduce_scatter | solution.py:318
  1221.8 291.0 %reduce-scatter.20.cloned.1.call-done = f32[4,48,1536]{2,1,0:T(8,128)} async-done(((f32[4,768,1536]{2,1,0:T(8,128)}), f32[4,48,1536]{2,1,0:T(8,128)}) %reduce-scatter.20.cloned.1.call-update) | async-done | bytes 1179664 | tf_op jit(solution)/shard_map/reduce_scatter | solution.py:321
  1512.8 291.1 %reduce-scatter.18.cloned.1.call-done = f32[4,48,1536]{2,1,0:T(8,128)} async-done(((f32[4,768,1536]{2,1,0:T(8,128)}), f32[4,48,1536]{2,1,0:T(8,128)}) %reduce-scatter.18.cloned.1.call-update) | async-done | bytes 1179664 | tf_op jit(solution)/shard_map/reduce_scatter | solution.py:320
  (239 shorter events, 43.7 us)
Async XLA Ops:
  7.2 87.0 %all-gather.10.cloned.1.call-start = ((), (), s32[]{:S(2)}) async-start(), calls=%async_computation.7 | async-start | bytes 2359296 | tf_op jit(solution)/shard_map/all_gather | solution.py:186
  7.9 88.1 %all-gather.12.cloned.1.call-start = ((), (), s32[]{:S(2)}) async-start(), calls=%async_computation.8 | async-start | bytes 1880064 | tf_op jit(solution)/shard_map/all_gather | solution.py:177
  8.7 133.4 %reduce-scatter.12.cloned.1.call-start = ((), (), s32[]{:S(2)}) async-start(), calls=%async_computation.9 | async-start | bytes 4718592 | tf_op jit(solution)/shard_map/reduce_scatter | solution.py:195
  51.2 48.9 %copy-start.39 = (f32[768]{0:T(1024)}, f32[768]{0:T(1024)S(1)}, u32[]{:S(2)}) copy-start(f32[768]{0:T(1024)S(1)} %get-tuple-element.332) | copy-start | bytes 9220
  96.0 4.2 copy-start.37
  128.1 4.9 copy-start.1
  128.1 4.9 copy-start.7
  128.1 4.9 copy-start.11
  132.9 14.5 copy-start.31
  133.0 25.5 %all-gather.14.cloned.1.call-start = ((), (), s32[]{:S(2)}) async-start(), calls=%async_computation.10 | async-start | bytes 4718592 | tf_op jit(solution)/shard_map/all_gather | solution.py:204
  145.0 140.0 %all-gather.16.cloned.1.call-start = ((), (), s32[]{:S(2)}) async-start(), calls=%async_computation.11 | async-start | bytes 10027008 | tf_op jit(solution)/shard_map/all_gather | solution.py:183
  145.6 262.9 %all-gather.18.cloned.1.call-start = ((), (), s32[]{:S(2)}) async-start(), calls=%async_computation.12 | async-start | bytes 10027008 | tf_op jit(solution)/shard_map/all_gather | solution.py:184
  146.1 314.1 %all-gather.20.cloned.1.call-start = ((), (), s32[]{:S(2)}) async-start(), calls=%async_computation.14 | async-start | bytes 2359296 | tf_op jit(solution)/shard_map/all_gather | solution.py:248
  146.9 377.5 %reduce-scatter.14.cloned.1.call-start = ((), (), s32[]{:S(2)}) async-start(), calls=%async_computation.13 | async-start | bytes 4718592 | tf_op jit(solution)/shard_map/reduce_scatter | solution.py:236
  158.4 2.8 copy-start.4
  292.3 2.6 copy-start.16
  309.1 104.6 %copy-start.14 = (bf16[4,256,1536]{2,1,0:T(8,128)(2,1)}, bf16[4,256,1536]{2,1,0:T(8,128)(2,1)S(1)}, u32[]{:S(2)}) copy-start(bf16[4,256,1536]{2,1,0:T(8,128)(2,1)S(1)} %fusion.33) | copy-start | bytes 9437188
  419.2 38.9 %copy-start.5 = (f32[1024,768]{1,0:T(8,128)S(1)}, f32[1024,768]{1,0:T(8,128)}, u32[]{:S(2)}) copy-start(f32[1024,768]{1,0:T(8,128)} %all-gather.14.cloned.1.call-done) | copy-start | bytes 9437188
  419.2 111.2 %all-reduce.7.cloned.1.call-start = ((), (), s32[]{:S(2)}) async-start(), calls=%async_computation.15 | async-start | bytes 6291456 | tf_op jit(solution)/shard_map/psum | solution.py:276
  466.8 8.0 copy-start.17
  474.8 6.4 copy-start.21
  486.7 43.6 %copy-start.6 = (f32[1024,768]{1,0:T(8,128)S(1)}, f32[1024,768]{1,0:T(8,128)}, u32[]{:S(2)}) copy-start(f32[1024,768]{1,0:T(8,128)} %all-gather.14.cloned.1.call-done) | copy-start | bytes 9437188
  486.7 168.7 %all-reduce.9.cloned.1.call-start = ((), (), s32[]{:S(2)}) async-start(), calls=%async_computation.16 | async-start | bytes 6291456 | tf_op jit(solution)/shard_map/psum | solution.py:304
  523.6 11.8 copy-start.47
  523.7 11.7 copy-start.42
  524.4 11.1 copy-start.29
  524.4 11.1 copy-start.33
  530.3 5.1 copy-start.35
  530.4 5.1 copy-start.19
  535.5 2.6 copy-start.20
  538.1 1.7 copy-start.2
  538.1 1.7 copy-start.8
  550.4 7.8 slice-start
  550.4 7.8 slice-start.1
  550.4 8.6 slice-start.2
  564.2 5.4 copy-start
  564.2 5.4 copy-start.24
  569.5 2.9 copy-start.15
  590.5 7.8 slice-start
  590.5 7.8 slice-start.1
  590.5 8.6 slice-start.2
  604.2 5.8 copy-start
  604.2 5.8 copy-start.24
  610.0 2.9 copy-start.15
  621.4 3.8 copy-start.3
  625.3 3.5 copy-start.22
  625.7 2.2 copy-start.26
  628.8 5.5 copy-start.41
  628.8 5.6 copy-start.30
  628.8 5.6 copy-start.43
  634.2 21.2 %copy-start.18 = (bf16[1024,768]{1,0:T(8,128)(2,1)S(1)}, bf16[1024,768]{1,0:T(8,128)(2,1)}, u32[]{:S(2)}) copy-start(bf16[1024,768]{1,0:T(8,128)(2,1)} %all-gather.10.cloned.1.call-done) | copy-start | bytes 4718596
  634.2 21.2 %copy-start.38 = (f32[1024]{0:T(1024)S(1)}, f32[1024]{0:T(1024)}, u32[]{:S(2)}) copy-start(f32[1024]{0:T(1024)} %copy-done.37) | copy-start | bytes 12292
  634.2 21.2 %copy-start.40 = (f32[768]{0:T(1024)S(1)}, f32[768]{0:T(1024)}, u32[]{:S(2)}) copy-start(f32[768]{0:T(1024)} %copy-done.39) | copy-start | bytes 9220
  634.3 148.6 %reduce-scatter.24.cloned.1.call-start = ((), (), s32[]{:S(2)}) async-start(), calls=%async_computation.21 | async-start | bytes 417792
  638.2 23.7 %copy-start.23 = (bf16[1024,1,384]{2,0,1:T(8,128)(2,1)S(1)}, bf16[1024,1,384]{2,0,1:T(8,128)(2,1)}, u32[]{:S(2)}) copy-start(bf16[1024,1,384]{2,0,1:T(8,128)(2,1)} %copy.41) | copy-start | bytes 2359300
  638.2 23.7 %copy-start.27 = (bf16[1024,1,384]{2,0,1:T(8,128)(2,1)S(1)}, bf16[1024,1,384]{2,0,1:T(8,128)(2,1)}, u32[]{:S(2)}) copy-start(bf16[1024,1,384]{2,0,1:T(8,128)(2,1)} %copy-done.26) | copy-start | bytes 2359300
  638.2 270.6 %reduce-scatter.22.cloned.1.call-start = ((), (), s32[]{:S(2)}) async-start(), calls=%async_computation.20 | async-start | bytes 417792
  661.8 431.7 %all-reduce.11.cloned.1.call-start = ((), (), s32[]{:S(2)}) async-start(), calls=%async_computation.22 | async-start | bytes 9437184
  673.3 1.9 copy-start.10
  673.3 548.5 %reduce-scatter.16.cloned.1.call-start = ((), (), s32[]{:S(2)}) async-start(), calls=%async_computation.17 | async-start | bytes 1253376 | tf_op jit(solution)/shard_map/reduce_scatter | solution.py:318
  678.4 834.4 %reduce-scatter.20.cloned.1.call-start = ((), (), s32[]{:S(2)}) async-start(), calls=%async_computation.19 | async-start | bytes 20054016 | tf_op jit(solution)/shard_map/reduce_scatter | solution.py:321
  690.2 1113.8 %reduce-scatter.18.cloned.1.call-start = ((), (), s32[]{:S(2)}) async-start(), calls=%async_computation.18 | async-start | bytes 20054016 | tf_op jit(solution)/shard_map/reduce_scatter | solution.py:320
  701.7 2.0 copy-start.45
  701.7 43.9 %copy-start.48 = (f32[4]{0:T(128)S(1)}, f32[4]{0:T(128)}, u32[]{:S(2)}) copy-start(f32[4]{0:T(128)} %copy-done.47) | copy-start | bytes 52
  (11 other events, 12.4 us)
Sparse Core Ops, SparseCore 0:
  9.6 12.4 all-gather.9
  24.8 62.7 all-gather.11
  133.0 8.9 reduce-scatter.11
  145.1 13.2 all-gather.13
  161.3 123.5 all-gather.15
  287.8 120.5 all-gather.17
  410.0 7.9 all-gather.19
  420.4 12.0 reduce-scatter.13
  486.8 19.0 all-reduce.6
  634.4 20.9 all-reduce.8
  660.1 122.7 reduce-scatter.23
  788.1 120.6 reduce-scatter.21
  914.6 178.8 all-reduce.10
  1099.3 122.4 reduce-scatter.15
  1229.0 283.8 reduce-scatter.19
  1520.0 283.9 reduce-scatter.17
where the time goes:
time: 1820 us; the launch traced here: 1810 us
  waiting for transfers between devices  1300 us (71%)
  blocking collectives  205 us (11%)
  matrix products  155 us (9%)
  other arithmetic  74.4 us (4%)
  local copies, waits for them, and re-layouts  48 us (3%)
    unnamed x19, waiting for transfers between devices  344 us
    reduce_scatter x1, waiting for transfers between devices, per_device(): lax.psum_scatter(up_grad, 'fsdp', scatter_dimension=1, tiled=True)  291 us
    reduce_scatter x1, waiting for transfers between devices, per_device(): lax.psum_scatter(down_grad, 'fsdp', scatter_dimension=1, tiled=True)  291 us
    reduce_scatter x1, waiting for transfers between devices, per_device(): lax.psum_scatter(out_grad[None], 'fsdp', scatter_dimension=1, tiled=True)  127 us
    all_gather x1, waiting for transfers between devices, per_device(): lax.all_gather(up_weight, 'fsdp', axis=1, tiled=True)  117 us
    all_gather x1, waiting for transfers between devices, per_device(): lax.all_gather(down_weight, 'fsdp', axis=1, tiled=True)  99.4 us
    psum x2, blocking collectives, per_device(): lax.psum((jnp.sum(onehot, axis=0), jnp.sum(router_prob, axis=0)), 'fsdp')  78.8 us
    all_gather x1, blocking collectives, per_device(): lax.all_gather(out_weight[None], 'fsdp', axis=1, tiled=True)  43 us
  transfers between devices with their start and end apart: 16, of which 11 were waited for; matrix products, arithmetic and copies ran while one was open for 7% of the time, Pallas kernels for 0%

commit v1 on v0

--- a/solution.py
+++ b/solution.py
@@ -25,7 +25,15 @@
 
 def slot_index(group_ids):
     onehot = (group_ids[:, None] == jnp.arange(EXPERTS, dtype=jnp.int32)[None, :]).astype(jnp.int32)
-    running = jnp.cumsum(onehot, axis=0)
+    rows = group_ids.shape[0]
+    earlier = lax.broadcasted_iota(jnp.int32, (rows, rows), 1) <= lax.broadcasted_iota(
+        jnp.int32, (rows, rows), 0
+    )
+    running = jnp.dot(
+        earlier.astype(jnp.bfloat16),
+        onehot.astype(jnp.bfloat16),
+        preferred_element_type=jnp.float32,
+    ).astype(jnp.int32)
     placed = jnp.sum(running * onehot, axis=1) - 1
     return jnp.where(placed < CAP, group_ids * CAP + placed, EXPERTS * CAP)
 
@@ -151,6 +159,12 @@
         axis=1,
     )
     return stacked.astype(jnp.bfloat16)
+
+
+def low_scatter(grad):
+    return lax.psum_scatter(
+        grad.astype(jnp.bfloat16), "fsdp", scatter_dimension=1, tiled=True
+    ).astype(jnp.float32)
 
 
 def per_device(
@@ -314,11 +328,11 @@
             scatter_dimension=1,
             tiled=True,
         ),
-        lax.psum_scatter(qkv_grad, "fsdp", scatter_dimension=1, tiled=True),
-        lax.psum_scatter(out_grad[None], "fsdp", scatter_dimension=1, tiled=True),
+        low_scatter(qkv_grad),
+        low_scatter(out_grad[None]),
         lax.psum_scatter(router_grad, "fsdp", scatter_dimension=1, tiled=True),
-        lax.psum_scatter(up_grad, "fsdp", scatter_dimension=1, tiled=True),
-        lax.psum_scatter(down_grad, "fsdp", scatter_dimension=1, tiled=True),
+        low_scatter(up_grad),
+        low_scatter(down_grad),
     )
     return (
         block_out,

time: 1820 us -> 1520 us (0.84)
  waiting for transfers between devices: 1300 us -> 1030 us
  matrix products: 155 us -> 125 us
    reduce_scatter x3, waiting for transfers between devices: 709 us -> 474 us  [low_scatter(): lax.psum_scatter(grad.astype(jnp.bfloat16), 'fsdp', scatter_dimension=1,...]
    unnamed x19, waiting for transfers between devices: 344 us -> 317 us
  transfers between devices with their start and end apart: 16 -> 16, of which waited for: 11 -> 11; matrix products, arithmetic and copies ran while one was open for 7% -> 9% of each run, Pallas kernels for 0% -> 0%
where the time goes in v1:
time: 1520 us; the launch traced here: 1510 us
  waiting for transfers between devices  1030 us (68%)
  blocking collectives  205 us (13%)
  matrix products  125 us (8%)
  other arithmetic  83.2 us (5%)
  local copies, waits for them, and re-layouts  39.7 us (3%)
  between operations  17.5 us (1%)
    reduce_scatter x3, waiting for transfers between devices, low_scatter(): lax.psum_scatter(grad.astype(jnp.bfloat16), 'fsdp', scatter_dimension=1,...  474 us
    unnamed x19, waiting for transfers between devices  317 us
    all_gather x1, waiting for transfers between devices, per_device(): lax.all_gather(up_weight, 'fsdp', axis=1, tiled=True)  117 us
    all_gather x1, waiting for transfers between devices, per_device(): lax.all_gather(down_weight, 'fsdp', axis=1, tiled=True)  99.4 us
    psum x2, blocking collectives, per_device(): lax.psum((jnp.sum(onehot, axis=0), jnp.sum(router_prob, axis=0)), 'fsdp')  78.7 us
    all_gather x1, blocking collectives, per_device(): lax.all_gather(out_weight[None], 'fsdp', axis=1, tiled=True)  43 us
    all_gather x1, blocking collectives, per_device(): lax.all_gather(norm_gains, 'fsdp', axis=1, tiled=True)  42.4 us
    all_gather x1, blocking collectives, per_device(): lax.all_gather(router_weight, 'fsdp', axis=1, tiled=True)  38.4 us
  transfers between devices with their start and end apart: 16, of which 11 were waited for; matrix products, arithmetic and copies ran while one was open for 9% of the time, Pallas kernels for 0%

profile of v1, /device:TPU:0, one launch (start us, length us, event | category | flops | bytes accessed | tf_op | source)
XLA Modules:
  0.0 1508.0 jit_solution(2672836378105426482)
XLA Ops:
  8.7 42.4 %all-gather.1 = bf16[16,48,2]{1,2,0:T(2,128)(2,1)S(1)} all-gather(bf16[1,48,2]{1,2,0:T(2,128)(2,1)} %bitcast.163), channel_id=1, replica_groups=mesh['fsdp'=16,'tensor'=2] {'fsdp'}, dimensions={0}, use_global_device_ids=true | all-gather | bytes 3264 | tf_op jit(solution)/shard_map/all_gather | solution.py:190
  51.2 43.0 %all-gather = bf16[768,384]{1,0:T(8,128)(2,1)} all-gather(bf16[48,384]{1,0:T(8,128)(2,1)} %param.20), channel_id=2, replica_groups=mesh['fsdp'=16,'tensor'=2] {'fsdp'}, dimensions={0}, use_global_device_ids=true | all-gather | bytes 626688 | tf_op jit(solution)/shard_map/all_gather | solution.py:192
  96.1 4.1 convolution_convert_fusion.2
  100.5 27.6 %while.31 = (s32[]{:T(128)}, bf16[2,512,384]{2,1,0:T(8,128)(2,1)}, f32[2,6,512]{2,1,0:T(8,128)S(1)}, s32[2]{0:T(128)S(1)}, s32[1]{0:T(128)}, /*index=5*/bf16[102...) while((s32[]{:T(128)}, bf16[2,512,384]{2,1,0:T(8,128)(2,1)}, ...), condition=%wide.region_4.5_spmd, body=%wide.region_1.4_spmd.sunk | while | flops 844298752 | bytes 43895176 | solution.py:99
  102.9 2.4 fusion.135
  105.3 3.6 fusion.136
  109.0 4.3 fusion.137
  116.7 2.4 fusion.135
  119.1 3.6 fusion.136
  122.7 4.3 fusion.137
  128.1 4.8 fusion.82
  133.1 9.1 reduce-scatter.12.cloned.1.call-done
  142.1 2.7 convert_add_fusion.1
  147.6 10.7 all-gather.14.cloned.1.call-done
  158.3 2.3 multiply_reduce_fusion.3
  161.1 6.9 scatter_custom_fusion
  168.0 116.8 %all-gather.16.cloned.1.call-done = bf16[4,768,1536]{2,1,0:T(8,128)(2,1)} async-done(((bf16[4,48,1536]{2,1,0:T(8,128)(2,1)}), bf16[4,768,1536]{2,1,0:T(8,128)(2,1)}) %all-gather.16.cloned.1.call-update) | async-done | bytes 9437200 | tf_op jit(solution)/shard_map/all_gather | solution.py:197
  284.8 7.4 fusion.59
  292.2 2.6 copy-done.17
  294.8 14.1 fusion.33
  308.9 99.4 %all-gather.18.cloned.1.call-done = bf16[4,768,1536]{2,1,0:T(8,128)(2,1)} async-done(((bf16[4,48,1536]{2,1,0:T(8,128)(2,1)}), bf16[4,768,1536]{2,1,0:T(8,128)(2,1)}) %all-gather.18.cloned.1.call-update) | async-done | bytes 9437200 | tf_op jit(solution)/shard_map/all_gather | solution.py:198
  408.3 5.2 fusion.83
  413.8 5.3 gather_fusion
  419.8 38.4 %all-gather.2 = bf16[16,48,4]{1,2,0:T(4,128)(2,1)S(1)} all-gather(bf16[1,48,4]{1,2,0:T(4,128)(2,1)S(1)} %bitcast.162), channel_id=1, replica_groups=mesh['fsdp'=16,'tensor'=2] {'fsdp'}, dimensions={0}, use_global_device_ids=true | all-gather | bytes 6528 | tf_op jit(solution)/shard_map/all_gather | solution.py:196
  460.5 6.5 scatter_custom_fusion.1
  467.0 8.0 fusion.39
  475.0 6.4 fusion.84
  481.7 5.3 gather_fusion.1
  487.0 36.7 %psum.37 = f32[4]{0:T(128)S(1)} all-reduce(f32[4]{0:T(128)S(1)} %get-tuple-element.330), channel_id=1, replica_groups=mesh['fsdp'=16,'tensor'=2] {'fsdp'}, use_global_device_ids=true, to_apply=%region_18.19 | all-reduce | flops 4 | bytes 32 | tf_op jit(solution)/shard_map/psum | solution.py:231
  524.5 2.8 multiply_reduce_fusion.4
  527.5 2.4 psum.36
  530.0 6.1 multiply_reduce_fusion.1
  540.4 54.6 %while.32 = (s32[]{:T(128)}, f32[1024,6,64]{0,2,1:T(8,128)S(1)}, f32[1024,6,64]{0,2,1:T(8,128)}, bf16[2,512,6,64]{1,3,2,0:T(8,128)(2,1)}, s32[2]{0:T(128)S(1)}, ...) while((s32[]{:T(128)}, f32[1024,6,64]{0,2,1:T(8,128)S(1)}, ...), condition=%wide.region_23.24_spmd.clone, body=%wide.region_21.23_spmd.clone.sunk | while | flops 2063661568 | bytes 132745864 | solution.py:149
  544.8 1.8 fusion.147
  546.7 3.4 bitcast_add_fusion.5
  550.1 7.1 multiply_reduce_fusion.8
  557.3 6.9 multiply_convert_fusion.5
  564.2 2.0 fusion.149
  571.9 1.8 fusion.147
  573.8 3.5 bitcast_add_fusion.5
  577.3 7.1 multiply_reduce_fusion.8
  584.4 6.9 multiply_convert_fusion.5
  591.3 2.0 fusion.149
  595.0 1.9 copy.40
  599.2 1.8 convert.17
  602.2 5.4 convolution_bitcast_fusion
  608.3 4.2 convolution_bitcast_fusion.1
  612.6 3.0 fusion.60
  615.7 5.7 convert_bitcast_fusion
  621.3 5.3 copy.45
  626.8 2.0 all-reduce.9.cloned.1.call-done
  628.8 5.9 fusion.51
  636.0 8.6 convolution_convert_fusion.1
  644.7 8.7 convolution_convert_fusion
  655.3 42.0 %psum.39 = f32[4]{0:T(128)S(1)} all-reduce(f32[4]{0:T(128)S(1)} %copy-done.44), channel_id=1, replica_groups=mesh['fsdp'=16,'tensor'=2] {'fsdp'}, use_global_device_ids=true, to_apply=%region_35.36 | all-reduce | flops 4 | bytes 32 | tf_op jit(solution)/shard_map/psum | solution.py:231
  698.6 57.7 %reduce-scatter.24.cloned.1.call-done = f32[48,4]{1,0:T(8,128)} async-done(((f32[768,4]{1,0:T(8,128)}), f32[48,4]{1,0:T(8,128)}) %reduce-scatter.24.cloned.1.call-update) | async-done | bytes 784
  757.6 125.2 %reduce-scatter.16.cloned.1.call-done = bf16[1,48,384]{2,1,0:T(8,128)(2,1)} async-done(((bf16[1,768,384]{2,1,0:T(8,128)(2,1)}), bf16[1,48,384]{2,1,0:T(8,128)(2,1)}) %reduce-scatter.16.cloned.1.call-update) | async-done | bytes 36880 | tf_op jit(solution)/shard_map/reduce_scatter | solution.py:165
  884.2 134.3 %all-reduce.11.cloned.1.call-done = bf16[3,768,384]{2,0,1:T(4,128)(2,1)} async-done(((bf16[3,768,384]{2,0,1:T(4,128)(2,1)}), bf16[3,768,384]{2,0,1:T(4,128)(2,1)}) %all-reduce.11.cloned.1.call-update) | async-done | bytes 1769488
  1020.3 3.4 dynamic-slice_add_fusion
  1023.6 121.6 %reduce-scatter.22.cloned.1.call-done = f32[48,2]{1,0:T(8,128)} async-done(((f32[768,2]{1,0:T(8,128)}), f32[48,2]{1,0:T(8,128)}) %reduce-scatter.22.cloned.1.call-update) | async-done | bytes 400
  1146.6 174.5 %reduce-scatter.18.cloned.1.call-done = bf16[4,48,1536]{2,1,0:T(8,128)(2,1)} async-done(((bf16[4,768,1536]{2,1,0:T(8,128)(2,1)}), bf16[4,48,1536]{2,1,0:T(8,128)(2,1)}) %reduce-scatter.18.cloned.1.call-update) | async-done | bytes 589840 | tf_op jit(solution)/shard_map/reduce_scatter | solution.py:165
  1321.0 2.2 convert_element_type.149
  1323.2 174.4 %reduce-scatter.20.cloned.1.call-done = bf16[4,48,1536]{2,1,0:T(8,128)(2,1)} async-done(((bf16[4,768,1536]{2,1,0:T(8,128)(2,1)}), bf16[4,48,1536]{2,1,0:T(8,128)(2,1)}) %reduce-scatter.20.cloned.1.call-update) | async-done | bytes 589840 | tf_op jit(solution)/shard_map/reduce_scatter | solution.py:165
  1497.7 2.2 convert_element_type.151
  (225 shorter events, 40.5 us)
Async XLA Ops:
  7.2 87.1 %all-gather.10.cloned.1.call-start = ((), (), s32[]{:S(2)}) async-start(), calls=%async_computation.7 | async-start | bytes 2359296 | tf_op jit(solution)/shard_map/all_gather | solution.py:200
  7.9 88.2 %all-gather.12.cloned.1.call-start = ((), (), s32[]{:S(2)}) async-start(), calls=%async_computation.8 | async-start | bytes 1880064 | tf_op jit(solution)/shard_map/all_gather | solution.py:191
  8.7 133.5 %reduce-scatter.12.cloned.1.call-start = ((), (), s32[]{:S(2)}) async-start(), calls=%async_computation.9 | async-start | bytes 4718592 | tf_op jit(solution)/shard_map/reduce_scatter | solution.py:209
  51.2 49.0 %copy-start.38 = (f32[768]{0:T(1024)}, f32[768]{0:T(1024)S(1)}, u32[]{:S(2)}) copy-start(f32[768]{0:T(1024)S(1)} %get-tuple-element.332) | copy-start | bytes 9220
  96.1 4.2 copy-start.36
  128.1 4.9 copy-start
  128.1 4.9 copy-start.5
  128.1 4.9 copy-start.9
  128.1 14.0 copy-start.20
  133.0 14.0 copy-start.30
  133.0 25.3 %all-gather.14.cloned.1.call-start = ((), (), s32[]{:S(2)}) async-start(), calls=%async_computation.10 | async-start | bytes 4718592 | tf_op jit(solution)/shard_map/all_gather | solution.py:218
  144.9 140.0 %all-gather.16.cloned.1.call-start = ((), (), s32[]{:S(2)}) async-start(), calls=%async_computation.11 | async-start | bytes 10027008 | tf_op jit(solution)/shard_map/all_gather | solution.py:197
  145.4 262.9 %all-gather.18.cloned.1.call-start = ((), (), s32[]{:S(2)}) async-start(), calls=%async_computation.12 | async-start | bytes 10027008 | tf_op jit(solution)/shard_map/all_gather | solution.py:198
  146.0 314.4 %all-gather.20.cloned.1.call-start = ((), (), s32[]{:S(2)}) async-start(), calls=%async_computation.14 | async-start | bytes 2359296 | tf_op jit(solution)/shard_map/all_gather | solution.py:262
  146.8 377.7 %reduce-scatter.14.cloned.1.call-start = ((), (), s32[]{:S(2)}) async-start(), calls=%async_computation.13 | async-start | bytes 4718592 | tf_op jit(solution)/shard_map/reduce_scatter | solution.py:250
  158.3 2.8 copy-start.2
  292.2 2.6 copy-start.17
  308.9 104.6 %copy-start.11 = (bf16[4,256,1536]{2,1,0:T(8,128)(2,1)}, bf16[4,256,1536]{2,1,0:T(8,128)(2,1)S(1)}, u32[]{:S(2)}) copy-start(bf16[4,256,1536]{2,1,0:T(8,128)(2,1)S(1)} %fusion.33) | copy-start | bytes 9437188
  419.1 39.1 %copy-start.3 = (f32[1024,768]{1,0:T(8,128)S(1)}, f32[1024,768]{1,0:T(8,128)}, u32[]{:S(2)}) copy-start(f32[1024,768]{1,0:T(8,128)} %all-gather.14.cloned.1.call-done) | copy-start | bytes 9437188
  419.1 110.8 %all-reduce.7.cloned.1.call-start = ((), (), s32[]{:S(2)}) async-start(), calls=%async_computation.15 | async-start | bytes 6291456 | tf_op jit(solution)/shard_map/psum | solution.py:290
  467.0 8.0 copy-start.14
  475.0 6.4 copy-start.16
  486.9 37.6 %copy-start.13 = (f32[512,768]{1,0:T(8,128)S(1)}, f32[512,768]{1,0:T(8,128)}, u32[]{:S(2)}) copy-start(f32[512,768]{1,0:T(8,128)} %convert_add_fusion.1) | copy-start | bytes 4718596
  487.0 141.8 %all-reduce.9.cloned.1.call-start = ((), (), s32[]{:S(2)}) async-start(), calls=%async_computation.16 | async-start | bytes 6291456 | tf_op jit(solution)/shard_map/psum | solution.py:318
  523.8 12.3 copy-start.46
  523.8 12.2 copy-start.41
  524.5 11.6 copy-start.28
  524.5 11.6 copy-start.32
  529.9 6.1 copy-start.34
  530.0 6.1 copy-start.4
  530.0 6.1 copy-start.18
  536.1 2.6 copy-start.19
  537.0 1.7 copy-start.7
  538.7 1.7 copy-start.1
  538.7 1.7 copy-start.6
  544.8 1.9 copy-start.15
  544.8 1.9 copy-start.21
  546.7 3.5 copy-start.10
  550.1 7.1 copy-start.22
  557.3 6.9 copy-start.23
  571.9 1.9 copy-start.15
  571.9 1.9 copy-start.21
  573.7 3.5 copy-start.10
  577.2 7.1 copy-start.22
  584.4 6.9 copy-start.23
  593.3 1.4 copy-start.24
  598.8 3.5 copy-start.25
  599.1 2.2 copy-start.26
  602.2 5.5 copy-start.29
  602.2 5.5 copy-start.31
  602.2 5.5 copy-start.33
  602.2 5.5 copy-start.35
  607.6 5.0 copy-start.8
  607.7 148.6 %reduce-scatter.24.cloned.1.call-start = ((), (), s32[]{:S(2)}) async-start(), calls=%async_computation.21 | async-start | bytes 417792
  612.5 3.1 copy-start.37
  612.5 3.2 copy-start.39
  612.6 270.3 %reduce-scatter.16.cloned.1.call-start = ((), (), s32[]{:S(2)}) async-start(), calls=%async_computation.17 | async-start | bytes 626688 | tf_op jit(solution)/shard_map/reduce_scatter | solution.py:165
  615.6 402.9 %all-reduce.11.cloned.1.call-start = ((), (), s32[]{:S(2)}) async-start(), calls=%async_computation.22 | async-start | bytes 4718592
  621.3 5.4 copy-start.40
  626.7 518.5 %reduce-scatter.22.cloned.1.call-start = ((), (), s32[]{:S(2)}) async-start(), calls=%async_computation.20 | async-start | bytes 417792
  635.7 685.3 %reduce-scatter.18.cloned.1.call-start = ((), (), s32[]{:S(2)}) async-start(), calls=%async_computation.18 | async-start | bytes 10027008 | tf_op jit(solution)/shard_map/reduce_scatter | solution.py:165
  644.7 853.0 %reduce-scatter.20.cloned.1.call-start = ((), (), s32[]{:S(2)}) async-start(), calls=%async_computation.19 | async-start | bytes 10027008 | tf_op jit(solution)/shard_map/reduce_scatter | solution.py:165
  653.4 2.0 copy-start.44
  653.4 44.0 %copy-start.47 = (f32[4]{0:T(128)S(1)}, f32[4]{0:T(128)}, u32[]{:S(2)}) copy-start(f32[4]{0:T(128)} %copy-done.46) | copy-start | bytes 52
  (6 other events, 5.5 us)
Sparse Core Ops, SparseCore 0:
  9.6 12.4 all-gather.9
  24.8 62.7 all-gather.11
  133.1 8.9 reduce-scatter.11
  145.0 13.2 all-gather.13
  161.2 123.5 all-gather.15
  287.7 120.5 all-gather.17
  410.0 7.9 all-gather.19
  420.3 12.0 reduce-scatter.13
  487.1 19.0 all-reduce.6
  607.8 20.9 all-reduce.8
  633.4 122.7 reduce-scatter.23
  761.5 121.2 reduce-scatter.15
  888.4 130.0 all-reduce.10
  1024.3 120.8 reduce-scatter.21
  1150.7 170.2 reduce-scatter.17
  1327.5 170.1 reduce-scatter.19

commit v2 on v1

--- a/solution.py
+++ b/solution.py
@@ -1,9 +1,859 @@
 import math
+import types
 
 import jax
 import jax.numpy as jnp
 from jax import lax
+from jax.experimental import pallas as pl
+from jax.experimental.pallas import tpu as pltpu
 from jax.sharding import PartitionSpec as P
+
+MESH = pl.DeviceIdType.MESH
+BF = jnp.bfloat16
+F32 = jnp.float32
+ROWS = 1024
+WIDE = 768
+HALF = 384
+HID = 1536
+norm_eps = 1e-05
+balance_weight = 0.01
+masked_score = -1e30
+
+
+def mm(a, b, ca=1, cb=0):
+    return lax.dot_general(a, b, (((ca,), (cb,)), ((), ())), preferred_element_type=F32)
+
+
+def iota(shape, axis):
+    return lax.broadcasted_iota(jnp.int32, shape, axis)
+
+
+def blocks(count, size, body):
+    def step(i, carry):
+        body(pl.ds(pl.multiple_of(i * size, size), size))
+        return carry
+
+    lax.fori_loop(0, count // size, step, 0)
+
+
+class Place:
+    def __init__(self):
+        f, t = lax.axis_index("fsdp"), lax.axis_index("tensor")
+        self.f, self.t, self.o = f, t, 1 - t
+        self.z, self.c = lax.div(f, 4), lax.rem(f, 4)
+        c = self.c
+        self.cx = c + 1 - 2 * lax.rem(c, 2)
+        self.cy = c + 2 - 4 * lax.div(c, 2)
+        self.cd = 3 - c
+        base = 4 * self.z
+        self.X = {"fsdp": base + self.cx, "tensor": t}
+        self.Y = {"fsdp": base + self.cy, "tensor": t}
+        self.DIAG = {"fsdp": base + self.cd, "tensor": t}
+        self.PAIR = {"fsdp": f, "tensor": 1 - t}
+
+    def zto(self, k):
+        return lax.rem(self.z + k, 4)
+
+    def zfrom(self, k):
+        return lax.rem(self.z + 4 - k, 4)
+
+    def Z(self, k):
+        return {"fsdp": 4 * self.zto(k) + self.c, "tensor": self.t}
+
+
+class Wire:
+    def __init__(self, send, recv):
+        self.send, self.recv, self.n, self.open = send, recv, 0, []
+
+    def ids(self, n):
+        self.n += n
+        return self.n - n
+
+    def copy(self, i, src, dst, dev):
+        return pltpu.make_async_remote_copy(
+            src_ref=src,
+            dst_ref=dst,
+            send_sem=self.send.at[i],
+            recv_sem=self.recv.at[i],
+            device_id=dev,
+            device_id_type=MESH,
+        )
+
+    def go(self, i, src, dst, dev):
+        c = self.copy(i, src, dst, dev)
+        c.start()
+        self.open.append(c)
+        return c
+
+    def flush(self):
+        for c in self.open:
+            c.wait_send()
+        self.open = []
+
+
+def enter(pc):
+    barrier = pltpu.get_barrier_semaphore()
+    for dev in (pc.PAIR, pc.X, pc.Y, pc.DIAG, pc.Z(1), pc.Z(2), pc.Z(3)):
+        pl.semaphore_signal(barrier, inc=1, device_id=dev, device_id_type=MESH)
+    pl.semaphore_wait(barrier, 7)
+
+
+def visible(krow0, kn, qcol0, qn, prefix):
+    kpos = krow0 + iota((kn, qn), 0)
+    qpos = qcol0 + iota((kn, qn), 1)
+    ok = kpos <= qpos
+    if krow0 < 512 and qcol0 < 512:
+        ok = ok | (kpos < prefix)
+    return ok
+
+
+SEEN = (
+    ((0, 512, True),),
+    ((0, 512, True),),
+    ((0, 512, False), (512, 256, True)),
+    ((0, 512, False), (512, 256, False), (768, 256, True)),
+)
+
+
+def phase_a(R, pc, w):
+    f, t, z, c = pc.f, pc.t, pc.z, pc.c
+    idr = R.idr[...]
+    ohr = (iota((16, ROWS), 0) - 8 == idr).astype(F32)
+    cnt = jnp.sum(ohr, axis=1, keepdims=True)
+    hi = jnp.floor(cnt * (1.0 / 256.0))
+    lane16 = iota((16, 128), 1)
+    R.SM[f] = jnp.where(
+        lane16 == 48,
+        cnt - 256.0 * hi,
+        jnp.where(lane16 == 49, hi, R.small[...].astype(F32)),
+    ).astype(BF)
+    R.WA[z, c] = R.watt[...]
+    enter(pc)
+    own = pl.ds(pl.multiple_of(t * 512, 512), 512)
+    i_tok, i_cot, i_wo, i_att = w.ids(1), w.ids(1), w.ids(1), w.ids(1)
+    i_z, i_sz = w.ids(4), w.ids(4)
+    i_x, i_y, i_fx, i_fy, i_sx, i_sy, i_sf = (w.ids(4) for _ in range(7))
+    i_mu, i_md = w.ids(4), w.ids(4)
+    i_m = [w.ids(4) for _ in range(6)]
+    i_cz, i_dz, i_cp, i_dp = w.ids(4), w.ids(4), w.ids(1), w.ids(1)
+
+    za = [w.go(i_z + k, R.watt, R.WA.at[z, c], pc.Z(k)) for k in (1, 2, 3)]
+    zs = [w.go(i_sz + k, R.SM.at[f], R.SM.at[f], pc.Z(k)) for k in (1, 2, 3)]
+    cot_x = w.go(i_cot, R.cot, R.CT.at[own], pc.PAIR)
+    tok_x = w.go(i_tok, R.tok, R.TK.at[own], pc.PAIR)
+
+    def spread(k):
+        zz = pc.zfrom(k)
+        g = 4 * zz + c
+        a = w.go(i_x + k, R.WA.at[zz, c], R.WA.at[zz, c], pc.X)
+        b = w.go(i_y + k, R.WA.at[zz, c], R.WA.at[zz, c], pc.Y)
+        d = w.go(i_sx + k, R.SM.at[g], R.SM.at[g], pc.X)
+        e = w.go(i_sy + k, R.SM.at[g], R.SM.at[g], pc.Y)
+        return a, b, d, e
+
+    def forward(k, got):
+        zz = pc.zfrom(k)
+        a, b, d, e = got
+        a.wait_recv()
+        x = w.go(
+            i_fx + k,
+            R.WA.at[zz, pc.cx, pl.ds(0, 2)],
+            R.WA.at[zz, pc.cx, pl.ds(0, 2)],
+            pc.Y,
+        )
+        d.wait_recv()
+        g = 4 * zz + pc.cx
+        s = w.go(i_sf + k, R.SM.at[g], R.SM.at[g], pc.Y)
+        b.wait_recv()
+        y = w.go(
+            i_fy + k,
+            R.WA.at[zz, pc.cy, pl.ds(2, 2)],
+            R.WA.at[zz, pc.cy, pl.ds(2, 2)],
+            pc.X,
+        )
+        e.wait_recv()
+        return x, y, s
+
+    got = {0: spread(0)}
+    local = [
+        pltpu.make_async_copy(R.tok, R.TK.at[own], R.ls.at[0]),
+        pltpu.make_async_copy(R.cot, R.CT.at[own], R.ls.at[1]),
+        pltpu.make_async_copy(R.up.at[z], R.UE.at[z, c], R.ls.at[2]),
+        pltpu.make_async_copy(R.down.at[z], R.DE.at[z, c], R.ls.at[3]),
+    ]
+    for m in local:
+        m.start()
+    before_or_at = (iota((ROWS, ROWS), 0) <= iota((ROWS, ROWS), 1)).astype(F32).astype(BF)
+    running = mm(ohr.astype(BF), before_or_at)
+    placed = jnp.sum(running * ohr, axis=0, keepdims=True) - 1.0
+    key = jnp.where(placed < 256.0, idr.astype(F32) * 256.0 + placed, -1.0)
+    R.KC[...] = jnp.broadcast_to(key, (128, ROWS)).T
+    R.PR[...] = jnp.broadcast_to(idr.astype(F32), (128, ROWS)).T
+    r = iota((512, ROWS), 0)
+    want = lax.div(r, 128) * 256 + lax.rem(r, 128) + 128 * t
+    R.DM[...] = (key.astype(jnp.int32) == want).astype(F32).astype(BF)
+
+    za[0].wait_recv()
+    zs[0].wait_recv()
+    got[1] = spread(1)
+    for m in local:
+        m.wait()
+    cot_x.wait_recv()
+
+    def cot_rows(e, carry):
+        R.CS[e] = mm(R.DM[pl.ds(pl.multiple_of(e * 128, 128), 128)], R.CT[...]).astype(BF)
+        return carry
+
+    lax.fori_loop(0, 4, cot_rows, 0)
+    R.CR[z, t] = R.CS[z]
+    za[1].wait_recv()
+    zs[1].wait_recv()
+    got[2] = spread(2)
+    za[2].wait_recv()
+    zs[2].wait_recv()
+    got[3] = spread(3)
+    mu = [w.go(i_mu + k, R.up.at[pc.zto(k)], R.UE.at[z, c], pc.Z(k)) for k in (1, 2, 3)]
+    md = [w.go(i_md + k, R.down.at[pc.zto(k)], R.DE.at[z, c], pc.Z(k)) for k in (1, 2, 3)]
+    cz = [w.go(i_cz + k, R.CS.at[pc.zto(k)], R.CR.at[z, t], pc.Z(k)) for k in (1, 2, 3)]
+    ends = [forward(k, got[k]) for k in range(4)]
+
+    tok_x.wait_recv()
+
+    def factors(rows):
+        x = R.TK[rows].astype(F32)
+        R.F1[rows] = lax.rsqrt(jnp.mean(x * x, axis=1, keepdims=True) + norm_eps)
+
+    blocks(ROWS, 128, factors)
+    for x, y, s in ends:
+        s.wait_recv()
+    parts = [R.SM[g].astype(F32)[:, 0:48] for g in range(16)]
+    vecs = jnp.concatenate(parts, axis=1)
+    R.VEC[...] = vecs
+    R.RW[...] = jnp.concatenate([vecs, jnp.zeros((112, WIDE), F32)], axis=0).T.astype(BF)
+    total = jnp.zeros((16, 128), F32)
+    for g in range(16):
+        total = total + R.SM[g].astype(F32)
+    counts = jnp.sum(
+        jnp.where(lane16 == 48, total, jnp.where(lane16 == 49, 256.0 * total, 0.0)),
+        axis=1,
+        keepdims=True,
+    )
+    share = jnp.sum(
+        jnp.where(iota((16, 128), 0) - 8 == lane16 - 2, counts, 0.0), axis=0, keepdims=True
+    ) * (1.0 / (16 * ROWS))
+    R.SHARE[...] = jnp.broadcast_to(share, (8, 128))
+
+    def norm_one(rows):
+        x = R.TK[rows].astype(F32)
+        R.NM[rows] = (x * R.F1[rows] * R.VEC[0:1]).astype(BF)
+
+    blocks(ROWS, 128, norm_one)
+    for x, y, s in ends:
+        x.wait_recv()
+        y.wait_recv()
+    wo = w.go(i_wo, R.WA.at[:, :, 3], R.WO, pc.PAIR)
+
+    def moe_spread(k):
+        zz = pc.zfrom(k)
+        u, d = R.UE.at[zz, c], R.DE.at[zz, c]
+        return [
+            w.copy(i_m[0] + k, u, u, pc.X),
+            w.copy(i_m[1] + k, d, d, pc.Y),
+            w.copy(i_m[2] + k, u, u, pc.Y),
+            w.copy(i_m[3] + k, d, d, pc.X),
+        ]
+
+    def moe_forward(k):
+        zz = pc.zfrom(k)
+        u, d = R.UE.at[zz, pc.cx], R.DE.at[zz, pc.cy]
+        return [
+            w.copy(i_m[4] + k, u, u, pc.Y),
+            w.copy(i_m[5] + k, d, d, pc.X),
+        ]
+
+    for m in moe_spread(0):
+        m.start()
+
+    def project(rows):
+        x = R.NM[rows]
+        for s, ref in enumerate((R.QS, R.KS, R.VS)):
+            y = mm(x, R.WA[:, :, s].reshape(WIDE, HALF))
+            if s == 0:
+                y = y.astype(BF).astype(F32) * 0.125
+            for p in range(3):
+                ref[p, rows] = y[:, 128 * p : 128 * p + 128].astype(BF)
+
+    blocks(ROWS, 256, project)
+    prefix = R.pre[0]
+
+    def pair_of_heads(p, carry):
+        value_t = R.VS[p].astype(F32).T.astype(BF)
+        even = iota((256, 128), 1) < 64
+        for qb in range(4):
+            cols = pl.ds(qb * 256, 256)
+            outs = []
+            for i in range(2):
+                q = R.QS[p, cols]
+                q = jnp.where(even if i == 0 else ~even, q.astype(F32), 0.0).astype(BF)
+                pieces = []
+                for k0, kn, masked in SEEN[qb]:
+                    s = mm(R.KS[p, pl.ds(k0, kn)], q, 1, 1)
+                    if masked:
+                        s = jnp.where(visible(k0, kn, qb * 256, 256, prefix), s, masked_score)
+                    pieces.append(s)
+                top = pieces[0].max(axis=0, keepdims=True)
+                for s in pieces[1:]:
+                    top = jnp.maximum(top, s.max(axis=0, keepdims=True))
+                total_e = jnp.zeros((1, 256), F32)
+                out = jnp.zeros((128, 256), F32)
+                for (k0, kn, _), s in zip(SEEN[qb], pieces):
+                    e = jnp.exp(s - top)
+                    total_e = total_e + e.sum(axis=0, keepdims=True)
+                    out = out + mm(value_t[:, k0 : k0 + kn], e.astype(BF))
+                R.LT[p, i : i + 1, cols] = top + jnp.log(total_e)
+                outs.append(out / total_e)
+            both = jnp.where(iota((128, 256), 0) < 64, outs[0], outs[1])
+            R.ATO[cols, pl.ds(pl.multiple_of(p * 128, 128), 128)] = both.T.astype(BF)
+
+        @pl.when(p < 3)
+        def _():
+            k = p + 1
+            for ref, i0 in ((R.UE, i_mu), (R.DE, i_md)):
+                w.copy(i0 + k, ref.at[z, c], ref.at[z, c], pc.Z(k)).wait_recv()
+            for m in moe_spread(k):
+                m.start()
+
+        a = moe_spread(p)
+        a[0].wait_recv()
+        a[1].wait_recv()
+        for m in moe_forward(p):
+            m.start()
+        return carry
+
+    lax.fori_loop(0, 3, pair_of_heads, 0)
+    att = w.go(i_att, R.ATO, R.ATX, pc.PAIR)
+    a = moe_spread(3)
+    a[0].wait_recv()
+    a[1].wait_recv()
+    for m in moe_forward(3):
+        m.start()
+    for m in cz:
+        m.wait_recv()
+    cp = w.go(i_cp, R.CR.at[:, t], R.CR.at[:, t], pc.PAIR)
+    wo.wait_recv()
+    att.wait_recv()
+    lane = iota((256, 128), 1)
+    real = (lane >= 2) & (lane < 6)
+    R.PS[...] = jnp.zeros((8, 128), F32)
+
+    def out_block(rows):
+        b = mm(R.ATO[rows], R.WA[:, :, 3].reshape(WIDE, HALF), 1, 1)
+        b = b + mm(R.ATX[rows], R.WO[...].reshape(WIDE, HALF), 1, 1)
+        h = R.TK[rows].astype(F32) + b
+        R.HIDN[rows] = h
+        f2 = lax.rsqrt(jnp.mean(h * h, axis=1, keepdims=True) + norm_eps)
+        R.F2[rows] = f2
+        moe = (h * f2 * R.VEC[1:2]).astype(BF)
+        R.MOE[rows] = moe
+        logits = mm(moe, R.RW[...])
+        mine = jnp.where((lane - 2).astype(F32) == R.PR[rows], logits, 0.0)
+        picked = jnp.sum(jnp.where(real, mine, 0.0), axis=1, keepdims=True)
+        R.GV[rows] = jax.nn.sigmoid(picked)
+        lg = jnp.where(real, logits, masked_score)
+        e = jnp.exp(lg - jnp.max(lg, axis=1, keepdims=True))
+        e = jnp.where(real, e, 0.0)
+        pr = e / jnp.sum(e, axis=1, keepdims=True)
+        R.PR[rows] = pr
+        R.PS[0:1] = R.PS[0:1] + jnp.sum(pr, axis=0, keepdims=True)
+
+    blocks(ROWS, 256, out_block)
+
+    def moe_rows(e, carry):
+        R.CS[e] = mm(R.DM[pl.ds(pl.multiple_of(e * 128, 128), 128)], R.MOE[...]).astype(BF)
+        return carry
+
+    w.flush()
+    lax.fori_loop(0, 4, moe_rows, 0)
+    R.DR[z, t] = R.CS[z]
+    dz = [w.go(i_dz + k, R.CS.at[pc.zto(k)], R.DR.at[z, t], pc.Z(k)) for k in (1, 2, 3)]
+    for k in range(4):
+        a = moe_spread(k)
+        b = moe_forward(k)
+        a[2].wait_recv()
+        a[3].wait_recv()
+        b[0].wait_recv()
+        b[1].wait_recv()
+        for m in a + b:
+            m.wait_send()
+    for m in dz:
+        m.wait_recv()
+    dp = w.go(i_dp, R.DR.at[:, t], R.DR.at[:, t], pc.PAIR)
+    cp.wait_recv()
+    dp.wait_recv()
+    w.flush()
+
+
+def gelu_parts(v):
+    cdf = 0.5 * (1.0 + lax.erf(v * (1.0 / math.sqrt(2.0))))
+    slope = cdf + v * (jnp.exp(-0.5 * v * v) * (1.0 / math.sqrt(2.0 * math.pi)))
+    return v * cdf, slope
+
+
+def phase_b(R, pc, w):
+    f, t, z, c, o = pc.f, pc.t, pc.z, pc.c, pc.o
+    i_xe, i_xg = w.ids(1), w.ids(1)
+    i_rg, i_re, i_rgp, i_rep = w.ids(4), w.ids(4), w.ids(1), w.ids(1)
+    i_u1, i_u2, i_d1, i_d2 = w.ids(2), w.ids(1), w.ids(2), w.ids(1)
+    DR, CR = R.DR.reshape(ROWS, WIDE), R.CR.reshape(ROWS, WIDE)
+    EO, GM = R.EO.reshape(ROWS, WIDE), R.GM.reshape(ROWS, WIDE)
+    lane = iota((256, 128), 1)
+
+    def gates(rows):
+        logits = mm(DR[rows], R.RW[...])
+        gate = jax.nn.sigmoid(
+            jnp.sum(jnp.where(lane == 2 + z, logits, 0.0), axis=1, keepdims=True)
+        )
+        R.GATE[rows] = gate
+        R.GC[rows] = (gate * CR[rows].astype(F32)).astype(BF)
+        EO[rows] = jnp.zeros((256, WIDE), F32)
+        GM[rows] = jnp.zeros((256, WIDE), F32)
+
+    blocks(ROWS, 256, gates)
+
+    def hidden_units(cols):
+        up = R.UE[:, :, :, cols].reshape(WIDE, 512)
+        down = R.DE[:, :, :, cols].reshape(WIDE, 512)
+
+        def tokens_block(rows):
+            act, slope = gelu_parts(mm(DR[rows], up))
+            act = act.astype(BF)
+            gb = (mm(R.GC[rows], down) * slope).astype(BF)
+            R.ACT[rows] = act
+            R.GB[rows] = gb
+            EO[rows] += mm(act, down, 1, 1)
+            GM[rows] += mm(gb, up, 1, 1)
+
+        blocks(ROWS, 256, tokens_block)
+        R.UE[:, :, :, cols] = mm(DR[...], R.GB[...], 0, 0).astype(BF).reshape(4, 4, 48, 512)
+        R.DE[:, :, :, cols] = mm(R.GC[...], R.ACT[...], 0, 0).astype(BF).reshape(4, 4, 48, 512)
+
+    blocks(HID, 512, hidden_units)
+
+    def partials(e, carry):
+        R.CS[e] = R.GM[e, o].astype(BF)
+        R.ES[e] = R.EO[e, o].astype(BF)
+        return carry
+
+    lax.fori_loop(0, 4, partials, 0)
+    xg = w.go(i_xg, R.CS, R.XG, pc.PAIR)
+    xe = w.go(i_xe, R.ES, R.XE, pc.PAIR)
+    R.moe_sums = [
+        w.go(i_u1, R.UE.at[:, pc.cx], R.RU.at[0], pc.X),
+        w.go(i_u1 + 1, R.UE.at[:, pc.cd], R.RU.at[1], pc.X),
+        w.go(i_d1, R.DE.at[:, pc.cy], R.RD.at[0], pc.Y),
+        w.go(i_d1 + 1, R.DE.at[:, pc.cd], R.RD.at[1], pc.Y),
+    ]
+    R.i_u2, R.i_d2 = i_u2, i_d2
+    xg.wait()
+    xe.wait()
+    w.open = [m for m in w.open if m is not xg and m is not xe]
+    row = jnp.sum(
+        jnp.where(iota((16, WIDE), 0) == 2 + z, R.VEC[...], 0.0), axis=0, keepdims=True
+    )
+    R.RGR[...] = jnp.zeros((16, WIDE), F32)
+
+    def finish(e, carry):
+        eo = R.EO[e, t] + R.XE[e].astype(F32)
+        gate = R.GATE.reshape(4, 2, 128, 1)[e, t]
+        gate_grad = jnp.sum(R.CR[e, t].astype(F32) * eo, axis=1, keepdims=True)
+        gs = gate_grad * gate * (1.0 - gate)
+        R.RGR[0:1] += jnp.sum(gs * R.DR[e, t].astype(F32), axis=0, keepdims=True)
+        R.CS[e] = (R.GM[e, t] + R.XG[e].astype(F32) + gs * row).astype(BF)
+        R.ES[e] = eo.astype(BF)
+        return carry
+
+    lax.fori_loop(0, 4, finish, 0)
+    R.RGR[...] = jnp.where(iota((16, WIDE), 0) == 2 + z, R.RGR[0:1], 0.0)
+    rg = [w.go(i_rg + k, R.CS.at[pc.zto(k)], R.RG.at[z, t], pc.Z(k)) for k in (1, 2, 3)]
+    re = [w.go(i_re + k, R.ES.at[pc.zto(k)], R.RE.at[z, t], pc.Z(k)) for k in (1, 2, 3)]
+    R.RG[z, t] = R.CS[z]
+    R.RE[z, t] = R.ES[z]
+    for m in rg:
+        m.wait_recv()
+    w.go(i_rgp, R.RG.at[:, t], R.RG.at[:, t], pc.PAIR).wait_recv()
+    R.expert_rows = (re, i_rep)
+
+
+def combine(key, rows, got):
+    n = key.shape[0]
+    keys = jnp.concatenate([key] * 8, axis=1)
+    pick = (keys == iota((n, ROWS), 1).astype(F32)).astype(F32).astype(BF)
+    return mm(pick, got)
+
+
+def phase_c(R, pc, w):
+    f, t, z, c, o = pc.f, pc.t, pc.z, pc.c, pc.o
+    i_uz, i_dz = w.ids(4), w.ids(4)
+    i_a1, i_a2, i_b1, i_b2, i_az = w.ids(2), w.ids(1), w.ids(2), w.ids(1), w.ids(4)
+    i_n = w.ids(1)
+    i_sp, i_sc, i_sz = w.ids(1), w.ids(4), w.ids(4)
+    own = pl.ds(pl.multiple_of(t * 512, 512), 512)
+    other = pl.ds(pl.multiple_of(o * 512, 512), 512)
+    GH, GN = R.GM.reshape(ROWS, WIDE), R.EO.reshape(ROWS, WIDE)
+    RG, RE = R.RG.reshape(ROWS, WIDE), R.RE.reshape(ROWS, WIDE)
+    GBR = R.GC
+    share = R.SHARE[0:1]
+    vec = R.VEC[...]
+    head = iota((24, HALF), 0)
+    head = jnp.where(lax.rem(head, 8) < 2, 2 * lax.div(head, 8) + lax.rem(head, 8), -1)
+    pick_head = (head == lax.div(iota((24, HALF), 1), 64)).astype(F32).astype(BF)
+    R.SB[...] = jnp.zeros((16, WIDE), F32)
+
+    def residual(i, carry):
+        rows = pl.ds(pl.multiple_of(i * 256, 256), 256)
+        gm = combine(R.KC[rows], rows, RG[...])
+        pr = R.PR[rows]
+        mixed = jnp.sum(pr * share, axis=1, keepdims=True)
+        aux = (balance_weight * 4.0 / (16 * ROWS)) * pr * (share - mixed)
+        aux = aux[:, 0:16]
+        gm = gm + mm(aux.astype(BF), vec.astype(BF))
+        mine = jnp.where(lax.div(i, 2) == t, 1.0, 0.0)
+        R.SB[...] += mine * mm(aux.astype(BF), R.MOE[rows], 0, 0)
+        h, f2 = R.HIDN[rows], R.F2[rows]
+        g = gm * vec[1:2]
+        inner = jnp.mean(g * h, axis=1, keepdims=True)
+        gh = R.CT[rows].astype(F32) + f2 * (g - h * (f2 * f2 * inner))
+        R.G2[0:1] += mine * jnp.sum(gm * h * f2, axis=0, keepdims=True)
+        GH[rows] = gh
+        low = gh.astype(BF)
+        GBR[rows] = low
+        ga = mm(low, R.WA[:, :, 3].reshape(WIDE, HALF)).astype(BF)
+        for p in range(3):
+            R.GAP[p, rows] = ga[:, 128 * p : 128 * p + 128]
+        prod = ga.astype(F32) * R.ATO[rows].astype(F32)
+        top = prod.astype(BF)
+        rest = (prod - top.astype(F32)).astype(BF)
+        dd = mm(pick_head, top, 1, 1) + mm(pick_head, rest, 1, 1)
+        for p in range(3):
+            R.DD[p, :, rows] = dd[8 * p : 8 * p + 8]
+        return carry
+
+    R.G2[...] = jnp.zeros((8, WIDE), F32)
+    lax.fori_loop(0, 4, residual, 0)
+    part = jnp.where(iota((16, WIDE), 0) == 1, R.G2[0:1], 0.0)
+    sums6 = jnp.concatenate([0.5 * R.PS[0:1], jnp.zeros((1, WIDE - 128), F32)], axis=1)
+    keep = (iota((16, WIDE), 0) >= 2) & (iota((16, WIDE), 0) < 6)
+    R.SB[...] = (
+        jnp.where(keep, R.SB[...] + R.RGR[...], 0.0)
+        + part
+        + jnp.where(iota((16, WIDE), 0) == 6, sums6, 0.0)
+    )
+    R.AG[:, :, 3] = mm(GBR[...], R.ATO[...], 0, 0).astype(BF).reshape(4, 4, 48, HALF)
+    prefix = R.pre[0]
+
+    def pair_of_heads(p, carry):
+        key_t = R.KS[p].astype(F32).T.astype(BF)
+        R.DK[...] = jnp.zeros((ROWS, 128), F32)
+        R.DV[...] = jnp.zeros((ROWS, 128), F32)
+        even = iota((256, 128), 1) < 64
+        for qb in range(4):
+            cols = pl.ds(qb * 256, 256)
+            outs = []
+            for i in range(2):
+                side = even if i == 0 else ~even
+                q = jnp.where(side, R.QS[p, cols].astype(F32), 0.0).astype(BF)
+                do = jnp.where(side, R.GAP[p, cols].astype(F32), 0.0).astype(BF)
+                lt, dd = R.LT[p, i : i + 1, cols], R.DD[p, i : i + 1, cols]
+                dq = jnp.zeros((128, 256), F32)
+                for kb in range(max(2, qb + 1)):
+                    keys = pl.ds(kb * 256, 256)
+                    s = mm(R.KS[p, keys], q, 1, 1)
+                    if kb == qb or qb < 2:
+                        ok = visible(kb * 256, 256, qb * 256, 256, prefix)
+                        s = jnp.where(ok, s, masked_score)
+                    prob = jnp.exp(s - lt)
+                    ds = prob * (mm(R.VS[p, keys], do, 1, 1) - dd)
+                    ds = ds.astype(BF)
+                    R.DV[keys] += mm(prob.astype(BF), do)
+                    R.DK[keys] += mm(ds, q)
+                    dq = dq + mm(key_t[:, kb * 256 : kb * 256 + 256], ds)
+                outs.append(dq)
+            both = jnp.where(iota((128, 256), 0) < 64, outs[0], outs[1])
+            R.QS[p, cols] = (both * 0.125).T.astype(BF)
+        R.KS[p] = R.DK[...].astype(BF)
+        R.VS[p] = R.DV[...].astype(BF)
+        mu, md = R.UE.at[:, c], R.DE.at[:, c]
+
+        @pl.when(p == 0)
+        def _():
+            for m in R.moe_sums:
+                m.wait_recv()
+            for zz in range(4):
+                R.UE[zz, c] = R.UE[zz, c] + R.RU[0, zz]
+                R.UE[zz, pc.cy] = R.UE[zz, pc.cy] + R.RU[1, zz]
+                R.DE[zz, c] = R.DE[zz, c] + R.RD[0, zz]
+                R.DE[zz, pc.cx] = R.DE[zz, pc.cx] + R.RD[1, zz]
+            w.copy(R.i_u2, R.UE.at[:, pc.cy], R.RU2, pc.Y).start()
+            w.copy(R.i_d2, R.DE.at[:, pc.cx], R.RD2, pc.X).start()
+
+        @pl.when(p == 1)
+        def _():
+            w.copy(R.i_u2, R.UE.at[:, pc.cy], R.RU2, pc.Y).wait()
+            w.copy(R.i_d2, R.DE.at[:, pc.cx], R.RD2, pc.X).wait()
+            for zz in range(4):
+                R.UE[zz, c] = R.UE[zz, c] + R.RU2[zz]
+                R.DE[zz, c] = R.DE[zz, c] + R.RD2[zz]
+            for k in (1, 2, 3):
+                w.copy(i_uz + k, R.UE.at[pc.zto(k), c], R.ZU.at[z], pc.Z(k)).start()
+                w.copy(i_dz + k, R.DE.at[pc.zto(k), c], R.ZD.at[z], pc.Z(k)).start()
+
+        return carry
+
+    lax.fori_loop(0, 3, pair_of_heads, 0)
+    GP = (R.QS, R.KS, R.VS)
+
+    def grads(ref, rows):
+        return jnp.concatenate([ref[p, rows] for p in range(3)], axis=1)
+
+    def normed_grad(rows):
+        acc = jnp.zeros((256, WIDE), F32)
+        for s in range(3):
+            acc = acc + mm(grads(GP[s], rows), R.WA[:, :, s].reshape(WIDE, HALF), 1, 1)
+        GN[rows] = acc
+
+    blocks(ROWS, 256, normed_grad)
+    w.flush()
+    XS, XN, BO = (r.reshape(512, WIDE) for r in (R.CS, R.XG, R.ES))
+    XS[...] = GN[other].astype(BF)
+    xn = w.go(i_n, XS, XN, pc.PAIR)
+    every = pl.ds(0, ROWS)
+    for s in range(3):
+        R.AG[:, :, s] = mm(R.NM[...], grads(GP[s], every), 0, 0).astype(BF).reshape(4, 4, 48, HALF)
+    a_half, b_half = pl.ds(0, 2), pl.ds(2, 2)
+    a1 = [
+        w.go(i_a1, R.AG.at[:, pc.cx, a_half], R.RA.at[0], pc.X),
+        w.go(i_a1 + 1, R.AG.at[:, pc.cd, a_half], R.RA.at[1], pc.X),
+    ]
+    b1 = [
+        w.go(i_b1, R.AG.at[:, pc.cy, b_half], R.RB.at[0], pc.Y),
+        w.go(i_b1 + 1, R.AG.at[:, pc.cd, b_half], R.RB.at[1], pc.Y),
+    ]
+    xn.wait_recv()
+    R.G2[...] = jnp.zeros((8, WIDE), F32)
+
+    def input_grad(i, carry):
+        rows = pl.ds(pl.multiple_of(i * 128, 128), 128)
+        full = pl.ds(pl.multiple_of(t * 512 + i * 128, 128), 128)
+        gn = GN[full] + XN[rows].astype(F32)
+        x, f1 = R.TK[full].astype(F32), R.F1[full]
+        g = gn * R.VEC[0:1]
+        inner = jnp.mean(g * x, axis=1, keepdims=True)
+        GH[full] = GH[full] + f1 * (g - x * (f1 * f1 * inner))
+        R.G2[0:1] += jnp.sum(gn * x * f1, axis=0, keepdims=True)
+        return carry
+
+    lax.fori_loop(0, 4, input_grad, 0)
+    out_t = pltpu.make_async_copy(GH.at[own], R.tokens_grad, R.ls.at[0])
+    out_t.start()
+    R.SB[0:1] = R.G2[0:1]
+    sp = w.go(i_sp, R.SB, R.SP, pc.PAIR)
+    for m in a1 + b1:
+        m.wait_recv()
+    for zz in range(4):
+        R.AG[zz, c, a_half] = R.AG[zz, c, a_half] + R.RA[0, zz]
+        R.AG[zz, pc.cy, a_half] = R.AG[zz, pc.cy, a_half] + R.RA[1, zz]
+        R.AG[zz, c, b_half] = R.AG[zz, c, b_half] + R.RB[0, zz]
+        R.AG[zz, pc.cx, b_half] = R.AG[zz, pc.cx, b_half] + R.RB[1, zz]
+    a2 = w.go(i_a2, R.AG.at[:, pc.cy, a_half], R.RA2, pc.Y)
+    b2 = w.go(i_b2, R.AG.at[:, pc.cx, b_half], R.RB2, pc.X)
+    sp.wait_recv()
+    me = R.SB[...] + R.SP[...]
+    R.SC[c] = me
+    sc = [
+        w.go(i_sc, R.SC.at[c], R.SC.at[c], pc.X),
+        w.go(i_sc + 1, R.SC.at[c], R.SC.at[c], pc.Y),
+        w.go(i_sc + 2, R.SC.at[c], R.SC.at[c], pc.DIAG),
+    ]
+    re, i_rep = R.expert_rows
+    for m in re:
+        m.wait_recv()
+    w.go(i_rep, R.RE.at[:, t], R.RE.at[:, t], pc.PAIR).wait_recv()
+
+    def block_rows(i, carry):
+        rows = pl.ds(pl.multiple_of(i * 256, 256), 256)
+        full = pl.ds(pl.multiple_of(t * 512 + i * 256, 256), 256)
+        eo = combine(R.KC[full], full, RE[...])
+        BO[rows] = (R.HIDN[full] + R.GV[full] * eo).astype(BF)
+        return carry
+
+    lax.fori_loop(0, 2, block_rows, 0)
+    out_b = pltpu.make_async_copy(BO, R.block_out, R.ls.at[1])
+    out_b.start()
+    a2.wait_recv()
+    b2.wait_recv()
+    for zz in range(4):
+        R.AG[zz, c, a_half] = R.AG[zz, c, a_half] + R.RA2[zz]
+        R.AG[zz, c, b_half] = R.AG[zz, c, b_half] + R.RB2[zz]
+    az = [w.go(i_az + k, R.AG.at[pc.zto(k), c], R.ZA.at[z], pc.Z(k)) for k in (1, 2, 3)]
+    for m in sc:
+        m.wait_recv()
+    R.SZ[z] = R.SC[0] + R.SC[1] + R.SC[2] + R.SC[3]
+    sz = [w.go(i_sz + k, R.SZ.at[z], R.SZ.at[z], pc.Z(k)) for k in (1, 2, 3)]
+    R.ZU[z] = R.UE[z, c]
+    R.ZD[z] = R.DE[z, c]
+    for k in (1, 2, 3):
+        w.copy(i_uz + k, R.UE.at[pc.zto(k), c], R.ZU.at[z], pc.Z(k)).wait()
+        w.copy(i_dz + k, R.DE.at[pc.zto(k), c], R.ZD.at[z], pc.Z(k)).wait()
+    R.up_grad[...] = R.ZU[...].astype(F32)
+    R.down_grad[...] = R.ZD[...].astype(F32)
+    for m in sz:
+        m.wait_recv()
+    total = R.SZ[0] + R.SZ[1] + R.SZ[2] + R.SZ[3]
+    probs = total[6:7, 0:128]
+    R.balance[...] = (4.0 / (16 * ROWS)) * jnp.sum(share * probs, axis=1, keepdims=True)
+    column = (iota((WIDE, 128), 0) == 48 * f + iota((WIDE, 128), 1)).astype(F32).astype(BF)
+    mine = jnp.zeros((16, 128), F32)
+    for _ in range(3):
+        top = total.astype(BF)
+        mine = mine + mm(top, column)
+        total = total - top.astype(F32)
+    R.gains_grad[...] = mine[0:2, 0:48]
+    R.router_grad[...] = mine[2:6, 0:48]
+    R.ZA[z] = R.AG[z, c]
+    for m in az:
+        m.wait_recv()
+    summed = R.ZA[0].astype(F32)
+    for zz in range(1, 4):
+        summed = summed + R.ZA[zz].astype(F32)
+    R.qkv_grad[...] = summed[0:3]
+    R.out_grad[...] = summed[3]
+    out_t.wait()
+    out_b.wait()
+    w.flush()
+
+
+OUTS = {
+    "block_out": ((512, WIDE), BF),
+    "tokens_grad": ((512, WIDE), F32),
+    "gains_grad": ((2, 48), F32),
+    "qkv_grad": ((3, 48, HALF), F32),
+    "out_grad": ((48, HALF), F32),
+    "router_grad": ((4, 48), F32),
+    "up_grad": ((4, 48, HID), F32),
+    "down_grad": ((4, 48, HID), F32),
+    "balance": ((1, 1), F32),
+}
+SCRATCH = {
+    "TK": ((ROWS, WIDE), BF),
+    "CT": ((ROWS, WIDE), BF),
+    "WA": ((4, 4, 4, 48, HALF), BF),
+    "WO": ((4, 4, 48, HALF), BF),
+    "UE": ((4, 4, 48, HID), BF),
+    "DE": ((4, 4, 48, HID), BF),
+    "KC": ((ROWS, 128), F32),
+    "CR": ((4, 2, 128, WIDE), BF),
+    "DR": ((4, 2, 128, WIDE), BF),
+    "F1": ((ROWS, 1), F32),
+    "F2": ((ROWS, 1), F32),
+    "VEC": ((16, WIDE), F32),
+    "RW": ((WIDE, 128), BF),
+    "SHARE": ((8, 128), F32),
+    "NM": ((ROWS, WIDE), BF),
+    "QS": ((3, ROWS, 128), BF),
+    "KS": ((3, ROWS, 128), BF),
+    "VS": ((3, ROWS, 128), BF),
+    "LT": ((3, 8, ROWS), F32),
+    "ATO": ((ROWS, HALF), BF),
+    "ATX": ((ROWS, HALF), BF),
+    "HIDN": ((ROWS, WIDE), F32),
+    "MOE": ((ROWS, WIDE), BF),
+    "GV": ((ROWS, 1), F32),
+    "PR": ((ROWS, 128), F32),
+    "PS": ((8, 128), F32),
+    "SM": ((16, 16, 128), BF),
+    "DM": ((512, ROWS), BF),
+    "CS": ((4, 128, WIDE), BF),
+    "ES": ((4, 128, WIDE), BF),
+    "GATE": ((ROWS, 1), F32),
+    "GC": ((ROWS, WIDE), BF),
+    "EO": ((4, 2, 128, WIDE), F32),
+    "GM": ((4, 2, 128, WIDE), F32),
+    "ACT": ((ROWS, 512), BF),
+    "GB": ((ROWS, 512), BF),
+    "XE": ((4, 128, WIDE), BF),
+    "XG": ((4, 128, WIDE), BF),
+    "RG": ((4, 2, 128, WIDE), BF),
+    "RE": ((4, 2, 128, WIDE), BF),
+    "RGR": ((16, WIDE), F32),
+    "RU": ((2, 4, 48, HID), BF),
+    "RD": ((2, 4, 48, HID), BF),
+    "RU2": ((4, 48, HID), BF),
+    "RD2": ((4, 48, HID), BF),
+    "ZU": ((4, 48, HID), BF),
+    "ZD": ((4, 48, HID), BF),
+    "GAP": ((3, ROWS, 128), BF),
+    "DD": ((3, 8, ROWS), F32),
+    "DK": ((ROWS, 128), F32),
+    "DV": ((ROWS, 128), F32),
+    "AG": ((4, 4, 4, 48, HALF), BF),
+    "RA": ((2, 4, 2, 48, HALF), BF),
+    "RB": ((2, 4, 2, 48, HALF), BF),
+    "RA2": ((4, 2, 48, HALF), BF),
+    "RB2": ((4, 2, 48, HALF), BF),
+    "ZA": ((4, 4, 48, HALF), BF),
+    "G2": ((8, WIDE), F32),
+    "SB": ((16, WIDE), F32),
+    "SP": ((16, WIDE), F32),
+    "SC": ((4, 16, WIDE), F32),
+    "SZ": ((4, 16, WIDE), F32),
+}
+INS = ("tok", "cot", "pre", "idr", "watt", "small", "up", "down")
+IN_HBM = ("tok", "cot", "up", "down")
+OUT_HBM = ("block_out", "tokens_grad")
+SEMAPHORES = 160
+
+
+def fused(args):
+    names = INS + tuple(OUTS) + tuple(SCRATCH) + ("ss", "rs", "ls")
+
+    def body(*refs):
+        R = types.SimpleNamespace(**dict(zip(names, refs)))
+        pc = Place()
+        w = Wire(R.ss, R.rs)
+        phase_a(R, pc, w)
+        phase_b(R, pc, w)
+        phase_c(R, pc, w)
+
+    vm = pl.BlockSpec(memory_space=pltpu.VMEM)
+    hbm = pl.BlockSpec(memory_space=pl.ANY)
+    sm = pl.BlockSpec(memory_space=pltpu.SMEM)
+    dma = pltpu.SemaphoreType.DMA
+    return pl.pallas_call(
+        body,
+        out_shape=[jax.ShapeDtypeStruct(s, d) for s, d in OUTS.values()],
+        in_specs=[sm if n == "pre" else hbm if n in IN_HBM else vm for n in INS],
+        out_specs=[hbm if n in OUT_HBM else vm for n in OUTS],
+        scratch_shapes=[pltpu.VMEM(s, d) for s, d in SCRATCH.values()]
+        + [dma((SEMAPHORES,)), dma((SEMAPHORES,)), dma((4,))],
+        compiler_params=pltpu.CompilerParams(
+            collective_id=1, has_side_effects=True, vmem_limit_bytes=63 << 20
+        ),
+        name="block",
+    )(*args)
+
+
+def prepare(
+    tokens, cotangent, prefix_len, expert_ids, norm_gains, qkv_weight, out_weight, router_weight, up_weight, down_weight
+):
+    watt = jnp.concatenate([qkv_weight, out_weight[None]], axis=0)
+    small = jnp.pad(jnp.concatenate([norm_gains, router_weight], axis=0), ((0, 10), (0, 80)))
+    return (tokens, cotangent, prefix_len, expert_ids.reshape(1, ROWS), watt, small, up_weight, down_weight)
+
+
+def fast_device(*args):
+    outs = fused(prepare(*args))
+    return tuple(outs[:8]) + (outs[8].reshape(()),)
+
 
 HEAD = 64
 EXPERTS = 4
@@ -12,9 +862,6 @@
 
 
 highest = lax.Precision.HIGHEST
-norm_eps = 1e-05
-balance_weight = 0.01
-masked_score = -1e30
 
 
 def softmax_rows(scores):
@@ -360,8 +1207,9 @@
         P(None, "fsdp", "tensor"),
         P(None, "fsdp", "tensor"),
     )
+    fits = mesh.shape["fsdp"] == 16 and mesh.shape["tensor"] == 2
     return jax.shard_map(
-        per_device,
+        fast_device if fits else per_device,
         mesh=mesh,
         in_specs=placed,
         out_specs=(

time: 1520 us -> 244 us (0.16)
  waiting for transfers between devices: 1030 us -> 0 us
  Pallas kernels: 0 us -> 229 us
  blocking collectives: 205 us -> 0 us
  matrix products: 125 us -> 0 us
  other arithmetic: 83.2 us -> 2.88 us
  local copies, waits for them, and re-layouts: 39.7 us -> 8.52 us
    reduce_scatter x5 -> x0, waiting for transfers between devices: 483 us -> none  [the longest x3 474 us: low_scatter(): lax.psum_scatter(grad.astype(jnp.bfloat16), 'fsdp', scatter_dimension=1,...]
    unnamed x19 -> x0, waiting for transfers between devices: 317 us -> none
    pallas_call x0 -> x1, Pallas kernels: none -> 229 us  [fused(): pl.pallas_call(body, out_shape=[jax.ShapeDtypeStruct(s, d) for s, d in OU...]
    all_gather x6 -> x0, waiting for transfers between devices: 227 us -> none  [the longest x1 117 us: per_device(): lax.all_gather(up_weight, 'fsdp', axis=1, tiled=True)]
    all_gather x3 -> x0, blocking collectives: 124 us -> none  [the longest x1 43 us: per_device(): lax.all_gather(out_weight[None], 'fsdp', axis=1, tiled=True)]
    dot_general x29 -> x0, matrix products: 121 us -> none  [the longest x2 14.2 us: one_block(): jnp.einsum('qhd,khd->hqk', grad_block, value_all, preferred_element_type=...]
    psum x3 -> x0, blocking collectives: 81.2 us -> none  [the longest x2 78.7 us: per_device(): lax.psum((jnp.sum(onehot, axis=0), jnp.sum(router_prob, axis=0)), 'fsdp')]
    convert_element_type x7 -> x0, other arithmetic: 33.7 us -> none  [the longest x1 14.1 us: per_device(): activated = jax.nn.gelu(before, approximate=False).astype(jnp.bfloat16)]
  transfers between devices with their start and end apart: 16 -> 0, of which waited for: 11 -> 0; matrix products, arithmetic and copies ran while one was open for 9% -> 0% of each run, Pallas kernels for 0% -> 0%
where the time goes in v2:
time: 244 us
  Pallas kernels  229 us (94%)
  local copies, waits for them, and re-layouts  8.52 us (3%)
  between operations  3.1 us (1%)
  other arithmetic  2.88 us (1%)
    pallas_call x1, Pallas kernels, fused(): pl.pallas_call(body, out_shape=[jax.ShapeDtypeStruct(s, d) for s, d in OU...  229 us
    unnamed x22, local copies, waits for them, and re-layouts  8.52 us

profile of v2, /device:TPU:0, one launch (start us, length us, event | category | flops | bytes accessed | tf_op | source)
XLA Modules:
  0.0 243.9 jit_solution(7479403539067639453)
XLA Ops:
  1.3 1.3 fusion.5.refs_5_
  2.6 1.6 pad_maximum_fusion.refs_4_
  4.2 229.4 %block.1 = (bf16[512,768]{1,0:T(8,128)(2,1)}, f32[512,768]{1,0:T(8,128)}, f32[2,48]{1,0:T(2,128)}, f32[3,48,384]{2,1,0:T(8,128)}, f32[48,384]{1,0:T(8,128)}, /*i...) custom-call(bf16[512,768]{1,0:T(8,128)(2,1)} %refs_0_.1, ...), custom_call_target="tpu_custom_call" | custom-call | tf_op jit(solution)/shard_map/block/pallas_call | solution.py:831
  233.5 0.0 copy-start
  233.6 2.2 copy.29
  235.7 0.0 copy-done
  235.7 0.0 copy-start.6
  235.7 0.0 copy-start.3
  235.7 0.0 copy-start.4
  235.8 0.0 copy-start.5
  235.8 0.0 copy-start.2
  235.8 1.1 copy.30
  236.9 0.0 copy-done.6
  236.9 0.6 copy.31
  237.5 0.0 copy-done.3
  237.5 0.7 copy.32
  238.2 0.0 copy-done.4
  238.2 0.6 copy.33
  238.8 0.0 copy-done.5
  238.8 0.6 copy.34
  239.4 0.0 copy-done.2
  239.4 0.0 copy-start.1
  239.4 1.0 copy.35
  240.4 0.7 copy-done.1
  241.1 1.0 copy.36
Async XLA Ops:
  233.5 2.2 copy-start
  235.7 1.2 copy-start.6
  235.7 1.7 copy-start.3
  235.7 2.4 copy-start.4
  235.8 3.1 %copy-start.5 = (f32[4,48]{1,0:T(4,128)S(1)}, f32[4,48]{1,0:T(4,128)}, u32[]{:S(2)}) copy-start(f32[4,48]{1,0:T(4,128)} %get-tuple-element.41) | copy-start | bytes 2308
  235.8 3.6 %copy-start.2 = (f32[4,48,1536]{2,1,0:T(8,128)S(1)}, f32[4,48,1536]{2,1,0:T(8,128)}, u32[]{:S(2)}) copy-start(f32[4,48,1536]{2,1,0:T(8,128)} %get-tuple-element.42) | copy-start | bytes 3538948
  239.4 1.7 copy-start.1

commit v3 on v2

--- a/solution.py
+++ b/solution.py
@@ -122,12 +122,17 @@
     cnt = jnp.sum(ohr, axis=1, keepdims=True)
     hi = jnp.floor(cnt * (1.0 / 256.0))
     lane16 = iota((16, 128), 1)
+    six = jnp.concatenate(
+        [R.gains[...].astype(F32), R.router[...].astype(F32), jnp.zeros((10, 48), F32)], axis=0
+    )
+    small = jnp.concatenate([six, jnp.zeros((16, 80), F32)], axis=1)
     R.SM[f] = jnp.where(
         lane16 == 48,
         cnt - 256.0 * hi,
-        jnp.where(lane16 == 49, hi, R.small[...].astype(F32)),
+        jnp.where(lane16 == 49, hi, small),
     ).astype(BF)
-    R.WA[z, c] = R.watt[...]
+    R.WA[z, c, pl.ds(0, 3)] = R.qkv[...]
+    R.WA[z, c, 3] = R.out[...]
     enter(pc)
     own = pl.ds(pl.multiple_of(t * 512, 512), 512)
     i_tok, i_cot, i_wo, i_att = w.ids(1), w.ids(1), w.ids(1), w.ids(1)
@@ -137,23 +142,26 @@
     i_m = [w.ids(4) for _ in range(6)]
     i_cz, i_dz, i_cp, i_dp = w.ids(4), w.ids(4), w.ids(1), w.ids(1)
 
-    za = [w.go(i_z + k, R.watt, R.WA.at[z, c], pc.Z(k)) for k in (1, 2, 3)]
     zs = [w.go(i_sz + k, R.SM.at[f], R.SM.at[f], pc.Z(k)) for k in (1, 2, 3)]
+    za = [w.go(i_z + k, R.WA.at[z, c], R.WA.at[z, c], pc.Z(k)) for k in (1, 2, 3)]
     cot_x = w.go(i_cot, R.cot, R.CT.at[own], pc.PAIR)
     tok_x = w.go(i_tok, R.tok, R.TK.at[own], pc.PAIR)
 
     def spread(k):
         zz = pc.zfrom(k)
         g = 4 * zz + c
+        d = w.go(i_sx + k, R.SM.at[g], R.SM.at[g], pc.X)
+        e = w.go(i_sy + k, R.SM.at[g], R.SM.at[g], pc.Y)
         a = w.go(i_x + k, R.WA.at[zz, c], R.WA.at[zz, c], pc.X)
         b = w.go(i_y + k, R.WA.at[zz, c], R.WA.at[zz, c], pc.Y)
-        d = w.go(i_sx + k, R.SM.at[g], R.SM.at[g], pc.X)
-        e = w.go(i_sy + k, R.SM.at[g], R.SM.at[g], pc.Y)
         return a, b, d, e
 
     def forward(k, got):
         zz = pc.zfrom(k)
         a, b, d, e = got
+        d.wait_recv()
+        g = 4 * zz + pc.cx
+        s = w.go(i_sf + k, R.SM.at[g], R.SM.at[g], pc.Y)
         a.wait_recv()
         x = w.go(
             i_fx + k,
@@ -161,9 +169,6 @@
             R.WA.at[zz, pc.cx, pl.ds(0, 2)],
             pc.Y,
         )
-        d.wait_recv()
-        g = 4 * zz + pc.cx
-        s = w.go(i_sf + k, R.SM.at[g], R.SM.at[g], pc.Y)
         b.wait_recv()
         y = w.go(
             i_fy + k,
@@ -332,14 +337,6 @@
 
     lax.fori_loop(0, 3, pair_of_heads, 0)
     att = w.go(i_att, R.ATO, R.ATX, pc.PAIR)
-    a = moe_spread(3)
-    a[0].wait_recv()
-    a[1].wait_recv()
-    for m in moe_forward(3):
-        m.start()
-    for m in cz:
-        m.wait_recv()
-    cp = w.go(i_cp, R.CR.at[:, t], R.CR.at[:, t], pc.PAIR)
     wo.wait_recv()
     att.wait_recv()
     lane = iota((256, 128), 1)
@@ -376,6 +373,14 @@
     lax.fori_loop(0, 4, moe_rows, 0)
     R.DR[z, t] = R.CS[z]
     dz = [w.go(i_dz + k, R.CS.at[pc.zto(k)], R.DR.at[z, t], pc.Z(k)) for k in (1, 2, 3)]
+    a = moe_spread(3)
+    a[0].wait_recv()
+    a[1].wait_recv()
+    for m in moe_forward(3):
+        m.start()
+    for m in cz:
+        m.wait_recv()
+    cp = w.go(i_cp, R.CR.at[:, t], R.CR.at[:, t], pc.PAIR)
     for k in range(4):
         a = moe_spread(k)
         b = moe_forward(k)
@@ -399,11 +404,158 @@
     return v * cdf, slope
 
 
+class ExpertSums:
+    def __init__(self, R, pc, w):
+        self.R, self.pc, self.w = R, pc, w
+        self.i1, self.i2, self.i3 = w.ids(8), w.ids(4), w.ids(16)
+
+    def step_one(self, g):
+        R, pc, w = self.R, self.pc, self.w
+        cols, i = pl.ds(768 * g, 768), self.i1 + 4 * g
+        return [
+            w.copy(i, R.UE.at[:, pc.cx, :, cols], R.RU.at[0, :, :, cols], pc.X),
+            w.copy(i + 1, R.UE.at[:, pc.cd, :, cols], R.RU.at[1, :, :, cols], pc.X),
+            w.copy(i + 2, R.DE.at[:, pc.cy, :, cols], R.RD.at[0, :, :, cols], pc.Y),
+            w.copy(i + 3, R.DE.at[:, pc.cd, :, cols], R.RD.at[1, :, :, cols], pc.Y),
+        ]
+
+    def step_two(self, g):
+        R, pc, w = self.R, self.pc, self.w
+        cols, i = pl.ds(768 * g, 768), self.i2 + 2 * g
+        return [
+            w.copy(i, R.UE.at[:, pc.cy, :, cols], R.RU2.at[:, :, cols], pc.Y),
+            w.copy(i + 1, R.DE.at[:, pc.cx, :, cols], R.RD2.at[:, :, cols], pc.X),
+        ]
+
+    def step_three(self, g):
+        R, pc, w = self.R, self.pc, self.w
+        cols, i, out = pl.ds(768 * g, 768), self.i3 + 8 * g, []
+        for k in (1, 2, 3):
+            to, z = pc.zto(k), pc.z
+            out.append(w.copy(i + k, R.UE.at[to, pc.c, :, cols], R.ZU.at[z, :, cols], pc.Z(k)))
+            out.append(w.copy(i + 4 + k, R.DE.at[to, pc.c, :, cols], R.ZD.at[z, :, cols], pc.Z(k)))
+        return out
+
+    def one(self, g):
+        for m in self.step_one(g):
+            m.start()
+
+    def two(self, g):
+        R, pc, cols = self.R, self.pc, pl.ds(768 * g, 768)
+        for m in self.step_one(g):
+            m.wait()
+
+        def add(zz, carry):
+            R.UE[zz, pc.cy, :, cols] = R.UE[zz, pc.cy, :, cols] + R.RU[1, zz, :, cols]
+            R.DE[zz, pc.cx, :, cols] = R.DE[zz, pc.cx, :, cols] + R.RD[1, zz, :, cols]
+            R.UE[zz, pc.c, :, cols] = R.UE[zz, pc.c, :, cols] + R.RU[0, zz, :, cols]
+            R.DE[zz, pc.c, :, cols] = R.DE[zz, pc.c, :, cols] + R.RD[0, zz, :, cols]
+            return carry
+
+        lax.fori_loop(0, 4, add, 0)
+        for m in self.step_two(g):
+            m.start()
+
+    def three(self, g):
+        R, pc, cols = self.R, self.pc, pl.ds(768 * g, 768)
+        for m in self.step_two(g):
+            m.wait()
+
+        def add(zz, carry):
+            R.UE[zz, pc.c, :, cols] = R.UE[zz, pc.c, :, cols] + R.RU2[zz, :, cols]
+            R.DE[zz, pc.c, :, cols] = R.DE[zz, pc.c, :, cols] + R.RD2[zz, :, cols]
+            return carry
+
+        lax.fori_loop(0, 4, add, 0)
+        for m in self.step_three(g):
+            m.start()
+
+    def last(self):
+        R, pc = self.R, self.pc
+        R.ZU[pc.z] = R.UE[pc.z, pc.c]
+        R.ZD[pc.z] = R.DE[pc.z, pc.c]
+        for g in (0, 1):
+            for m in self.step_three(g):
+                m.wait()
+        R.up_grad[...] = R.ZU[...].astype(F32)
+        R.down_grad[...] = R.ZD[...].astype(F32)
+
+
+class AttentionSums:
+    def __init__(self, R, pc, w):
+        self.R, self.pc, self.w = R, pc, w
+        self.i1, self.i2, self.i3 = w.ids(16), w.ids(8), w.ids(16)
+        self.low, self.high = pl.ds(0, 2), pl.ds(2, 2)
+
+    def step_one(self, n):
+        R, pc, w, i = self.R, self.pc, self.w, self.i1 + 4 * n
+        return [
+            w.copy(i, R.AG.at[n, self.low, pc.cx], R.RA.at[n, 0], pc.X),
+            w.copy(i + 1, R.AG.at[n, self.low, pc.cd], R.RA.at[n, 1], pc.X),
+            w.copy(i + 2, R.AG.at[n, self.high, pc.cy], R.RB.at[n, 0], pc.Y),
+            w.copy(i + 3, R.AG.at[n, self.high, pc.cd], R.RB.at[n, 1], pc.Y),
+        ]
+
+    def step_two(self, n):
+        R, pc, w, i = self.R, self.pc, self.w, self.i2 + 2 * n
+        return [
+            w.copy(i, R.AG.at[n, self.low, pc.cy], R.RA2.at[n], pc.Y),
+            w.copy(i + 1, R.AG.at[n, self.high, pc.cx], R.RB2.at[n], pc.X),
+        ]
+
+    def step_three(self, n):
+        R, pc, w, i = self.R, self.pc, self.w, self.i3 + 4 * n
+        return [
+            w.copy(i + k, R.AG.at[n, pc.zto(k), pc.c], R.ZA.at[n, pc.z], pc.Z(k))
+            for k in (1, 2, 3)
+        ]
+
+    def one(self, n):
+        for m in self.step_one(n):
+            m.start()
+
+    def two(self, n):
+        R, pc = self.R, self.pc
+        for m in self.step_one(n):
+            m.wait()
+        for j in range(2):
+            R.AG[n, j, pc.cy] = R.AG[n, j, pc.cy] + R.RA[n, 1, j]
+            R.AG[n, 2 + j, pc.cx] = R.AG[n, 2 + j, pc.cx] + R.RB[n, 1, j]
+            R.AG[n, j, pc.c] = R.AG[n, j, pc.c] + R.RA[n, 0, j]
+            R.AG[n, 2 + j, pc.c] = R.AG[n, 2 + j, pc.c] + R.RB[n, 0, j]
+        for m in self.step_two(n):
+            m.start()
+
+    def three(self, n):
+        R, pc = self.R, self.pc
+        for m in self.step_two(n):
+            m.wait()
+        for j in range(2):
+            R.AG[n, j, pc.c] = R.AG[n, j, pc.c] + R.RA2[n, j]
+            R.AG[n, 2 + j, pc.c] = R.AG[n, 2 + j, pc.c] + R.RB2[n, j]
+        for m in self.step_three(n):
+            m.start()
+
+    def last(self, n):
+        R, pc = self.R, self.pc
+        R.ZA[n, pc.z] = R.AG[n, pc.z, pc.c]
+        for m in self.step_three(n):
+            m.wait()
+        total = R.ZA[n, 0].astype(F32)
+        for zz in range(1, 4):
+            total = total + R.ZA[n, zz].astype(F32)
+        for j in range(3):
+            block = total[48 * j : 48 * j + 48]
+            if n == 0:
+                R.out_grad[:, 128 * j : 128 * j + 128] = block
+            else:
+                R.qkv_grad[j, :, 128 * (n - 1) : 128 * n] = block
+
+
 def phase_b(R, pc, w):
     f, t, z, c, o = pc.f, pc.t, pc.z, pc.c, pc.o
     i_xe, i_xg = w.ids(1), w.ids(1)
     i_rg, i_re, i_rgp, i_rep = w.ids(4), w.ids(4), w.ids(1), w.ids(1)
-    i_u1, i_u2, i_d1, i_d2 = w.ids(2), w.ids(1), w.ids(2), w.ids(1)
     DR, CR = R.DR.reshape(ROWS, WIDE), R.CR.reshape(ROWS, WIDE)
     EO, GM = R.EO.reshape(ROWS, WIDE), R.GM.reshape(ROWS, WIDE)
     lane = iota((256, 128), 1)
@@ -447,13 +599,9 @@
     lax.fori_loop(0, 4, partials, 0)
     xg = w.go(i_xg, R.CS, R.XG, pc.PAIR)
     xe = w.go(i_xe, R.ES, R.XE, pc.PAIR)
-    R.moe_sums = [
-        w.go(i_u1, R.UE.at[:, pc.cx], R.RU.at[0], pc.X),
-        w.go(i_u1 + 1, R.UE.at[:, pc.cd], R.RU.at[1], pc.X),
-        w.go(i_d1, R.DE.at[:, pc.cy], R.RD.at[0], pc.Y),
-        w.go(i_d1 + 1, R.DE.at[:, pc.cd], R.RD.at[1], pc.Y),
-    ]
-    R.i_u2, R.i_d2 = i_u2, i_d2
+    sums = ExpertSums(R, pc, w)
+    sums.one(0)
+    sums.one(1)
     xg.wait()
     xe.wait()
     w.open = [m for m in w.open if m is not xg and m is not xe]
@@ -475,13 +623,15 @@
     lax.fori_loop(0, 4, finish, 0)
     R.RGR[...] = jnp.where(iota((16, WIDE), 0) == 2 + z, R.RGR[0:1], 0.0)
     rg = [w.go(i_rg + k, R.CS.at[pc.zto(k)], R.RG.at[z, t], pc.Z(k)) for k in (1, 2, 3)]
-    re = [w.go(i_re + k, R.ES.at[pc.zto(k)], R.RE.at[z, t], pc.Z(k)) for k in (1, 2, 3)]
     R.RG[z, t] = R.CS[z]
     R.RE[z, t] = R.ES[z]
     for m in rg:
         m.wait_recv()
-    w.go(i_rgp, R.RG.at[:, t], R.RG.at[:, t], pc.PAIR).wait_recv()
-    R.expert_rows = (re, i_rep)
+    back = w.go(i_rgp, R.RG.at[:, t], R.RG.at[:, t], pc.PAIR)
+    re = [w.go(i_re + k, R.ES.at[pc.zto(k)], R.RE.at[z, t], pc.Z(k)) for k in (1, 2, 3)]
+    back.wait_recv()
+    sums.two(0)
+    return sums, re, i_rep
 
 
 def combine(key, rows, got):
@@ -491,10 +641,9 @@
     return mm(pick, got)
 
 
-def phase_c(R, pc, w):
+def phase_c(R, pc, w, sums, re, i_rep):
     f, t, z, c, o = pc.f, pc.t, pc.z, pc.c, pc.o
-    i_uz, i_dz = w.ids(4), w.ids(4)
-    i_a1, i_a2, i_b1, i_b2, i_az = w.ids(2), w.ids(1), w.ids(2), w.ids(1), w.ids(4)
+    att = AttentionSums(R, pc, w)
     i_n = w.ids(1)
     i_sp, i_sc, i_sz = w.ids(1), w.ids(4), w.ids(4)
     own = pl.ds(pl.multiple_of(t * 512, 512), 512)
@@ -548,7 +697,15 @@
         + part
         + jnp.where(iota((16, WIDE), 0) == 6, sums6, 0.0)
     )
-    R.AG[:, :, 3] = mm(GBR[...], R.ATO[...], 0, 0).astype(BF).reshape(4, 4, 48, HALF)
+
+    def place(n, grad):
+        for j in range(3):
+            block = grad[:, 128 * j : 128 * j + 128].astype(BF).reshape(4, 4, 48, 128)
+            R.AG[n, :, :, pl.ds(48 * j, 48)] = block
+
+    place(0, mm(GBR[...], R.ATO[...], 0, 0))
+    sums.two(1)
+    att.one(0)
     prefix = R.pre[0]
 
     def pair_of_heads(p, carry):
@@ -582,30 +739,23 @@
             R.QS[p, cols] = (both * 0.125).T.astype(BF)
         R.KS[p] = R.DK[...].astype(BF)
         R.VS[p] = R.DV[...].astype(BF)
-        mu, md = R.UE.at[:, c], R.DE.at[:, c]
+        joined = jnp.concatenate([R.QS[p], R.KS[p], R.VS[p]], axis=1)
+        place(p + 1, mm(R.NM[...], joined, 0, 0))
+        att.one(p + 1)
 
         @pl.when(p == 0)
         def _():
-            for m in R.moe_sums:
-                m.wait_recv()
-            for zz in range(4):
-                R.UE[zz, c] = R.UE[zz, c] + R.RU[0, zz]
-                R.UE[zz, pc.cy] = R.UE[zz, pc.cy] + R.RU[1, zz]
-                R.DE[zz, c] = R.DE[zz, c] + R.RD[0, zz]
-                R.DE[zz, pc.cx] = R.DE[zz, pc.cx] + R.RD[1, zz]
-            w.copy(R.i_u2, R.UE.at[:, pc.cy], R.RU2, pc.Y).start()
-            w.copy(R.i_d2, R.DE.at[:, pc.cx], R.RD2, pc.X).start()
+            sums.three(0)
 
         @pl.when(p == 1)
         def _():
-            w.copy(R.i_u2, R.UE.at[:, pc.cy], R.RU2, pc.Y).wait()
-            w.copy(R.i_d2, R.DE.at[:, pc.cx], R.RD2, pc.X).wait()
-            for zz in range(4):
-                R.UE[zz, c] = R.UE[zz, c] + R.RU2[zz]
-                R.DE[zz, c] = R.DE[zz, c] + R.RD2[zz]
-            for k in (1, 2, 3):
-                w.copy(i_uz + k, R.UE.at[pc.zto(k), c], R.ZU.at[z], pc.Z(k)).start()
-                w.copy(i_dz + k, R.DE.at[pc.zto(k), c], R.ZD.at[z], pc.Z(k)).start()
+            sums.three(1)
+            att.two(0)
+
+        @pl.when(p == 2)
+        def _():
+            att.three(0)
+            att.two(1)
 
         return carry
 
@@ -626,18 +776,8 @@
     XS, XN, BO = (r.reshape(512, WIDE) for r in (R.CS, R.XG, R.ES))
     XS[...] = GN[other].astype(BF)
     xn = w.go(i_n, XS, XN, pc.PAIR)
-    every = pl.ds(0, ROWS)
-    for s in range(3):
-        R.AG[:, :, s] = mm(R.NM[...], grads(GP[s], every), 0, 0).astype(BF).reshape(4, 4, 48, HALF)
-    a_half, b_half = pl.ds(0, 2), pl.ds(2, 2)
-    a1 = [
-        w.go(i_a1, R.AG.at[:, pc.cx, a_half], R.RA.at[0], pc.X),
-        w.go(i_a1 + 1, R.AG.at[:, pc.cd, a_half], R.RA.at[1], pc.X),
-    ]
-    b1 = [
-        w.go(i_b1, R.AG.at[:, pc.cy, b_half], R.RB.at[0], pc.Y),
-        w.go(i_b1 + 1, R.AG.at[:, pc.cd, b_half], R.RB.at[1], pc.Y),
-    ]
+    att.two(2)
+    att.three(1)
     xn.wait_recv()
     R.G2[...] = jnp.zeros((8, WIDE), F32)
 
@@ -657,15 +797,8 @@
     out_t.start()
     R.SB[0:1] = R.G2[0:1]
     sp = w.go(i_sp, R.SB, R.SP, pc.PAIR)
-    for m in a1 + b1:
-        m.wait_recv()
-    for zz in range(4):
-        R.AG[zz, c, a_half] = R.AG[zz, c, a_half] + R.RA[0, zz]
-        R.AG[zz, pc.cy, a_half] = R.AG[zz, pc.cy, a_half] + R.RA[1, zz]
-        R.AG[zz, c, b_half] = R.AG[zz, c, b_half] + R.RB[0, zz]
-        R.AG[zz, pc.cx, b_half] = R.AG[zz, pc.cx, b_half] + R.RB[1, zz]
-    a2 = w.go(i_a2, R.AG.at[:, pc.cy, a_half], R.RA2, pc.Y)
-    b2 = w.go(i_b2, R.AG.at[:, pc.cx, b_half], R.RB2, pc.X)
+    att.two(3)
+    att.three(2)
     sp.wait_recv()
     me = R.SB[...] + R.SP[...]
     R.SC[c] = me
@@ -674,7 +807,6 @@
         w.go(i_sc + 1, R.SC.at[c], R.SC.at[c], pc.Y),
         w.go(i_sc + 2, R.SC.at[c], R.SC.at[c], pc.DIAG),
     ]
-    re, i_rep = R.expert_rows
     for m in re:
         m.wait_recv()
     w.go(i_rep, R.RE.at[:, t], R.RE.at[:, t], pc.PAIR).wait_recv()
@@ -689,23 +821,14 @@
     lax.fori_loop(0, 2, block_rows, 0)
     out_b = pltpu.make_async_copy(BO, R.block_out, R.ls.at[1])
     out_b.start()
-    a2.wait_recv()
-    b2.wait_recv()
-    for zz in range(4):
-        R.AG[zz, c, a_half] = R.AG[zz, c, a_half] + R.RA2[zz]
-        R.AG[zz, c, b_half] = R.AG[zz, c, b_half] + R.RB2[zz]
-    az = [w.go(i_az + k, R.AG.at[pc.zto(k), c], R.ZA.at[z], pc.Z(k)) for k in (1, 2, 3)]
+    att.three(3)
     for m in sc:
         m.wait_recv()
     R.SZ[z] = R.SC[0] + R.SC[1] + R.SC[2] + R.SC[3]
     sz = [w.go(i_sz + k, R.SZ.at[z], R.SZ.at[z], pc.Z(k)) for k in (1, 2, 3)]
-    R.ZU[z] = R.UE[z, c]
-    R.ZD[z] = R.DE[z, c]
-    for k in (1, 2, 3):
-        w.copy(i_uz + k, R.UE.at[pc.zto(k), c], R.ZU.at[z], pc.Z(k)).wait()
-        w.copy(i_dz + k, R.DE.at[pc.zto(k), c], R.ZD.at[z], pc.Z(k)).wait()
-    R.up_grad[...] = R.ZU[...].astype(F32)
-    R.down_grad[...] = R.ZD[...].astype(F32)
+    sums.last()
+    for n in range(3):
+        att.last(n)
     for m in sz:
         m.wait_recv()
     total = R.SZ[0] + R.SZ[1] + R.SZ[2] + R.SZ[3]
@@ -719,14 +842,7 @@
         total = total - top.astype(F32)
     R.gains_grad[...] = mine[0:2, 0:48]
     R.router_grad[...] = mine[2:6, 0:48]
-    R.ZA[z] = R.AG[z, c]
-    for m in az:
-        m.wait_recv()
-    summed = R.ZA[0].astype(F32)
-    for zz in range(1, 4):
-        summed = summed + R.ZA[zz].astype(F32)
-    R.qkv_grad[...] = summed[0:3]
-    R.out_grad[...] = summed[3]
+    att.last(3)
     out_t.wait()
     out_b.wait()
     w.flush()
@@ -795,22 +911,22 @@
     "DD": ((3, 8, ROWS), F32),
     "DK": ((ROWS, 128), F32),
     "DV": ((ROWS, 128), F32),
-    "AG": ((4, 4, 4, 48, HALF), BF),
-    "RA": ((2, 4, 2, 48, HALF), BF),
-    "RB": ((2, 4, 2, 48, HALF), BF),
-    "RA2": ((4, 2, 48, HALF), BF),
-    "RB2": ((4, 2, 48, HALF), BF),
-    "ZA": ((4, 4, 48, HALF), BF),
+    "AG": ((4, 4, 4, 144, 128), BF),
+    "RA": ((4, 2, 2, 144, 128), BF),
+    "RB": ((4, 2, 2, 144, 128), BF),
+    "RA2": ((4, 2, 144, 128), BF),
+    "RB2": ((4, 2, 144, 128), BF),
+    "ZA": ((4, 4, 144, 128), BF),
     "G2": ((8, WIDE), F32),
     "SB": ((16, WIDE), F32),
     "SP": ((16, WIDE), F32),
     "SC": ((4, 16, WIDE), F32),
     "SZ": ((4, 16, WIDE), F32),
 }
-INS = ("tok", "cot", "pre", "idr", "watt", "small", "up", "down")
+INS = ("tok", "cot", "pre", "idr", "gains", "qkv", "out", "router", "up", "down")
 IN_HBM = ("tok", "cot", "up", "down")
 OUT_HBM = ("block_out", "tokens_grad")
-SEMAPHORES = 160
+SEMAPHORES = 192
 
 
 def fused(args):
@@ -821,8 +937,8 @@
         pc = Place()
         w = Wire(R.ss, R.rs)
         phase_a(R, pc, w)
-        phase_b(R, pc, w)
-        phase_c(R, pc, w)
+        sums, re, i_rep = phase_b(R, pc, w)
+        phase_c(R, pc, w, sums, re, i_rep)
 
     vm = pl.BlockSpec(memory_space=pltpu.VMEM)
     hbm = pl.BlockSpec(memory_space=pl.ANY)
@@ -845,9 +961,8 @@
 def prepare(
     tokens, cotangent, prefix_len, expert_ids, norm_gains, qkv_weight, out_weight, router_weight, up_weight, down_weight
 ):
-    watt = jnp.concatenate([qkv_weight, out_weight[None]], axis=0)
-    small = jnp.pad(jnp.concatenate([norm_gains, router_weight], axis=0), ((0, 10), (0, 80)))
-    return (tokens, cotangent, prefix_len, expert_ids.reshape(1, ROWS), watt, small, up_weight, down_weight)
+    ids = expert_ids.reshape(1, ROWS)
+    return (tokens, cotangent, prefix_len, ids, norm_gains, qkv_weight, out_weight, router_weight, up_weight, down_weight)
 
 
 def fast_device(*args):

time: 244 us -> 211 us (0.86)
  Pallas kernels: 229 us -> 199 us
  other arithmetic: 2.88 us -> 0 us
    pallas_call x1, Pallas kernels: 229 us -> 199 us  [fused(): pl.pallas_call(body, out_shape=[jax.ShapeDtypeStruct(s, d) for s, d in OU...]
    concatenate x2 -> x0, other arithmetic: 2.88 us -> none  [the longest x1 1.6 us: prepare(): watt = jnp.concatenate([qkv_weight, out_weight[None]], axis=0)]
where the time goes in v3:
time: 211 us
  Pallas kernels  199 us (94%)
  local copies, waits for them, and re-layouts  8.52 us (4%)
  between operations  3.1 us (1%)
    pallas_call x1, Pallas kernels, fused(): pl.pallas_call(body, out_shape=[jax.ShapeDtypeStruct(s, d) for s, d in OU...  199 us
    unnamed x22, local copies, waits for them, and re-layouts  8.52 us

profile of v3, /device:TPU:0, one launch (start us, length us, event | category | flops | bytes accessed | tf_op | source)
XLA Modules:
  0.0 210.6 jit_solution(2195739007230112902)
XLA Ops:
  1.3 198.9 %block.1 = (bf16[512,768]{1,0:T(8,128)(2,1)}, f32[512,768]{1,0:T(8,128)}, f32[2,48]{1,0:T(2,128)}, f32[3,48,384]{2,1,0:T(8,128)}, f32[48,384]{1,0:T(8,128)}, /*i...) custom-call(bf16[512,768]{1,0:T(8,128)(2,1)} %refs_0_.1, ...), custom_call_target="tpu_custom_call" | custom-call | tf_op jit(solution)/shard_map/block/pallas_call | solution.py:947
  200.2 0.0 copy-start
  200.2 2.2 %copy.29 = bf16[512,768]{1,0:T(8,128)(2,1)} copy(bf16[512,768]{1,0:T(8,128)(2,1)} %get-tuple-element.36) | data formatting | bytes 1572864
  202.4 0.0 copy-done
  202.4 0.0 copy-start.6
  202.4 0.0 copy-start.3
  202.4 0.0 copy-start.4
  202.4 0.0 copy-start.5
  202.4 0.0 copy-start.2
  202.5 1.1 copy.30
  203.6 0.0 copy-done.6
  203.6 0.6 copy.31
  204.2 0.0 copy-done.3
  204.2 0.7 copy.32
  204.9 0.0 copy-done.4
  204.9 0.6 copy.33
  205.5 0.0 copy-done.5
  205.5 0.6 copy.34
  206.1 0.0 copy-done.2
  206.1 0.0 copy-start.1
  206.1 1.0 copy.35
  207.1 0.7 copy-done.1
  207.8 1.0 copy.36
Async XLA Ops:
  200.2 2.2 %copy-start = (f32[512,768]{1,0:T(8,128)S(1)}, f32[512,768]{1,0:T(8,128)}, u32[]{:S(2)}) copy-start(f32[512,768]{1,0:T(8,128)} %get-tuple-element.37) | copy-start | bytes 4718596
  202.4 1.2 copy-start.6
  202.4 1.7 copy-start.3
  202.4 2.4 %copy-start.4 = (f32[48,384]{1,0:T(8,128)S(1)}, f32[48,384]{1,0:T(8,128)}, u32[]{:S(2)}) copy-start(f32[48,384]{1,0:T(8,128)} %get-tuple-element.40) | copy-start | bytes 221188
  202.4 3.1 %copy-start.5 = (f32[4,48]{1,0:T(4,128)S(1)}, f32[4,48]{1,0:T(4,128)}, u32[]{:S(2)}) copy-start(f32[4,48]{1,0:T(4,128)} %get-tuple-element.41) | copy-start | bytes 2308
  202.4 3.6 %copy-start.2 = (f32[4,48,1536]{2,1,0:T(8,128)S(1)}, f32[4,48,1536]{2,1,0:T(8,128)}, u32[]{:S(2)}) copy-start(f32[4,48,1536]{2,1,0:T(8,128)} %get-tuple-element.42) | copy-start | bytes 3538948
  206.1 1.7 copy-start.1

commit v4 on v3

--- a/solution.py
+++ b/solution.py
@@ -91,11 +91,19 @@
         self.open = []
 
 
+def joined(ref, rows):
+    return jnp.concatenate([ref[p, rows] for p in range(3)], axis=1)
+
+
 def enter(pc):
     barrier = pltpu.get_barrier_semaphore()
     for dev in (pc.PAIR, pc.X, pc.Y, pc.DIAG, pc.Z(1), pc.Z(2), pc.Z(3)):
         pl.semaphore_signal(barrier, inc=1, device_id=dev, device_id_type=MESH)
     pl.semaphore_wait(barrier, 7)
+
+
+def order(i):
+    return i + lax.div(i, 2) * (5 - 2 * i)
 
 
 def visible(krow0, kn, qcol0, qn, prefix):
@@ -135,12 +143,12 @@
     R.WA[z, c, 3] = R.out[...]
     enter(pc)
     own = pl.ds(pl.multiple_of(t * 512, 512), 512)
-    i_tok, i_cot, i_wo, i_att = w.ids(1), w.ids(1), w.ids(1), w.ids(1)
+    i_tok, i_cot, i_wo, i_att = w.ids(1), w.ids(1), w.ids(1), w.ids(3)
     i_z, i_sz = w.ids(4), w.ids(4)
     i_x, i_y, i_fx, i_fy, i_sx, i_sy, i_sf = (w.ids(4) for _ in range(7))
     i_mu, i_md = w.ids(4), w.ids(4)
     i_m = [w.ids(4) for _ in range(6)]
-    i_cz, i_dz, i_cp, i_dp = w.ids(4), w.ids(4), w.ids(1), w.ids(1)
+    i_cz, i_dz, i_cp, i_dp = w.ids(4), w.ids(4), w.ids(1), w.ids(4)
 
     zs = [w.go(i_sz + k, R.SM.at[f], R.SM.at[f], pc.Z(k)) for k in (1, 2, 3)]
     za = [w.go(i_z + k, R.WA.at[z, c], R.WA.at[z, c], pc.Z(k)) for k in (1, 2, 3)]
@@ -206,11 +214,11 @@
     cot_x.wait_recv()
 
     def cot_rows(e, carry):
-        R.CS[e] = mm(R.DM[pl.ds(pl.multiple_of(e * 128, 128), 128)], R.CT[...]).astype(BF)
+        R.PG[e] = mm(R.DM[pl.ds(pl.multiple_of(e * 128, 128), 128)], R.CT[...]).astype(BF)
         return carry
 
     lax.fori_loop(0, 4, cot_rows, 0)
-    R.CR[z, t] = R.CS[z]
+    R.CR[z, t] = R.PG[z]
     za[1].wait_recv()
     zs[1].wait_recv()
     got[2] = spread(2)
@@ -219,14 +227,14 @@
     got[3] = spread(3)
     mu = [w.go(i_mu + k, R.up.at[pc.zto(k)], R.UE.at[z, c], pc.Z(k)) for k in (1, 2, 3)]
     md = [w.go(i_md + k, R.down.at[pc.zto(k)], R.DE.at[z, c], pc.Z(k)) for k in (1, 2, 3)]
-    cz = [w.go(i_cz + k, R.CS.at[pc.zto(k)], R.CR.at[z, t], pc.Z(k)) for k in (1, 2, 3)]
+    cz = [w.go(i_cz + k, R.PG.at[pc.zto(k)], R.CR.at[z, t], pc.Z(k)) for k in (1, 2, 3)]
     ends = [forward(k, got[k]) for k in range(4)]
 
     tok_x.wait_recv()
 
     def factors(rows):
         x = R.TK[rows].astype(F32)
-        R.F1[rows] = lax.rsqrt(jnp.mean(x * x, axis=1, keepdims=True) + norm_eps)
+        R.STAT[rows, 0:1] = lax.rsqrt(jnp.mean(x * x, axis=1, keepdims=True) + norm_eps)
 
     blocks(ROWS, 128, factors)
     for x, y, s in ends:
@@ -250,7 +258,7 @@
 
     def norm_one(rows):
         x = R.TK[rows].astype(F32)
-        R.NM[rows] = (x * R.F1[rows] * R.VEC[0:1]).astype(BF)
+        R.NM[rows] = (x * R.STAT[rows, 0:1] * R.VEC[0:1]).astype(BF)
 
     blocks(ROWS, 128, norm_one)
     for x, y, s in ends:
@@ -318,7 +326,8 @@
                 R.LT[p, i : i + 1, cols] = top + jnp.log(total_e)
                 outs.append(out / total_e)
             both = jnp.where(iota((128, 256), 0) < 64, outs[0], outs[1])
-            R.ATO[cols, pl.ds(pl.multiple_of(p * 128, 128), 128)] = both.T.astype(BF)
+            R.ATO[p, cols] = both.T.astype(BF)
+        w.copy(i_att + p, R.ATO.at[p], R.ATX.at[p], pc.PAIR).start()
 
         @pl.when(p < 3)
         def _():
@@ -336,26 +345,26 @@
         return carry
 
     lax.fori_loop(0, 3, pair_of_heads, 0)
-    att = w.go(i_att, R.ATO, R.ATX, pc.PAIR)
     wo.wait_recv()
-    att.wait_recv()
+    for p in range(3):
+        w.copy(i_att + p, R.ATO.at[p], R.ATX.at[p], pc.PAIR).wait()
     lane = iota((256, 128), 1)
     real = (lane >= 2) & (lane < 6)
     R.PS[...] = jnp.zeros((8, 128), F32)
 
     def out_block(rows):
-        b = mm(R.ATO[rows], R.WA[:, :, 3].reshape(WIDE, HALF), 1, 1)
-        b = b + mm(R.ATX[rows], R.WO[...].reshape(WIDE, HALF), 1, 1)
+        b = mm(joined(R.ATO, rows), R.WA[:, :, 3].reshape(WIDE, HALF), 1, 1)
+        b = b + mm(joined(R.ATX, rows), R.WO[...].reshape(WIDE, HALF), 1, 1)
         h = R.TK[rows].astype(F32) + b
         R.HIDN[rows] = h
         f2 = lax.rsqrt(jnp.mean(h * h, axis=1, keepdims=True) + norm_eps)
-        R.F2[rows] = f2
+        R.STAT[rows, 1:2] = f2
         moe = (h * f2 * R.VEC[1:2]).astype(BF)
-        R.MOE[rows] = moe
+        R.GC[rows] = moe
         logits = mm(moe, R.RW[...])
         mine = jnp.where((lane - 2).astype(F32) == R.PR[rows], logits, 0.0)
         picked = jnp.sum(jnp.where(real, mine, 0.0), axis=1, keepdims=True)
-        R.GV[rows] = jax.nn.sigmoid(picked)
+        R.STAT[rows, 2:3] = jax.nn.sigmoid(picked)
         lg = jnp.where(real, logits, masked_score)
         e = jnp.exp(lg - jnp.max(lg, axis=1, keepdims=True))
         e = jnp.where(real, e, 0.0)
@@ -365,14 +374,20 @@
 
     blocks(ROWS, 256, out_block)
 
-    def moe_rows(e, carry):
-        R.CS[e] = mm(R.DM[pl.ds(pl.multiple_of(e * 128, 128), 128)], R.MOE[...]).astype(BF)
+    def moe_rows(i, carry):
+        k = order(lax.rem(i + 1, 4))
+        e = pc.zto(k)
+        R.CS[e] = mm(R.DM[pl.ds(pl.multiple_of(e * 128, 128), 128)], R.GC[...]).astype(BF)
+
+        @pl.when(i < 3)
+        def _():
+            w.copy(i_dz + k, R.CS.at[e], R.DR.at[z, t], pc.Z(k)).start()
+
         return carry
 
-    w.flush()
     lax.fori_loop(0, 4, moe_rows, 0)
     R.DR[z, t] = R.CS[z]
-    dz = [w.go(i_dz + k, R.CS.at[pc.zto(k)], R.DR.at[z, t], pc.Z(k)) for k in (1, 2, 3)]
+    w.copy(i_dp, R.DR.at[z, t], R.DR.at[z, t], pc.PAIR).start()
     a = moe_spread(3)
     a[0].wait_recv()
     a[1].wait_recv()
@@ -390,12 +405,9 @@
         b[1].wait_recv()
         for m in a + b:
             m.wait_send()
-    for m in dz:
-        m.wait_recv()
-    dp = w.go(i_dp, R.DR.at[:, t], R.DR.at[:, t], pc.PAIR)
     cp.wait_recv()
-    dp.wait_recv()
     w.flush()
+    return i_dz, i_dp
 
 
 def gelu_parts(v):
@@ -411,7 +423,7 @@
 
     def step_one(self, g):
         R, pc, w = self.R, self.pc, self.w
-        cols, i = pl.ds(768 * g, 768), self.i1 + 4 * g
+        cols, i = pl.ds(pl.multiple_of(768 * g, 128), 768), self.i1 + 4 * g
         return [
             w.copy(i, R.UE.at[:, pc.cx, :, cols], R.RU.at[0, :, :, cols], pc.X),
             w.copy(i + 1, R.UE.at[:, pc.cd, :, cols], R.RU.at[1, :, :, cols], pc.X),
@@ -436,10 +448,6 @@
             out.append(w.copy(i + 4 + k, R.DE.at[to, pc.c, :, cols], R.ZD.at[z, :, cols], pc.Z(k)))
         return out
 
-    def one(self, g):
-        for m in self.step_one(g):
-            m.start()
-
     def two(self, g):
         R, pc, cols = self.R, self.pc, pl.ds(768 * g, 768)
         for m in self.step_one(g):
@@ -474,11 +482,18 @@
         R, pc = self.R, self.pc
         R.ZU[pc.z] = R.UE[pc.z, pc.c]
         R.ZD[pc.z] = R.DE[pc.z, pc.c]
+        out = []
         for g in (0, 1):
             for m in self.step_three(g):
                 m.wait()
-        R.up_grad[...] = R.ZU[...].astype(F32)
-        R.down_grad[...] = R.ZD[...].astype(F32)
+            cols = pl.ds(768 * g, 768)
+            for j, (got, to) in enumerate(((R.ZU, R.up_grad), (R.ZD, R.down_grad))):
+                held = R.HIDN.at[pl.ds(192 * (2 * g + j), 192)].reshape(4, 48, 768)
+                held[...] = got[:, :, cols].astype(F32)
+                m = pltpu.make_async_copy(held, to.at[:, :, cols], R.ls.at[2 * g + j])
+                m.start()
+                out.append(m)
+        return out
 
 
 class AttentionSums:
@@ -552,86 +567,130 @@
                 R.qkv_grad[j, :, 128 * (n - 1) : 128 * n] = block
 
 
-def phase_b(R, pc, w):
+def phase_b(R, pc, w, i_dz, i_dp):
     f, t, z, c, o = pc.f, pc.t, pc.z, pc.c, pc.o
-    i_xe, i_xg = w.ids(1), w.ids(1)
+    i_xe, i_xg = w.ids(4), w.ids(4)
     i_rg, i_re, i_rgp, i_rep = w.ids(4), w.ids(4), w.ids(1), w.ids(1)
-    DR, CR = R.DR.reshape(ROWS, WIDE), R.CR.reshape(ROWS, WIDE)
-    EO, GM = R.EO.reshape(ROWS, WIDE), R.GM.reshape(ROWS, WIDE)
     lane = iota((256, 128), 1)
-
-    def gates(rows):
-        logits = mm(DR[rows], R.RW[...])
+    row = jnp.sum(
+        jnp.where(iota((16, WIDE), 0) == 2 + z, R.VEC[...], 0.0), axis=0, keepdims=True
+    )
+    R.RGR[...] = jnp.zeros((16, WIDE), F32)
+
+    def to_plane(s):
+        return {"fsdp": 4 * s + c, "tensor": t}
+
+    def rows_in(k):
+        return w.copy(i_dz + k, R.CS.at[pc.zto(k)], R.DR.at[z, t], pc.Z(k))
+
+    def rows_pair(k):
+        s = pc.zfrom(k)
+        return w.copy(i_dp + k, R.DR.at[s, t], R.DR.at[s, t], pc.PAIR)
+
+    def pair_sums(k):
+        s = pc.zfrom(k)
+        return (
+            w.copy(i_xg + k, R.PG.at[s], R.XG.at[s], pc.PAIR),
+            w.copy(i_xe + k, R.PE.at[s], R.XE.at[s], pc.PAIR),
+        )
+
+    def home(k):
+        s = pc.zfrom(k)
+        return w.copy(i_rg + k, R.XG.at[s], R.RG.at[z, t], to_plane(s))
+
+    def home_out(k):
+        s = pc.zfrom(k)
+        return w.copy(i_re + k, R.XE.at[s], R.RE.at[z, t], to_plane(s))
+
+    def finish(k):
+        s = pc.zfrom(k)
+        for m in pair_sums(k):
+            m.wait()
+        eo = R.EOO[s] + R.XE[s].astype(F32)
+        gate = R.STAT[pl.ds(pl.multiple_of(s * 256 + t * 128, 128), 128), 3:4]
+        gate_grad = jnp.sum(R.CR[s, t].astype(F32) * eo, axis=1, keepdims=True)
+        gs = gate_grad * gate * (1.0 - gate)
+        R.RGR[0:1] += jnp.sum(gs * R.DR[s, t].astype(F32), axis=0, keepdims=True)
+        R.XG[s] = (R.GMO[s] + R.XG[s].astype(F32) + gs * row).astype(BF)
+        R.XE[s] = eo.astype(BF)
+
+    def source(i, carry):
+        k = order(i)
+        s = pc.zfrom(k)
+        rows = pl.ds(pl.multiple_of(s * 256, 256), 256)
+
+        @pl.when(i > 0)
+        def _():
+            rows_in(k).wait()
+            rows_pair(k).start()
+            last = order(i - 1)
+            finish(last)
+
+            @pl.when(i > 1)
+            def _():
+                home(last).start()
+
+        rows_pair(k).wait()
+        x = R.DR[s].reshape(256, WIDE)
+        logits = mm(x, R.RW[...])
         gate = jax.nn.sigmoid(
             jnp.sum(jnp.where(lane == 2 + z, logits, 0.0), axis=1, keepdims=True)
         )
-        R.GATE[rows] = gate
-        R.GC[rows] = (gate * CR[rows].astype(F32)).astype(BF)
-        EO[rows] = jnp.zeros((256, WIDE), F32)
-        GM[rows] = jnp.zeros((256, WIDE), F32)
-
-    blocks(ROWS, 256, gates)
-
-    def hidden_units(cols):
-        up = R.UE[:, :, :, cols].reshape(WIDE, 512)
-        down = R.DE[:, :, :, cols].reshape(WIDE, 512)
-
-        def tokens_block(rows):
-            act, slope = gelu_parts(mm(DR[rows], up))
+        R.STAT[rows, 3:4] = gate
+        R.GC[rows] = (gate * R.CR[s].reshape(256, WIDE).astype(F32)).astype(BF)
+        R.EOB[...] = jnp.zeros((2, 128, WIDE), F32)
+        R.GMB[...] = jnp.zeros((2, 128, WIDE), F32)
+
+        def hidden_units(cols):
+            up = R.UE[:, :, :, cols].reshape(WIDE, 512)
+            down = R.DE[:, :, :, cols].reshape(WIDE, 512)
+            act, slope = gelu_parts(mm(R.DR[s].reshape(256, WIDE), up))
             act = act.astype(BF)
             gb = (mm(R.GC[rows], down) * slope).astype(BF)
-            R.ACT[rows] = act
-            R.GB[rows] = gb
-            EO[rows] += mm(act, down, 1, 1)
-            GM[rows] += mm(gb, up, 1, 1)
-
-        blocks(ROWS, 256, tokens_block)
-        R.UE[:, :, :, cols] = mm(DR[...], R.GB[...], 0, 0).astype(BF).reshape(4, 4, 48, 512)
-        R.DE[:, :, :, cols] = mm(R.GC[...], R.ACT[...], 0, 0).astype(BF).reshape(4, 4, 48, 512)
-
-    blocks(HID, 512, hidden_units)
-
-    def partials(e, carry):
-        R.CS[e] = R.GM[e, o].astype(BF)
-        R.ES[e] = R.EO[e, o].astype(BF)
+            R.ACT[rows, cols] = act
+            R.GB[rows, cols] = gb
+            R.EOB[...] += mm(act, down, 1, 1).reshape(2, 128, WIDE)
+            R.GMB[...] += mm(gb, up, 1, 1).reshape(2, 128, WIDE)
+
+        blocks(HID, 512, hidden_units)
+        R.PG[s] = R.GMB[o].astype(BF)
+        R.PE[s] = R.EOB[o].astype(BF)
+        for m in pair_sums(k):
+            m.start()
+        R.GMO[s] = R.GMB[t]
+        R.EOO[s] = R.EOB[t]
         return carry
 
-    lax.fori_loop(0, 4, partials, 0)
-    xg = w.go(i_xg, R.CS, R.XG, pc.PAIR)
-    xe = w.go(i_xe, R.ES, R.XE, pc.PAIR)
+    lax.fori_loop(0, 4, source, 0)
+    finish(2)
+    home(2).start()
+    R.RG[z, t] = R.XG[z]
+    R.RE[z, t] = R.XE[z]
+    R.RGR[...] = jnp.where(iota((16, WIDE), 0) == 2 + z, R.RGR[0:1], 0.0)
     sums = ExpertSums(R, pc, w)
-    sums.one(0)
-    sums.one(1)
-    xg.wait()
-    xe.wait()
-    w.open = [m for m in w.open if m is not xg and m is not xe]
-    row = jnp.sum(
-        jnp.where(iota((16, WIDE), 0) == 2 + z, R.VEC[...], 0.0), axis=0, keepdims=True
-    )
-    R.RGR[...] = jnp.zeros((16, WIDE), F32)
-
-    def finish(e, carry):
-        eo = R.EO[e, t] + R.XE[e].astype(F32)
-        gate = R.GATE.reshape(4, 2, 128, 1)[e, t]
-        gate_grad = jnp.sum(R.CR[e, t].astype(F32) * eo, axis=1, keepdims=True)
-        gs = gate_grad * gate * (1.0 - gate)
-        R.RGR[0:1] += jnp.sum(gs * R.DR[e, t].astype(F32), axis=0, keepdims=True)
-        R.CS[e] = (R.GM[e, t] + R.XG[e].astype(F32) + gs * row).astype(BF)
-        R.ES[e] = eo.astype(BF)
+    DR = R.DR.reshape(ROWS, WIDE)
+
+    def weight_grads(i, carry):
+        cols = pl.ds(pl.multiple_of(i * 384, 128), 384)
+        R.UE[:, :, :, cols] = mm(DR[...], R.GB[:, cols], 0, 0).astype(BF).reshape(4, 4, 48, 384)
+        R.DE[:, :, :, cols] = mm(R.GC[...], R.ACT[:, cols], 0, 0).astype(BF).reshape(4, 4, 48, 384)
+
+        @pl.when(lax.rem(i, 2) == 1)
+        def _():
+            for m in sums.step_one(lax.div(i, 2)):
+                m.start()
+
         return carry
 
-    lax.fori_loop(0, 4, finish, 0)
-    R.RGR[...] = jnp.where(iota((16, WIDE), 0) == 2 + z, R.RGR[0:1], 0.0)
-    rg = [w.go(i_rg + k, R.CS.at[pc.zto(k)], R.RG.at[z, t], pc.Z(k)) for k in (1, 2, 3)]
-    R.RG[z, t] = R.CS[z]
-    R.RE[z, t] = R.ES[z]
-    for m in rg:
-        m.wait_recv()
+    lax.fori_loop(0, 4, weight_grads, 0)
+    for k in (1, 3, 2):
+        home(k).wait()
     back = w.go(i_rgp, R.RG.at[:, t], R.RG.at[:, t], pc.PAIR)
-    re = [w.go(i_re + k, R.ES.at[pc.zto(k)], R.RE.at[z, t], pc.Z(k)) for k in (1, 2, 3)]
+    for k in (1, 3, 2):
+        home_out(k).start()
     back.wait_recv()
     sums.two(0)
-    return sums, re, i_rep
+    return sums, home_out, i_rep
 
 
 def combine(key, rows, got):
@@ -641,14 +700,13 @@
     return mm(pick, got)
 
 
-def phase_c(R, pc, w, sums, re, i_rep):
+def phase_c(R, pc, w, sums, home_out, i_rep):
     f, t, z, c, o = pc.f, pc.t, pc.z, pc.c, pc.o
     att = AttentionSums(R, pc, w)
     i_n = w.ids(1)
     i_sp, i_sc, i_sz = w.ids(1), w.ids(4), w.ids(4)
     own = pl.ds(pl.multiple_of(t * 512, 512), 512)
-    other = pl.ds(pl.multiple_of(o * 512, 512), 512)
-    GH, GN = R.GM.reshape(ROWS, WIDE), R.EO.reshape(ROWS, WIDE)
+    GH, GN = R.GH, R.EOO.reshape(512, WIDE)
     RG, RE = R.RG.reshape(ROWS, WIDE), R.RE.reshape(ROWS, WIDE)
     GBR = R.GC
     share = R.SHARE[0:1]
@@ -667,8 +725,8 @@
         aux = aux[:, 0:16]
         gm = gm + mm(aux.astype(BF), vec.astype(BF))
         mine = jnp.where(lax.div(i, 2) == t, 1.0, 0.0)
-        R.SB[...] += mine * mm(aux.astype(BF), R.MOE[rows], 0, 0)
-        h, f2 = R.HIDN[rows], R.F2[rows]
+        R.SB[...] += mine * mm(aux.astype(BF), (R.HIDN[rows] * R.STAT[rows, 1:2] * vec[1:2]).astype(BF), 0, 0)
+        h, f2 = R.HIDN[rows], R.STAT[rows, 1:2]
         g = gm * vec[1:2]
         inner = jnp.mean(g * h, axis=1, keepdims=True)
         gh = R.CT[rows].astype(F32) + f2 * (g - h * (f2 * f2 * inner))
@@ -678,8 +736,8 @@
         GBR[rows] = low
         ga = mm(low, R.WA[:, :, 3].reshape(WIDE, HALF)).astype(BF)
         for p in range(3):
-            R.GAP[p, rows] = ga[:, 128 * p : 128 * p + 128]
-        prod = ga.astype(F32) * R.ATO[rows].astype(F32)
+            R.ATX[p, rows] = ga[:, 128 * p : 128 * p + 128]
+        prod = ga.astype(F32) * joined(R.ATO, rows).astype(F32)
         top = prod.astype(BF)
         rest = (prod - top.astype(F32)).astype(BF)
         dd = mm(pick_head, top, 1, 1) + mm(pick_head, rest, 1, 1)
@@ -703,7 +761,7 @@
             block = grad[:, 128 * j : 128 * j + 128].astype(BF).reshape(4, 4, 48, 128)
             R.AG[n, :, :, pl.ds(48 * j, 48)] = block
 
-    place(0, mm(GBR[...], R.ATO[...], 0, 0))
+    place(0, mm(GBR[...], joined(R.ATO, pl.ds(0, ROWS)), 0, 0))
     sums.two(1)
     att.one(0)
     prefix = R.pre[0]
@@ -719,7 +777,7 @@
             for i in range(2):
                 side = even if i == 0 else ~even
                 q = jnp.where(side, R.QS[p, cols].astype(F32), 0.0).astype(BF)
-                do = jnp.where(side, R.GAP[p, cols].astype(F32), 0.0).astype(BF)
+                do = jnp.where(side, R.ATX[p, cols].astype(F32), 0.0).astype(BF)
                 lt, dd = R.LT[p, i : i + 1, cols], R.DD[p, i : i + 1, cols]
                 dq = jnp.zeros((128, 256), F32)
                 for kb in range(max(2, qb + 1)):
@@ -739,8 +797,8 @@
             R.QS[p, cols] = (both * 0.125).T.astype(BF)
         R.KS[p] = R.DK[...].astype(BF)
         R.VS[p] = R.DV[...].astype(BF)
-        joined = jnp.concatenate([R.QS[p], R.KS[p], R.VS[p]], axis=1)
-        place(p + 1, mm(R.NM[...], joined, 0, 0))
+        three = jnp.concatenate([R.QS[p], R.KS[p], R.VS[p]], axis=1)
+        place(p + 1, mm(R.NM[...], three, 0, 0))
         att.one(p + 1)
 
         @pl.when(p == 0)
@@ -762,19 +820,24 @@
     lax.fori_loop(0, 3, pair_of_heads, 0)
     GP = (R.QS, R.KS, R.VS)
 
-    def grads(ref, rows):
-        return jnp.concatenate([ref[p, rows] for p in range(3)], axis=1)
-
-    def normed_grad(rows):
-        acc = jnp.zeros((256, WIDE), F32)
-        for s in range(3):
-            acc = acc + mm(grads(GP[s], rows), R.WA[:, :, s].reshape(WIDE, HALF), 1, 1)
-        GN[rows] = acc
-
-    blocks(ROWS, 256, normed_grad)
+    XS, XN, BO = (r.reshape(512, WIDE) for r in (R.CS, R.XG, R.PE))
+
+    def normed_grad(i, carry):
+        mine = pl.ds(pl.multiple_of(i * 256, 256), 256)
+
+        def half(start):
+            rows = pl.ds(pl.multiple_of(start * 512 + i * 256, 256), 256)
+            acc = jnp.zeros((256, WIDE), F32)
+            for s in range(3):
+                acc = acc + mm(joined(GP[s], rows), R.WA[:, :, s].reshape(WIDE, HALF), 1, 1)
+            return acc
+
+        XS[mine] = half(o).astype(BF)
+        GN[mine] = half(t)
+        return carry
+
     w.flush()
-    XS, XN, BO = (r.reshape(512, WIDE) for r in (R.CS, R.XG, R.ES))
-    XS[...] = GN[other].astype(BF)
+    lax.fori_loop(0, 2, normed_grad, 0)
     xn = w.go(i_n, XS, XN, pc.PAIR)
     att.two(2)
     att.three(1)
@@ -784,8 +847,8 @@
     def input_grad(i, carry):
         rows = pl.ds(pl.multiple_of(i * 128, 128), 128)
         full = pl.ds(pl.multiple_of(t * 512 + i * 128, 128), 128)
-        gn = GN[full] + XN[rows].astype(F32)
-        x, f1 = R.TK[full].astype(F32), R.F1[full]
+        gn = GN[rows] + XN[rows].astype(F32)
+        x, f1 = R.TK[full].astype(F32), R.STAT[full, 0:1]
         g = gn * R.VEC[0:1]
         inner = jnp.mean(g * x, axis=1, keepdims=True)
         GH[full] = GH[full] + f1 * (g - x * (f1 * f1 * inner))
@@ -807,26 +870,28 @@
         w.go(i_sc + 1, R.SC.at[c], R.SC.at[c], pc.Y),
         w.go(i_sc + 2, R.SC.at[c], R.SC.at[c], pc.DIAG),
     ]
-    for m in re:
-        m.wait_recv()
+    for k in (1, 2, 3):
+        home_out(k).wait()
     w.go(i_rep, R.RE.at[:, t], R.RE.at[:, t], pc.PAIR).wait_recv()
 
     def block_rows(i, carry):
         rows = pl.ds(pl.multiple_of(i * 256, 256), 256)
         full = pl.ds(pl.multiple_of(t * 512 + i * 256, 256), 256)
         eo = combine(R.KC[full], full, RE[...])
-        BO[rows] = (R.HIDN[full] + R.GV[full] * eo).astype(BF)
+        BO[rows] = (R.HIDN[full] + R.STAT[full, 2:3] * eo).astype(BF)
         return carry
 
     lax.fori_loop(0, 2, block_rows, 0)
     out_b = pltpu.make_async_copy(BO, R.block_out, R.ls.at[1])
     out_b.start()
     att.three(3)
+    out_t.wait()
+    out_b.wait()
     for m in sc:
         m.wait_recv()
     R.SZ[z] = R.SC[0] + R.SC[1] + R.SC[2] + R.SC[3]
     sz = [w.go(i_sz + k, R.SZ.at[z], R.SZ.at[z], pc.Z(k)) for k in (1, 2, 3)]
-    sums.last()
+    written = sums.last()
     for n in range(3):
         att.last(n)
     for m in sz:
@@ -843,8 +908,8 @@
     R.gains_grad[...] = mine[0:2, 0:48]
     R.router_grad[...] = mine[2:6, 0:48]
     att.last(3)
-    out_t.wait()
-    out_b.wait()
+    for m in written:
+        m.wait()
     w.flush()
 
 
@@ -860,6 +925,18 @@
     "balance": ((1, 1), F32),
 }
 SCRATCH = {
+    "STAT": ((ROWS, 128), F32),
+    "ATO": ((3, ROWS, 128), BF),
+    "ATX": ((3, ROWS, 128), BF),
+    "PG": ((4, 128, WIDE), BF),
+    "PE": ((4, 128, WIDE), BF),
+    "EOB": ((2, 128, WIDE), F32),
+    "GMB": ((2, 128, WIDE), F32),
+    "EOO": ((4, 128, WIDE), F32),
+    "GMO": ((4, 128, WIDE), F32),
+    "GH": ((ROWS, WIDE), F32),
+    "ACT": ((ROWS, HID), BF),
+    "GB": ((ROWS, HID), BF),
     "TK": ((ROWS, WIDE), BF),
     "CT": ((ROWS, WIDE), BF),
     "WA": ((4, 4, 4, 48, HALF), BF),
@@ -869,8 +946,6 @@
     "KC": ((ROWS, 128), F32),
     "CR": ((4, 2, 128, WIDE), BF),
     "DR": ((4, 2, 128, WIDE), BF),
-    "F1": ((ROWS, 1), F32),
-    "F2": ((ROWS, 1), F32),
     "VEC": ((16, WIDE), F32),
     "RW": ((WIDE, 128), BF),
     "SHARE": ((8, 128), F32),
@@ -879,23 +954,13 @@
     "KS": ((3, ROWS, 128), BF),
     "VS": ((3, ROWS, 128), BF),
     "LT": ((3, 8, ROWS), F32),
-    "ATO": ((ROWS, HALF), BF),
-    "ATX": ((ROWS, HALF), BF),
     "HIDN": ((ROWS, WIDE), F32),
-    "MOE": ((ROWS, WIDE), BF),
-    "GV": ((ROWS, 1), F32),
     "PR": ((ROWS, 128), F32),
     "PS": ((8, 128), F32),
     "SM": ((16, 16, 128), BF),
     "DM": ((512, ROWS), BF),
     "CS": ((4, 128, WIDE), BF),
-    "ES": ((4, 128, WIDE), BF),
-    "GATE": ((ROWS, 1), F32),
     "GC": ((ROWS, WIDE), BF),
-    "EO": ((4, 2, 128, WIDE), F32),
-    "GM": ((4, 2, 128, WIDE), F32),
-    "ACT": ((ROWS, 512), BF),
-    "GB": ((ROWS, 512), BF),
     "XE": ((4, 128, WIDE), BF),
     "XG": ((4, 128, WIDE), BF),
     "RG": ((4, 2, 128, WIDE), BF),
@@ -907,7 +972,6 @@
     "RD2": ((4, 48, HID), BF),
     "ZU": ((4, 48, HID), BF),
     "ZD": ((4, 48, HID), BF),
-    "GAP": ((3, ROWS, 128), BF),
     "DD": ((3, 8, ROWS), F32),
     "DK": ((ROWS, 128), F32),
     "DV": ((ROWS, 128), F32),
@@ -925,8 +989,8 @@
 }
 INS = ("tok", "cot", "pre", "idr", "gains", "qkv", "out", "router", "up", "down")
 IN_HBM = ("tok", "cot", "up", "down")
-OUT_HBM = ("block_out", "tokens_grad")
-SEMAPHORES = 192
+OUT_HBM = ("block_out", "tokens_grad", "up_grad", "down_grad")
+SEMAPHORES = 208
 
 
 def fused(args):
@@ -936,9 +1000,7 @@
         R = types.SimpleNamespace(**dict(zip(names, refs)))
         pc = Place()
         w = Wire(R.ss, R.rs)
-        phase_a(R, pc, w)
-        sums, re, i_rep = phase_b(R, pc, w)
-        phase_c(R, pc, w, sums, re, i_rep)
+        phase_c(R, pc, w, *phase_b(R, pc, w, *phase_a(R, pc, w)))
 
     vm = pl.BlockSpec(memory_space=pltpu.VMEM)
     hbm = pl.BlockSpec(memory_space=pl.ANY)

time: 211 us -> 197 us (0.934)
  Pallas kernels: 199 us -> 185 us
    pallas_call x1, Pallas kernels: 199 us -> 185 us  [fused(): pl.pallas_call(body, out_shape=[jax.ShapeDtypeStruct(s, d) for s, d in OU...]
where the time goes in v4:
time: 197 us
  Pallas kernels  185 us (94%)
  local copies, waits for them, and re-layouts  8.52 us (4%)
  between operations  3.1 us (2%)
    pallas_call x1, Pallas kernels, fused(): pl.pallas_call(body, out_shape=[jax.ShapeDtypeStruct(s, d) for s, d in OU...  185 us
    unnamed x22, local copies, waits for them, and re-layouts  8.52 us

profile of v4, /device:TPU:0, one launch (start us, length us, event | category | flops | bytes accessed | tf_op | source)
XLA Modules:
  0.0 196.8 jit_solution(5439150441781048823)
XLA Ops:
  1.3 185.2 %block.1 = (bf16[512,768]{1,0:T(8,128)(2,1)}, f32[512,768]{1,0:T(8,128)}, f32[2,48]{1,0:T(2,128)}, f32[3,48,384]{2,1,0:T(8,128)}, f32[48,384]{1,0:T(8,128)}, /*i...) custom-call(bf16[512,768]{1,0:T(8,128)(2,1)} %refs_0_.1, ...), custom_call_target="tpu_custom_call" | custom-call | tf_op jit(solution)/shard_map/block/pallas_call | solution.py:1009
  186.5 0.0 copy-start
  186.5 2.2 %copy.29 = bf16[512,768]{1,0:T(8,128)(2,1)} copy(bf16[512,768]{1,0:T(8,128)(2,1)} %get-tuple-element.36) | data formatting | bytes 1572864
  188.7 0.0 copy-done
  188.7 0.0 copy-start.6
  188.7 0.0 copy-start.3
  188.7 0.0 copy-start.4
  188.7 0.0 copy-start.5
  188.7 0.0 copy-start.2
  188.7 1.1 copy.30
  189.9 0.0 copy-done.6
  189.9 0.6 copy.31
  190.4 0.0 copy-done.3
  190.4 0.7 copy.32
  191.1 0.0 copy-done.4
  191.1 0.6 copy.33
  191.7 0.0 copy-done.5
  191.7 0.6 copy.34
  192.3 0.0 copy-done.2
  192.3 0.0 copy-start.1
  192.3 1.0 copy.35
  193.3 0.7 copy-done.1
  194.0 1.0 copy.36
Async XLA Ops:
  186.5 2.2 %copy-start = (f32[512,768]{1,0:T(8,128)S(1)}, f32[512,768]{1,0:T(8,128)}, u32[]{:S(2)}) copy-start(f32[512,768]{1,0:T(8,128)} %get-tuple-element.37) | copy-start | bytes 4718596
  188.7 1.2 copy-start.6
  188.7 1.7 copy-start.3
  188.7 2.4 %copy-start.4 = (f32[48,384]{1,0:T(8,128)S(1)}, f32[48,384]{1,0:T(8,128)}, u32[]{:S(2)}) copy-start(f32[48,384]{1,0:T(8,128)} %get-tuple-element.40) | copy-start | bytes 221188
  188.7 3.1 %copy-start.5 = (f32[4,48]{1,0:T(4,128)S(1)}, f32[4,48]{1,0:T(4,128)}, u32[]{:S(2)}) copy-start(f32[4,48]{1,0:T(4,128)} %get-tuple-element.41) | copy-start | bytes 2308
  188.7 3.6 %copy-start.2 = (f32[4,48,1536]{2,1,0:T(8,128)S(1)}, f32[4,48,1536]{2,1,0:T(8,128)}, u32[]{:S(2)}) copy-start(f32[4,48,1536]{2,1,0:T(8,128)} %get-tuple-element.42) | copy-start | bytes 3538948
  192.3 1.7 copy-start.1

commit v5 on v4

--- a/solution.py
+++ b/solution.py
@@ -123,6 +123,20 @@
 )
 
 
+def hook(table, p, qb):
+    for (pp, qq), step in table.items():
+        if qq == qb:
+            pl.when(p == pp)(step)
+
+
+def both(*steps):
+    def run():
+        for step in steps:
+            step()
+
+    return run
+
+
 def phase_a(R, pc, w):
     f, t, z, c = pc.f, pc.t, pc.z, pc.c
     idr = R.idr[...]
@@ -146,9 +160,9 @@
     i_tok, i_cot, i_wo, i_att = w.ids(1), w.ids(1), w.ids(1), w.ids(3)
     i_z, i_sz = w.ids(4), w.ids(4)
     i_x, i_y, i_fx, i_fy, i_sx, i_sy, i_sf = (w.ids(4) for _ in range(7))
-    i_mu, i_md = w.ids(4), w.ids(4)
-    i_m = [w.ids(4) for _ in range(6)]
-    i_cz, i_dz, i_cp, i_dp = w.ids(4), w.ids(4), w.ids(1), w.ids(4)
+    i_mz = w.ids(24)
+    i_m = [w.ids(3) for _ in range(6)]
+    i_cz, i_dz, i_cp, i_dp = w.ids(4), w.ids(4), w.ids(4), w.ids(4)
 
     zs = [w.go(i_sz + k, R.SM.at[f], R.SM.at[f], pc.Z(k)) for k in (1, 2, 3)]
     za = [w.go(i_z + k, R.WA.at[z, c], R.WA.at[z, c], pc.Z(k)) for k in (1, 2, 3)]
@@ -204,31 +218,91 @@
     R.PR[...] = jnp.broadcast_to(idr.astype(F32), (128, ROWS)).T
     r = iota((512, ROWS), 0)
     want = lax.div(r, 128) * 256 + lax.rem(r, 128) + 128 * t
-    R.DM[...] = (key.astype(jnp.int32) == want).astype(F32).astype(BF)
+    R.ACT[0:512, 0:ROWS] = (key.astype(jnp.int32) == want).astype(F32).astype(BF)
 
     za[0].wait_recv()
     zs[0].wait_recv()
     got[1] = spread(1)
+    ends = [forward(0, got[0])]
     for m in local:
         m.wait()
     cot_x.wait_recv()
 
     def cot_rows(e, carry):
-        R.PG[e] = mm(R.DM[pl.ds(pl.multiple_of(e * 128, 128), 128)], R.CT[...]).astype(BF)
+        R.CQ[e] = mm(R.ACT[pl.ds(pl.multiple_of(e * 128, 128), 128), pl.ds(0, ROWS)], R.CT[...]).astype(BF)
         return carry
 
     lax.fori_loop(0, 4, cot_rows, 0)
-    R.CR[z, t] = R.PG[z]
+    R.CR[z, t] = R.CQ[z]
+    w.copy(i_cp, R.CR.at[z, t], R.CR.at[z, t], pc.PAIR).start()
     za[1].wait_recv()
     zs[1].wait_recv()
     got[2] = spread(2)
+
+    def chunk(j):
+        return pl.ds(pl.multiple_of(j * 512, 128), 512)
+
+    def from_plane(j):
+        out = []
+        for k in (1, 3, 2):
+            to, cols, i = pc.zto(k), chunk(j), i_mz + 8 * j + k
+            out.append(w.copy(i, R.up.at[to, :, cols], R.UE.at[z, c, :, cols], pc.Z(k)))
+            out.append(w.copy(i + 4, R.down.at[to, :, cols], R.DE.at[z, c, :, cols], pc.Z(k)))
+        return out
+
+    def moe_spread(j):
+        u, d = R.UE.at[:, c, :, chunk(j)], R.DE.at[:, c, :, chunk(j)]
+        return [
+            w.copy(i_m[0] + j, u, u, pc.X),
+            w.copy(i_m[1] + j, d, d, pc.Y),
+            w.copy(i_m[2] + j, u, u, pc.Y),
+            w.copy(i_m[3] + j, d, d, pc.X),
+        ]
+
+    def moe_forward(j):
+        u, d = R.UE.at[:, pc.cx, :, chunk(j)], R.DE.at[:, pc.cy, :, chunk(j)]
+        return [w.copy(i_m[4] + j, u, u, pc.Y), w.copy(i_m[5] + j, d, d, pc.X)]
+
+    def start_spread(j):
+        for m in from_plane(j):
+            m.wait()
+        for m in moe_spread(j):
+            m.start()
+
+    def start_forward(j):
+        a = moe_spread(j)
+        a[0].wait()
+        a[1].wait()
+        for m in moe_forward(j):
+            m.start()
+
+    def weights_here(j):
+        for m in moe_spread(j)[2:] + moe_forward(j):
+            m.wait()
+
+    def start_plane(j):
+        for m in from_plane(j):
+            m.start()
+
+    def start_cot():
+        for m in cz:
+            m.start()
+
+    start_plane(0)
+    cz = [w.copy(i_cz + k, R.CQ.at[pc.zto(k)], R.CR.at[z, t], pc.Z(k)) for k in (1, 3, 2)]
+    ends.append(forward(1, got[1]))
     za[2].wait_recv()
     zs[2].wait_recv()
     got[3] = spread(3)
-    mu = [w.go(i_mu + k, R.up.at[pc.zto(k)], R.UE.at[z, c], pc.Z(k)) for k in (1, 2, 3)]
-    md = [w.go(i_md + k, R.down.at[pc.zto(k)], R.DE.at[z, c], pc.Z(k)) for k in (1, 2, 3)]
-    cz = [w.go(i_cz + k, R.PG.at[pc.zto(k)], R.CR.at[z, t], pc.Z(k)) for k in (1, 2, 3)]
-    ends = [forward(k, got[k]) for k in range(4)]
+    ends.append(forward(2, got[2]))
+    ends.append(forward(3, got[3]))
+    start_plane(1)
+    agenda = {
+        (0, 3): lambda: start_spread(1),
+        (1, 1): lambda: start_forward(0),
+        (2, 1): both(lambda: start_spread(2), start_cot),
+        (2, 3): lambda: start_forward(1),
+    }
 
     tok_x.wait_recv()
 
@@ -266,26 +340,8 @@
         y.wait_recv()
     wo = w.go(i_wo, R.WA.at[:, :, 3], R.WO, pc.PAIR)
 
-    def moe_spread(k):
-        zz = pc.zfrom(k)
-        u, d = R.UE.at[zz, c], R.DE.at[zz, c]
-        return [
-            w.copy(i_m[0] + k, u, u, pc.X),
-            w.copy(i_m[1] + k, d, d, pc.Y),
-            w.copy(i_m[2] + k, u, u, pc.Y),
-            w.copy(i_m[3] + k, d, d, pc.X),
-        ]
-
-    def moe_forward(k):
-        zz = pc.zfrom(k)
-        u, d = R.UE.at[zz, pc.cx], R.DE.at[zz, pc.cy]
-        return [
-            w.copy(i_m[4] + k, u, u, pc.Y),
-            w.copy(i_m[5] + k, d, d, pc.X),
-        ]
-
-    for m in moe_spread(0):
-        m.start()
+    start_spread(0)
+    start_plane(2)
 
     def project(rows):
         x = R.NM[rows]
@@ -325,23 +381,11 @@
                     out = out + mm(value_t[:, k0 : k0 + kn], e.astype(BF))
                 R.LT[p, i : i + 1, cols] = top + jnp.log(total_e)
                 outs.append(out / total_e)
-            both = jnp.where(iota((128, 256), 0) < 64, outs[0], outs[1])
-            R.ATO[p, cols] = both.T.astype(BF)
-        w.copy(i_att + p, R.ATO.at[p], R.ATX.at[p], pc.PAIR).start()
-
-        @pl.when(p < 3)
-        def _():
-            k = p + 1
-            for ref, i0 in ((R.UE, i_mu), (R.DE, i_md)):
-                w.copy(i0 + k, ref.at[z, c], ref.at[z, c], pc.Z(k)).wait_recv()
-            for m in moe_spread(k):
-                m.start()
-
-        a = moe_spread(p)
-        a[0].wait_recv()
-        a[1].wait_recv()
-        for m in moe_forward(p):
-            m.start()
+            merged = jnp.where(iota((128, 256), 0) < 64, outs[0], outs[1])
+            R.ATO[p, cols] = merged.T.astype(BF)
+            if qb == 3:
+                w.copy(i_att + p, R.ATO.at[p], R.ATX.at[p], pc.PAIR).start()
+            hook(agenda, p, qb)
         return carry
 
     lax.fori_loop(0, 3, pair_of_heads, 0)
@@ -377,7 +421,7 @@
     def moe_rows(i, carry):
         k = order(lax.rem(i + 1, 4))
         e = pc.zto(k)
-        R.CS[e] = mm(R.DM[pl.ds(pl.multiple_of(e * 128, 128), 128)], R.GC[...]).astype(BF)
+        R.CS[e] = mm(R.ACT[pl.ds(pl.multiple_of(e * 128, 128), 128), pl.ds(0, ROWS)], R.GC[...]).astype(BF)
 
         @pl.when(i < 3)
         def _():
@@ -388,26 +432,9 @@
     lax.fori_loop(0, 4, moe_rows, 0)
     R.DR[z, t] = R.CS[z]
     w.copy(i_dp, R.DR.at[z, t], R.DR.at[z, t], pc.PAIR).start()
-    a = moe_spread(3)
-    a[0].wait_recv()
-    a[1].wait_recv()
-    for m in moe_forward(3):
-        m.start()
-    for m in cz:
-        m.wait_recv()
-    cp = w.go(i_cp, R.CR.at[:, t], R.CR.at[:, t], pc.PAIR)
-    for k in range(4):
-        a = moe_spread(k)
-        b = moe_forward(k)
-        a[2].wait_recv()
-        a[3].wait_recv()
-        b[0].wait_recv()
-        b[1].wait_recv()
-        for m in a + b:
-            m.wait_send()
-    cp.wait_recv()
+    start_forward(2)
     w.flush()
-    return i_dz, i_dp
+    return i_dz, i_dp, i_cz, i_cp, weights_here
 
 
 def gelu_parts(v):
@@ -419,11 +446,14 @@
 class ExpertSums:
     def __init__(self, R, pc, w):
         self.R, self.pc, self.w = R, pc, w
-        self.i1, self.i2, self.i3 = w.ids(8), w.ids(4), w.ids(16)
+        self.i1, self.i2, self.i3 = w.ids(16), w.ids(8), w.ids(32)
+
+    def cols(self, g):
+        return pl.ds(pl.multiple_of(384 * g, 128), 384)
 
     def step_one(self, g):
         R, pc, w = self.R, self.pc, self.w
-        cols, i = pl.ds(pl.multiple_of(768 * g, 128), 768), self.i1 + 4 * g
+        cols, i = self.cols(g), self.i1 + 4 * g
         return [
             w.copy(i, R.UE.at[:, pc.cx, :, cols], R.RU.at[0, :, :, cols], pc.X),
             w.copy(i + 1, R.UE.at[:, pc.cd, :, cols], R.RU.at[1, :, :, cols], pc.X),
@@ -433,7 +463,7 @@
 
     def step_two(self, g):
         R, pc, w = self.R, self.pc, self.w
-        cols, i = pl.ds(768 * g, 768), self.i2 + 2 * g
+        cols, i = self.cols(g), self.i2 + 2 * g
         return [
             w.copy(i, R.UE.at[:, pc.cy, :, cols], R.RU2.at[:, :, cols], pc.Y),
             w.copy(i + 1, R.DE.at[:, pc.cx, :, cols], R.RD2.at[:, :, cols], pc.X),
@@ -441,15 +471,19 @@
 
     def step_three(self, g):
         R, pc, w = self.R, self.pc, self.w
-        cols, i, out = pl.ds(768 * g, 768), self.i3 + 8 * g, []
+        cols, i, out = self.cols(g), self.i3 + 8 * g, []
         for k in (1, 2, 3):
             to, z = pc.zto(k), pc.z
             out.append(w.copy(i + k, R.UE.at[to, pc.c, :, cols], R.ZU.at[z, :, cols], pc.Z(k)))
             out.append(w.copy(i + 4 + k, R.DE.at[to, pc.c, :, cols], R.ZD.at[z, :, cols], pc.Z(k)))
         return out
 
+    def one(self, g):
+        for m in self.step_one(g):
+            m.start()
+
     def two(self, g):
-        R, pc, cols = self.R, self.pc, pl.ds(768 * g, 768)
+        R, pc, cols = self.R, self.pc, self.cols(g)
         for m in self.step_one(g):
             m.wait()
 
@@ -465,7 +499,7 @@
             m.start()
 
     def three(self, g):
-        R, pc, cols = self.R, self.pc, pl.ds(768 * g, 768)
+        R, pc, cols = self.R, self.pc, self.cols(g)
         for m in self.step_two(g):
             m.wait()
 
@@ -483,9 +517,10 @@
         R.ZU[pc.z] = R.UE[pc.z, pc.c]
         R.ZD[pc.z] = R.DE[pc.z, pc.c]
         out = []
-        for g in (0, 1):
+        for g in range(4):
             for m in self.step_three(g):
                 m.wait()
+        for g in (0, 1):
             cols = pl.ds(768 * g, 768)
             for j, (got, to) in enumerate(((R.ZU, R.up_grad), (R.ZD, R.down_grad))):
                 held = R.HIDN.at[pl.ds(192 * (2 * g + j), 192)].reshape(4, 48, 768)
@@ -567,7 +602,7 @@
                 R.qkv_grad[j, :, 128 * (n - 1) : 128 * n] = block
 
 
-def phase_b(R, pc, w, i_dz, i_dp):
+def phase_b(R, pc, w, i_dz, i_dp, i_cz, i_cp, weights_here):
     f, t, z, c, o = pc.f, pc.t, pc.z, pc.c, pc.o
     i_xe, i_xg = w.ids(4), w.ids(4)
     i_rg, i_re, i_rgp, i_rep = w.ids(4), w.ids(4), w.ids(1), w.ids(1)
@@ -583,9 +618,15 @@
     def rows_in(k):
         return w.copy(i_dz + k, R.CS.at[pc.zto(k)], R.DR.at[z, t], pc.Z(k))
 
+    def cot_in(k):
+        return w.copy(i_cz + k, R.CQ.at[pc.zto(k)], R.CR.at[z, t], pc.Z(k))
+
     def rows_pair(k):
         s = pc.zfrom(k)
-        return w.copy(i_dp + k, R.DR.at[s, t], R.DR.at[s, t], pc.PAIR)
+        return (
+            w.copy(i_dp + k, R.DR.at[s, t], R.DR.at[s, t], pc.PAIR),
+            w.copy(i_cp + k, R.CR.at[s, t], R.CR.at[s, t], pc.PAIR),
+        )
 
     def pair_sums(k):
         s = pc.zfrom(k)
@@ -619,18 +660,8 @@
         s = pc.zfrom(k)
         rows = pl.ds(pl.multiple_of(s * 256, 256), 256)
 
-        @pl.when(i > 0)
-        def _():
-            rows_in(k).wait()
-            rows_pair(k).start()
-            last = order(i - 1)
-            finish(last)
-
-            @pl.when(i > 1)
-            def _():
-                home(last).start()
-
-        rows_pair(k).wait()
+        for m in rows_pair(k):
+            m.wait()
         x = R.DR[s].reshape(256, WIDE)
         logits = mm(x, R.RW[...])
         gate = jax.nn.sigmoid(
@@ -638,10 +669,13 @@
         )
         R.STAT[rows, 3:4] = gate
         R.GC[rows] = (gate * R.CR[s].reshape(256, WIDE).astype(F32)).astype(BF)
-        R.EOB[...] = jnp.zeros((2, 128, WIDE), F32)
-        R.GMB[...] = jnp.zeros((2, 128, WIDE), F32)
-
-        def hidden_units(cols):
+
+        def hidden_units(j, carry):
+            @pl.when(i == 0)
+            def _():
+                weights_here(j)
+
+            cols = pl.ds(pl.multiple_of(j * 512, 128), 512)
             up = R.UE[:, :, :, cols].reshape(WIDE, 512)
             down = R.DE[:, :, :, cols].reshape(WIDE, 512)
             act, slope = gelu_parts(mm(R.DR[s].reshape(256, WIDE), up))
@@ -649,16 +683,36 @@
             gb = (mm(R.GC[rows], down) * slope).astype(BF)
             R.ACT[rows, cols] = act
             R.GB[rows, cols] = gb
-            R.EOB[...] += mm(act, down, 1, 1).reshape(2, 128, WIDE)
-            R.GMB[...] += mm(gb, up, 1, 1).reshape(2, 128, WIDE)
-
-        blocks(HID, 512, hidden_units)
+            return carry
+
+        lax.fori_loop(0, 3, hidden_units, 0)
+        @pl.when(i < 3)
+        def _():
+            after = order(i + 1)
+            cot_in(after).wait()
+            rows_pair(after)[1].start()
+            rows_in(after).wait()
+            rows_pair(after)[0].start()
+
+        up, down = R.UE[...].reshape(WIDE, HID), R.DE[...].reshape(WIDE, HID)
+        R.GMB[...] = mm(R.GB[rows], up, 1, 1).reshape(2, 128, WIDE)
         R.PG[s] = R.GMB[o].astype(BF)
-        R.PE[s] = R.EOB[o].astype(BF)
-        for m in pair_sums(k):
-            m.start()
+        pair_sums(k)[0].start()
         R.GMO[s] = R.GMB[t]
-        R.EOO[s] = R.EOB[t]
+        R.GMB[...] = mm(R.ACT[rows], down, 1, 1).reshape(2, 128, WIDE)
+        R.PE[s] = R.GMB[o].astype(BF)
+        pair_sums(k)[1].start()
+        R.EOO[s] = R.GMB[t]
+
+        @pl.when(i > 0)
+        def _():
+            last = order(i - 1)
+            finish(last)
+
+            @pl.when(i > 1)
+            def _():
+                home(last).start()
+
         return carry
 
     lax.fori_loop(0, 4, source, 0)
@@ -675,29 +729,46 @@
         R.UE[:, :, :, cols] = mm(DR[...], R.GB[:, cols], 0, 0).astype(BF).reshape(4, 4, 48, 384)
         R.DE[:, :, :, cols] = mm(R.GC[...], R.ACT[:, cols], 0, 0).astype(BF).reshape(4, 4, 48, 384)
 
-        @pl.when(lax.rem(i, 2) == 1)
+
+        @pl.when(i < 2)
         def _():
-            for m in sums.step_one(lax.div(i, 2)):
+            for m in sums.step_one(i):
                 m.start()
 
         return carry
 
     lax.fori_loop(0, 4, weight_grads, 0)
+    share, vec = R.SHARE[0:1], R.VEC[...]
+    R.SB[...] = jnp.zeros((16, WIDE), F32)
+
+    def prepared(i, carry):
+        rows = pl.ds(pl.multiple_of(i * 256, 256), 256)
+        R.ACT[rows, pl.ds(0, ROWS)] = pick_rows(R.KC[rows])
+        pr = R.PR[rows]
+        mixed = jnp.sum(pr * share, axis=1, keepdims=True)
+        aux = (balance_weight * 4.0 / (16 * ROWS)) * pr * (share - mixed)
+        aux = aux[:, 0:16].astype(BF)
+        R.GH[rows] = mm(aux, vec.astype(BF))
+        mine = jnp.where(lax.div(i, 2) == t, 1.0, 0.0)
+        moe = (R.HIDN[rows] * R.STAT[rows, 1:2] * vec[1:2]).astype(BF)
+        R.SB[...] += mine * mm(aux, moe, 0, 0)
+        return carry
+
+    lax.fori_loop(0, 4, prepared, 0)
+    sums.two(0)
+    sums.one(2)
     for k in (1, 3, 2):
         home(k).wait()
     back = w.go(i_rgp, R.RG.at[:, t], R.RG.at[:, t], pc.PAIR)
     for k in (1, 3, 2):
         home_out(k).start()
     back.wait_recv()
-    sums.two(0)
     return sums, home_out, i_rep
 
 
-def combine(key, rows, got):
-    n = key.shape[0]
+def pick_rows(key):
     keys = jnp.concatenate([key] * 8, axis=1)
-    pick = (keys == iota((n, ROWS), 1).astype(F32)).astype(F32).astype(BF)
-    return mm(pick, got)
+    return (keys == iota((key.shape[0], ROWS), 1).astype(F32)).astype(F32).astype(BF)
 
 
 def phase_c(R, pc, w, sums, home_out, i_rep):
@@ -714,18 +785,11 @@
     head = iota((24, HALF), 0)
     head = jnp.where(lax.rem(head, 8) < 2, 2 * lax.div(head, 8) + lax.rem(head, 8), -1)
     pick_head = (head == lax.div(iota((24, HALF), 1), 64)).astype(F32).astype(BF)
-    R.SB[...] = jnp.zeros((16, WIDE), F32)
 
     def residual(i, carry):
         rows = pl.ds(pl.multiple_of(i * 256, 256), 256)
-        gm = combine(R.KC[rows], rows, RG[...])
-        pr = R.PR[rows]
-        mixed = jnp.sum(pr * share, axis=1, keepdims=True)
-        aux = (balance_weight * 4.0 / (16 * ROWS)) * pr * (share - mixed)
-        aux = aux[:, 0:16]
-        gm = gm + mm(aux.astype(BF), vec.astype(BF))
+        gm = mm(R.ACT[rows, pl.ds(0, ROWS)], RG[...]) + R.GH[rows]
         mine = jnp.where(lax.div(i, 2) == t, 1.0, 0.0)
-        R.SB[...] += mine * mm(aux.astype(BF), (R.HIDN[rows] * R.STAT[rows, 1:2] * vec[1:2]).astype(BF), 0, 0)
         h, f2 = R.HIDN[rows], R.STAT[rows, 1:2]
         g = gm * vec[1:2]
         inner = jnp.mean(g * h, axis=1, keepdims=True)
@@ -743,6 +807,12 @@
         dd = mm(pick_head, top, 1, 1) + mm(pick_head, rest, 1, 1)
         for p in range(3):
             R.DD[p, :, rows] = dd[8 * p : 8 * p + 8]
+
+        @pl.when(i == 2)
+        def _():
+            sums.two(1)
+            sums.one(3)
+
         return carry
 
     R.G2[...] = jnp.zeros((8, WIDE), F32)
@@ -762,8 +832,26 @@
             R.AG[n, :, :, pl.ds(48 * j, 48)] = block
 
     place(0, mm(GBR[...], joined(R.ATO, pl.ds(0, ROWS)), 0, 0))
-    sums.two(1)
-    att.one(0)
+
+    def outputs_pair():
+        return w.copy(i_rep, R.RE.at[:, t], R.RE.at[:, t], pc.PAIR)
+
+    def outputs_home():
+        for k in (1, 2, 3):
+            home_out(k).wait()
+        outputs_pair().start()
+
+
+    agenda = {
+        (0, 1): both(lambda: sums.two(2), lambda: sums.three(0)),
+        (0, 3): lambda: sums.three(1),
+        (1, 2): lambda: sums.two(3),
+        (1, 3): lambda: att.one(0),
+        (2, 0): lambda: sums.three(2),
+        (2, 1): outputs_home,
+        (2, 2): lambda: sums.three(3),
+        (2, 3): lambda: att.two(0),
+    }
     prefix = R.pre[0]
 
     def pair_of_heads(p, carry):
@@ -793,27 +881,21 @@
                     R.DK[keys] += mm(ds, q)
                     dq = dq + mm(key_t[:, kb * 256 : kb * 256 + 256], ds)
                 outs.append(dq)
-            both = jnp.where(iota((128, 256), 0) < 64, outs[0], outs[1])
-            R.QS[p, cols] = (both * 0.125).T.astype(BF)
+            merged = jnp.where(iota((128, 256), 0) < 64, outs[0], outs[1])
+            R.QS[p, cols] = (merged * 0.125).T.astype(BF)
+            hook(agenda, p, qb)
         R.KS[p] = R.DK[...].astype(BF)
         R.VS[p] = R.DV[...].astype(BF)
         three = jnp.concatenate([R.QS[p], R.KS[p], R.VS[p]], axis=1)
         place(p + 1, mm(R.NM[...], three, 0, 0))
-        att.one(p + 1)
-
-        @pl.when(p == 0)
-        def _():
-            sums.three(0)
 
         @pl.when(p == 1)
         def _():
-            sums.three(1)
-            att.two(0)
-
-        @pl.when(p == 2)
+            att.one(1)
+
+        @pl.when(p > 0)
         def _():
-            att.three(0)
-            att.two(1)
+            att.one(p + 1)
 
         return carry
 
@@ -821,6 +903,8 @@
     GP = (R.QS, R.KS, R.VS)
 
     XS, XN, BO = (r.reshape(512, WIDE) for r in (R.CS, R.XG, R.PE))
+
+    R.G2[...] = jnp.zeros((8, WIDE), F32)
 
     def normed_grad(i, carry):
         mine = pl.ds(pl.multiple_of(i * 256, 256), 256)
@@ -830,6 +914,8 @@
             acc = jnp.zeros((256, WIDE), F32)
             for s in range(3):
                 acc = acc + mm(joined(GP[s], rows), R.WA[:, :, s].reshape(WIDE, HALF), 1, 1)
+            x = R.TK[rows].astype(F32) * R.STAT[rows, 0:1]
+            R.G2[0:1] += jnp.sum(acc * x, axis=0, keepdims=True)
             return acc
 
         XS[mine] = half(o).astype(BF)
@@ -839,10 +925,32 @@
     w.flush()
     lax.fori_loop(0, 2, normed_grad, 0)
     xn = w.go(i_n, XS, XN, pc.PAIR)
+    R.SB[0:1] = R.G2[0:1]
+    sp = w.go(i_sp, R.SB, R.SP, pc.PAIR)
+    att.two(1)
+    att.three(0)
+    outputs_pair().wait()
+
+    def block_rows(i, carry):
+        rows = pl.ds(pl.multiple_of(i * 256, 256), 256)
+        full = pl.ds(pl.multiple_of(t * 512 + i * 256, 256), 256)
+        eo = mm(R.ACT[full, pl.ds(0, ROWS)], RE[...])
+        BO[rows] = (R.HIDN[full] + R.STAT[full, 2:3] * eo).astype(BF)
+        return carry
+
+    lax.fori_loop(0, 2, block_rows, 0)
+    out_b = pltpu.make_async_copy(BO, R.block_out, R.ls.at[1])
+    out_b.start()
     att.two(2)
     att.three(1)
+    sp.wait_recv()
+    R.SC[c] = R.SB[...] + R.SP[...]
+    sc = [
+        w.go(i_sc, R.SC.at[c], R.SC.at[c], pc.X),
+        w.go(i_sc + 1, R.SC.at[c], R.SC.at[c], pc.Y),
+        w.go(i_sc + 2, R.SC.at[c], R.SC.at[c], pc.DIAG),
+    ]
     xn.wait_recv()
-    R.G2[...] = jnp.zeros((8, WIDE), F32)
 
     def input_grad(i, carry):
         rows = pl.ds(pl.multiple_of(i * 128, 128), 128)
@@ -852,45 +960,20 @@
         g = gn * R.VEC[0:1]
         inner = jnp.mean(g * x, axis=1, keepdims=True)
         GH[full] = GH[full] + f1 * (g - x * (f1 * f1 * inner))
-        R.G2[0:1] += jnp.sum(gn * x * f1, axis=0, keepdims=True)
         return carry
 
     lax.fori_loop(0, 4, input_grad, 0)
     out_t = pltpu.make_async_copy(GH.at[own], R.tokens_grad, R.ls.at[0])
     out_t.start()
-    R.SB[0:1] = R.G2[0:1]
-    sp = w.go(i_sp, R.SB, R.SP, pc.PAIR)
     att.two(3)
     att.three(2)
-    sp.wait_recv()
-    me = R.SB[...] + R.SP[...]
-    R.SC[c] = me
-    sc = [
-        w.go(i_sc, R.SC.at[c], R.SC.at[c], pc.X),
-        w.go(i_sc + 1, R.SC.at[c], R.SC.at[c], pc.Y),
-        w.go(i_sc + 2, R.SC.at[c], R.SC.at[c], pc.DIAG),
-    ]
-    for k in (1, 2, 3):
-        home_out(k).wait()
-    w.go(i_rep, R.RE.at[:, t], R.RE.at[:, t], pc.PAIR).wait_recv()
-
-    def block_rows(i, carry):
-        rows = pl.ds(pl.multiple_of(i * 256, 256), 256)
-        full = pl.ds(pl.multiple_of(t * 512 + i * 256, 256), 256)
-        eo = combine(R.KC[full], full, RE[...])
-        BO[rows] = (R.HIDN[full] + R.STAT[full, 2:3] * eo).astype(BF)
-        return carry
-
-    lax.fori_loop(0, 2, block_rows, 0)
-    out_b = pltpu.make_async_copy(BO, R.block_out, R.ls.at[1])
-    out_b.start()
-    att.three(3)
-    out_t.wait()
-    out_b.wait()
     for m in sc:
         m.wait_recv()
     R.SZ[z] = R.SC[0] + R.SC[1] + R.SC[2] + R.SC[3]
     sz = [w.go(i_sz + k, R.SZ.at[z], R.SZ.at[z], pc.Z(k)) for k in (1, 2, 3)]
+    att.three(3)
+    out_t.wait()
+    out_b.wait()
     written = sums.last()
     for n in range(3):
         att.last(n)
@@ -929,8 +1012,8 @@
     "ATO": ((3, ROWS, 128), BF),
     "ATX": ((3, ROWS, 128), BF),
     "PG": ((4, 128, WIDE), BF),
+    "CQ": ((4, 128, WIDE), BF),
     "PE": ((4, 128, WIDE), BF),
-    "EOB": ((2, 128, WIDE), F32),
     "GMB": ((2, 128, WIDE), F32),
     "EOO": ((4, 128, WIDE), F32),
     "GMO": ((4, 128, WIDE), F32),
@@ -958,7 +1041,6 @@
     "PR": ((ROWS, 128), F32),
     "PS": ((8, 128), F32),
     "SM": ((16, 16, 128), BF),
-    "DM": ((512, ROWS), BF),
     "CS": ((4, 128, WIDE), BF),
     "GC": ((ROWS, WIDE), BF),
     "XE": ((4, 128, WIDE), BF),
@@ -990,7 +1072,7 @@
 INS = ("tok", "cot", "pre", "idr", "gains", "qkv", "out", "router", "up", "down")
 IN_HBM = ("tok", "cot", "up", "down")
 OUT_HBM = ("block_out", "tokens_grad", "up_grad", "down_grad")
-SEMAPHORES = 208
+SEMAPHORES = 256
 
 
 def fused(args):
@@ -1020,6 +1102,33 @@
     )(*args)
 
 
+def copy_out(arrays):
+    n = len(arrays)
+
+    def body(*refs):
+        src, dst, held, sem = refs[:n], refs[n : 2 * n], refs[2 * n : 3 * n], refs[3 * n]
+        come = [pltpu.make_async_copy(src[i], held[i], sem.at[0, i]) for i in range(n)]
+        go = [pltpu.make_async_copy(held[i], dst[i], sem.at[1, i]) for i in range(n)]
+        for m in come:
+            m.start()
+        for i in range(n):
+            come[i].wait()
+            go[i].start()
+        for m in go:
+            m.wait()
+
+    hbm = pl.BlockSpec(memory_space=pl.ANY)
+    return pl.pallas_call(
+        body,
+        out_shape=[jax.ShapeDtypeStruct(a.shape, a.dtype) for a in arrays],
+        in_specs=[hbm] * n,
+        out_specs=[hbm] * n,
+        scratch_shapes=[pltpu.VMEM(a.shape, a.dtype) for a in arrays]
+        + [pltpu.SemaphoreType.DMA((2, n))],
+        name="outputs",
+    )(*arrays)
+
+
 def prepare(
     tokens, cotangent, prefix_len, expert_ids, norm_gains, qkv_weight, out_weight, router_weight, up_weight, down_weight
 ):
@@ -1028,7 +1137,7 @@
 
 
 def fast_device(*args):
-    outs = fused(prepare(*args))
+    outs = copy_out(fused(prepare(*args)))
     return tuple(outs[:8]) + (outs[8].reshape(()),)
 
 

time: 197 us -> 178 us (0.904)
  local copies, waits for them, and re-layouts: 8.52 us -> 0 us
  Pallas kernels: 185 us -> 177 us
    pallas_call x1, Pallas kernels: 185 us -> 172 us  [fused(): pl.pallas_call(body, out_shape=[jax.ShapeDtypeStruct(s, d) for s, d in OU...]
    unnamed x22 -> x0, local copies, waits for them, and re-layouts: 8.52 us -> none
    pallas_call x0 -> x1, Pallas kernels: none -> 4.84 us  [copy_out(): pl.pallas_call(body, out_shape=[jax.ShapeDtypeStruct(a.shape, a.dtype) fo...]
where the time goes in v5:
time: 178 us
  Pallas kernels  177 us (99%)
    pallas_call x1, Pallas kernels, fused(): pl.pallas_call(body, out_shape=[jax.ShapeDtypeStruct(s, d) for s, d in OU...  172 us
    pallas_call x1, Pallas kernels, copy_out(): pl.pallas_call(body, out_shape=[jax.ShapeDtypeStruct(a.shape, a.dtype) fo...  4.84 us

profile of v5, /device:TPU:0, one launch (start us, length us, event | category | flops | bytes accessed | tf_op | source)
XLA Modules:
  0.0 178.2 jit_solution(17489754018386955302)
XLA Ops:
  1.3 171.9 %block.1 = (bf16[512,768]{1,0:T(8,128)(2,1)}, f32[512,768]{1,0:T(8,128)}, f32[2,48]{1,0:T(2,128)}, f32[3,48,384]{2,1,0:T(8,128)}, f32[48,384]{1,0:T(8,128)}, /*i...) custom-call(bf16[512,768]{1,0:T(8,128)(2,1)} %refs_0_.1, ...), custom_call_target="tpu_custom_call" | custom-call | tf_op jit(solution)/shard_map/block/pallas_call | solution.py:1091
  173.2 4.8 %outputs.1 = (bf16[512,768]{1,0:T(8,128)(2,1)}, f32[512,768]{1,0:T(8,128)}, f32[2,48]{1,0:T(2,128)}, f32[3,48,384]{2,1,0:T(8,128)}, f32[48,384]{1,0:T(8,128)}, /...) custom-call(bf16[512,768]{1,0:T(8,128)(2,1)} %get-tuple-element.27.refs_0_, ...), custom_call_target="tpu_custom_call" | custom-call | tf_op jit(solution)/shard_map/outputs/pallas_call | solution.py:1121

commit v6 on v5

--- a/solution.py
+++ b/solution.py
@@ -57,6 +57,9 @@
     def zfrom(self, k):
         return lax.rem(self.z + 4 - k, 4)
 
+    def plane(self, z):
+        return {"fsdp": 4 * z + self.c, "tensor": self.t}
+
     def Z(self, k):
         return {"fsdp": 4 * self.zto(k) + self.c, "tensor": self.t}
 
@@ -158,50 +161,65 @@
     enter(pc)
     own = pl.ds(pl.multiple_of(t * 512, 512), 512)
     i_tok, i_cot, i_wo, i_att = w.ids(1), w.ids(1), w.ids(1), w.ids(3)
-    i_z, i_sz = w.ids(4), w.ids(4)
-    i_x, i_y, i_fx, i_fy, i_sx, i_sy, i_sf = (w.ids(4) for _ in range(7))
-    i_mz = w.ids(24)
+    i_up, i_dn, i_sz, i_s = w.ids(3) - 1, w.ids(3) - 1, w.ids(3) - 1, w.ids(3)
+    i_x, i_y, i_fx, i_fy = (w.ids(4) for _ in range(4))
+    i_mz = w.ids(18) - 1
     i_m = [w.ids(3) for _ in range(6)]
-    i_cz, i_dz, i_cp, i_dp = w.ids(4), w.ids(4), w.ids(4), w.ids(4)
-
-    zs = [w.go(i_sz + k, R.SM.at[f], R.SM.at[f], pc.Z(k)) for k in (1, 2, 3)]
-    za = [w.go(i_z + k, R.WA.at[z, c], R.WA.at[z, c], pc.Z(k)) for k in (1, 2, 3)]
+    i_cz, i_dz, i_cp, i_dp = w.ids(3) - 1, w.ids(3) - 1, w.ids(4), w.ids(4)
+
+    SM = R.SM.reshape(4, 4, 16, 128)
+    zs = [w.go(i_sz + k, SM.at[z, c], SM.at[z, c], pc.Z(k)) for k in (1, 2, 3)]
+
+    def up(d):
+        block = R.WA.at[z - d + 1, c]
+        return w.copy(i_up + d, block, block, pc.plane(z + 1))
+
+    def down(d):
+        block = R.WA.at[z + d - 1, c]
+        return w.copy(i_dn + d, block, block, pc.plane(z - 1))
+
+    def spread(zz):
+        block = R.WA.at[zz, c]
+        return w.copy(i_x + zz, block, block, pc.X), w.copy(i_y + zz, block, block, pc.Y)
+
+    def forward(zz):
+        a = R.WA.at[zz, pc.cx, pl.ds(0, 2)]
+        b = R.WA.at[zz, pc.cy, pl.ds(2, 2)]
+        return w.copy(i_fx + zz, a, a, pc.Y), w.copy(i_fy + zz, b, b, pc.X)
+
+    def start_all(copies):
+        for m in copies:
+            m.start()
+
+    def pass_on(zz):
+        for m in spread(zz):
+            m.wait_recv()
+        start_all(forward(zz))
+
+    def stage(d):
+        @pl.when(z >= d)
+        def _():
+            w.copy(i_up + d, R.WA.at[z, c], R.WA.at[z, c], pc.plane(z - 1)).wait_recv()
+            start_all(spread(z - d))
+            if d < 3:
+                pl.when(z < 3)(lambda: up(d + 1).start())
+
+        @pl.when(z + d <= 3)
+        def _():
+            w.copy(i_dn + d, R.WA.at[z, c], R.WA.at[z, c], pc.plane(z + 1)).wait_recv()
+            start_all(spread(z + d))
+            if d < 3:
+                pl.when(z > 0)(lambda: down(d + 1).start())
+
+    def pass_on_stage(d):
+        pl.when(z >= d)(lambda: pass_on(z - d))
+        pl.when(z + d <= 3)(lambda: pass_on(z + d))
+
+    pl.when(z < 3)(lambda: up(1).start())
+    pl.when(z > 0)(lambda: down(1).start())
+    start_all(spread(z))
     cot_x = w.go(i_cot, R.cot, R.CT.at[own], pc.PAIR)
     tok_x = w.go(i_tok, R.tok, R.TK.at[own], pc.PAIR)
-
-    def spread(k):
-        zz = pc.zfrom(k)
-        g = 4 * zz + c
-        d = w.go(i_sx + k, R.SM.at[g], R.SM.at[g], pc.X)
-        e = w.go(i_sy + k, R.SM.at[g], R.SM.at[g], pc.Y)
-        a = w.go(i_x + k, R.WA.at[zz, c], R.WA.at[zz, c], pc.X)
-        b = w.go(i_y + k, R.WA.at[zz, c], R.WA.at[zz, c], pc.Y)
-        return a, b, d, e
-
-    def forward(k, got):
-        zz = pc.zfrom(k)
-        a, b, d, e = got
-        d.wait_recv()
-        g = 4 * zz + pc.cx
-        s = w.go(i_sf + k, R.SM.at[g], R.SM.at[g], pc.Y)
-        a.wait_recv()
-        x = w.go(
-            i_fx + k,
-            R.WA.at[zz, pc.cx, pl.ds(0, 2)],
-            R.WA.at[zz, pc.cx, pl.ds(0, 2)],
-            pc.Y,
-        )
-        b.wait_recv()
-        y = w.go(
-            i_fy + k,
-            R.WA.at[zz, pc.cy, pl.ds(2, 2)],
-            R.WA.at[zz, pc.cy, pl.ds(2, 2)],
-            pc.X,
-        )
-        e.wait_recv()
-        return x, y, s
-
-    got = {0: spread(0)}
     local = [
         pltpu.make_async_copy(R.tok, R.TK.at[own], R.ls.at[0]),
         pltpu.make_async_copy(R.cot, R.CT.at[own], R.ls.at[1]),
@@ -220,10 +238,8 @@
     want = lax.div(r, 128) * 256 + lax.rem(r, 128) + 128 * t
     R.ACT[0:512, 0:ROWS] = (key.astype(jnp.int32) == want).astype(F32).astype(BF)
 
-    za[0].wait_recv()
-    zs[0].wait_recv()
-    got[1] = spread(1)
-    ends = [forward(0, got[0])]
+    stage(1)
+    pass_on(z)
     for m in local:
         m.wait()
     cot_x.wait_recv()
@@ -235,9 +251,12 @@
     lax.fori_loop(0, 4, cot_rows, 0)
     R.CR[z, t] = R.CQ[z]
     w.copy(i_cp, R.CR.at[z, t], R.CR.at[z, t], pc.PAIR).start()
-    za[1].wait_recv()
-    zs[1].wait_recv()
-    got[2] = spread(2)
+    stage(2)
+    for m in zs:
+        m.wait_recv()
+    mine = SM.at[:, c]
+    sx, sy = w.go(i_s, mine, mine, pc.X), w.go(i_s + 1, mine, mine, pc.Y)
+    pass_on_stage(1)
 
     def chunk(j):
         return pl.ds(pl.multiple_of(j * 512, 128), 512)
@@ -245,9 +264,9 @@
     def from_plane(j):
         out = []
         for k in (1, 3, 2):
-            to, cols, i = pc.zto(k), chunk(j), i_mz + 8 * j + k
+            to, cols, i = pc.zto(k), chunk(j), i_mz + 6 * j + k
             out.append(w.copy(i, R.up.at[to, :, cols], R.UE.at[z, c, :, cols], pc.Z(k)))
-            out.append(w.copy(i + 4, R.down.at[to, :, cols], R.DE.at[z, c, :, cols], pc.Z(k)))
+            out.append(w.copy(i + 3, R.down.at[to, :, cols], R.DE.at[z, c, :, cols], pc.Z(k)))
         return out
 
     def moe_spread(j):
@@ -288,14 +307,14 @@
         for m in cz:
             m.start()
 
+    cz = [w.copy(i_cz + k, R.CQ.at[pc.zto(k)], R.CR.at[z, t], pc.Z(k)) for k in (1, 3, 2)]
+    stage(3)
     start_plane(0)
-    cz = [w.copy(i_cz + k, R.CQ.at[pc.zto(k)], R.CR.at[z, t], pc.Z(k)) for k in (1, 3, 2)]
-    ends.append(forward(1, got[1]))
-    za[2].wait_recv()
-    zs[2].wait_recv()
-    got[3] = spread(3)
-    ends.append(forward(2, got[2]))
-    ends.append(forward(3, got[3]))
+    sx.wait_recv()
+    theirs = SM.at[:, pc.cx]
+    sf = w.go(i_s + 2, theirs, theirs, pc.Y)
+    pass_on_stage(2)
+    pass_on_stage(3)
     start_plane(1)
     agenda = {
         (0, 3): lambda: start_spread(1),
@@ -311,8 +330,8 @@
         R.STAT[rows, 0:1] = lax.rsqrt(jnp.mean(x * x, axis=1, keepdims=True) + norm_eps)
 
     blocks(ROWS, 128, factors)
-    for x, y, s in ends:
-        s.wait_recv()
+    sy.wait_recv()
+    sf.wait_recv()
     parts = [R.SM[g].astype(F32)[:, 0:48] for g in range(16)]
     vecs = jnp.concatenate(parts, axis=1)
     R.VEC[...] = vecs
@@ -335,9 +354,14 @@
         R.NM[rows] = (x * R.STAT[rows, 0:1] * R.VEC[0:1]).astype(BF)
 
     blocks(ROWS, 128, norm_one)
-    for x, y, s in ends:
-        x.wait_recv()
-        y.wait_recv()
+    for zz in range(4):
+        for m in spread(zz):
+            m.wait_send()
+        for m in forward(zz):
+            m.wait()
+    for d in (1, 2, 3):
+        pl.when((z < 3) & (z >= d - 1))(lambda: up(d).wait_send())
+        pl.when((z > 0) & (z + d - 1 <= 3))(lambda: down(d).wait_send())
     wo = w.go(i_wo, R.WA.at[:, :, 3], R.WO, pc.PAIR)
 
     start_spread(0)
@@ -446,7 +470,7 @@
 class ExpertSums:
     def __init__(self, R, pc, w):
         self.R, self.pc, self.w = R, pc, w
-        self.i1, self.i2, self.i3 = w.ids(16), w.ids(8), w.ids(32)
+        self.i1, self.i2, self.i3 = w.ids(16), w.ids(8), w.ids(24) - 1
 
     def cols(self, g):
         return pl.ds(pl.multiple_of(384 * g, 128), 384)
@@ -471,11 +495,11 @@
 
     def step_three(self, g):
         R, pc, w = self.R, self.pc, self.w
-        cols, i, out = self.cols(g), self.i3 + 8 * g, []
+        cols, i, out = self.cols(g), self.i3 + 6 * g, []
         for k in (1, 2, 3):
             to, z = pc.zto(k), pc.z
             out.append(w.copy(i + k, R.UE.at[to, pc.c, :, cols], R.ZU.at[z, :, cols], pc.Z(k)))
-            out.append(w.copy(i + 4 + k, R.DE.at[to, pc.c, :, cols], R.ZD.at[z, :, cols], pc.Z(k)))
+            out.append(w.copy(i + 3 + k, R.DE.at[to, pc.c, :, cols], R.ZD.at[z, :, cols], pc.Z(k)))
         return out
 
     def one(self, g):
@@ -534,7 +558,7 @@
 class AttentionSums:
     def __init__(self, R, pc, w):
         self.R, self.pc, self.w = R, pc, w
-        self.i1, self.i2, self.i3 = w.ids(16), w.ids(8), w.ids(16)
+        self.i1, self.i2, self.i3 = w.ids(16), w.ids(8), w.ids(12) - 1
         self.low, self.high = pl.ds(0, 2), pl.ds(2, 2)
 
     def step_one(self, n):
@@ -554,7 +578,7 @@
         ]
 
     def step_three(self, n):
-        R, pc, w, i = self.R, self.pc, self.w, self.i3 + 4 * n
+        R, pc, w, i = self.R, self.pc, self.w, self.i3 + 3 * n
         return [
             w.copy(i + k, R.AG.at[n, pc.zto(k), pc.c], R.ZA.at[n, pc.z], pc.Z(k))
             for k in (1, 2, 3)
@@ -605,7 +629,7 @@
 def phase_b(R, pc, w, i_dz, i_dp, i_cz, i_cp, weights_here):
     f, t, z, c, o = pc.f, pc.t, pc.z, pc.c, pc.o
     i_xe, i_xg = w.ids(4), w.ids(4)
-    i_rg, i_re, i_rgp, i_rep = w.ids(4), w.ids(4), w.ids(1), w.ids(1)
+    i_rg, i_re, i_rgp, i_rep = w.ids(3) - 1, w.ids(3) - 1, w.ids(1), w.ids(1)
     lane = iota((256, 128), 1)
     row = jnp.sum(
         jnp.where(iota((16, WIDE), 0) == 2 + z, R.VEC[...], 0.0), axis=0, keepdims=True
@@ -775,7 +799,7 @@
     f, t, z, c, o = pc.f, pc.t, pc.z, pc.c, pc.o
     att = AttentionSums(R, pc, w)
     i_n = w.ids(1)
-    i_sp, i_sc, i_sz = w.ids(1), w.ids(4), w.ids(4)
+    i_sp, i_sc, i_sz = w.ids(1), w.ids(3), w.ids(3) - 1
     own = pl.ds(pl.multiple_of(t * 512, 512), 512)
     GH, GN = R.GH, R.EOO.reshape(512, WIDE)
     RG, RE = R.RG.reshape(ROWS, WIDE), R.RE.reshape(ROWS, WIDE)
@@ -1072,7 +1096,7 @@
 INS = ("tok", "cot", "pre", "idr", "gains", "qkv", "out", "router", "up", "down")
 IN_HBM = ("tok", "cot", "up", "down")
 OUT_HBM = ("block_out", "tokens_grad", "up_grad", "down_grad")
-SEMAPHORES = 256
+SEMAPHORES = 192
 
 
 def fused(args):

time: 178 us -> 176 us (0.989)
  Pallas kernels: 177 us -> 174 us
    pallas_call x1, Pallas kernels: 172 us -> 169 us  [fused(): pl.pallas_call(body, out_shape=[jax.ShapeDtypeStruct(s, d) for s, d in OU...]
where the time goes in v6:
time: 176 us
  Pallas kernels  174 us (99%)
    pallas_call x1, Pallas kernels, fused(): pl.pallas_call(body, out_shape=[jax.ShapeDtypeStruct(s, d) for s, d in OU...  169 us
    pallas_call x1, Pallas kernels, copy_out(): pl.pallas_call(body, out_shape=[jax.ShapeDtypeStruct(a.shape, a.dtype) fo...  4.84 us

profile of v6, /device:TPU:0, one launch (start us, length us, event | category | flops | bytes accessed | tf_op | source)
XLA Modules:
  0.0 175.7 jit_solution(8721247825633702684)
XLA Ops:
  1.3 169.4 %block.1 = (bf16[512,768]{1,0:T(8,128)(2,1)}, f32[512,768]{1,0:T(8,128)}, f32[2,48]{1,0:T(2,128)}, f32[3,48,384]{2,1,0:T(8,128)}, f32[48,384]{1,0:T(8,128)}, /*i...) custom-call(bf16[512,768]{1,0:T(8,128)(2,1)} %refs_0_.1, ...), custom_call_target="tpu_custom_call" | custom-call | tf_op jit(solution)/shard_map/block/pallas_call | solution.py:1115
  170.7 4.8 %outputs.1 = (bf16[512,768]{1,0:T(8,128)(2,1)}, f32[512,768]{1,0:T(8,128)}, f32[2,48]{1,0:T(2,128)}, f32[3,48,384]{2,1,0:T(8,128)}, f32[48,384]{1,0:T(8,128)}, /...) custom-call(bf16[512,768]{1,0:T(8,128)(2,1)} %get-tuple-element.27.refs_0_, ...), custom_call_target="tpu_custom_call" | custom-call | tf_op jit(solution)/shard_map/outputs/pallas_call | solution.py:1145

commit v7 on v6

--- a/solution.py
+++ b/solution.py
@@ -308,8 +308,8 @@
             m.start()
 
     cz = [w.copy(i_cz + k, R.CQ.at[pc.zto(k)], R.CR.at[z, t], pc.Z(k)) for k in (1, 3, 2)]
+    start_plane(0)
     stage(3)
-    start_plane(0)
     sx.wait_recv()
     theirs = SM.at[:, pc.cx]
     sf = w.go(i_s + 2, theirs, theirs, pc.Y)

time: 176 us -> 174 us (0.989)
  Pallas kernels: 174 us -> 172 us
    pallas_call x1, Pallas kernels: 169 us -> 168 us  [fused(): pl.pallas_call(body, out_shape=[jax.ShapeDtypeStruct(s, d) for s, d in OU...]
where the time goes in v7:
time: 174 us
  Pallas kernels  172 us (99%)
    pallas_call x1, Pallas kernels, fused(): pl.pallas_call(body, out_shape=[jax.ShapeDtypeStruct(s, d) for s, d in OU...  168 us
    pallas_call x1, Pallas kernels, copy_out(): pl.pallas_call(body, out_shape=[jax.ShapeDtypeStruct(a.shape, a.dtype) fo...  4.84 us

profile of v7, /device:TPU:0, one launch (start us, length us, event | category | flops | bytes accessed | tf_op | source)
XLA Modules:
  0.0 173.8 jit_solution(14612849653502771439)
XLA Ops:
  1.3 167.5 %block.1 = (bf16[512,768]{1,0:T(8,128)(2,1)}, f32[512,768]{1,0:T(8,128)}, f32[2,48]{1,0:T(2,128)}, f32[3,48,384]{2,1,0:T(8,128)}, f32[48,384]{1,0:T(8,128)}, /*i...) custom-call(bf16[512,768]{1,0:T(8,128)(2,1)} %refs_0_.1, ...), custom_call_target="tpu_custom_call" | custom-call | tf_op jit(solution)/shard_map/block/pallas_call | solution.py:1115
  168.8 4.8 %outputs.1 = (bf16[512,768]{1,0:T(8,128)(2,1)}, f32[512,768]{1,0:T(8,128)}, f32[2,48]{1,0:T(2,128)}, f32[3,48,384]{2,1,0:T(8,128)}, f32[48,384]{1,0:T(8,128)}, /...) custom-call(bf16[512,768]{1,0:T(8,128)(2,1)} %get-tuple-element.27.refs_0_, ...), custom_call_target="tpu_custom_call" | custom-call | tf_op jit(solution)/shard_map/outputs/pallas_call | solution.py:1145

commit v8 on v7

--- a/solution.py
+++ b/solution.py
@@ -28,12 +28,12 @@
     return lax.broadcasted_iota(jnp.int32, shape, axis)
 
 
-def blocks(count, size, body):
+def blocks(count, size, body, unroll=1):
     def step(i, carry):
         body(pl.ds(pl.multiple_of(i * size, size), size))
         return carry
 
-    lax.fori_loop(0, count // size, step, 0)
+    lax.fori_loop(0, count // size, step, 0, unroll=unroll)
 
 
 class Place:
@@ -319,7 +319,8 @@
     agenda = {
         (0, 3): lambda: start_spread(1),
         (1, 1): lambda: start_forward(0),
-        (2, 1): both(lambda: start_spread(2), start_cot),
+        (1, 3): start_cot,
+        (2, 1): lambda: start_spread(2),
         (2, 3): lambda: start_forward(1),
     }
 
@@ -440,7 +441,7 @@
         R.PR[rows] = pr
         R.PS[0:1] = R.PS[0:1] + jnp.sum(pr, axis=0, keepdims=True)
 
-    blocks(ROWS, 256, out_block)
+    blocks(ROWS, 256, out_block, 2)
 
     def moe_rows(i, carry):
         k = order(lax.rem(i + 1, 4))
@@ -778,7 +779,7 @@
         R.SB[...] += mine * mm(aux, moe, 0, 0)
         return carry
 
-    lax.fori_loop(0, 4, prepared, 0)
+    lax.fori_loop(0, 4, prepared, 0, unroll=2)
     sums.two(0)
     sums.one(2)
     for k in (1, 3, 2):
@@ -840,7 +841,7 @@
         return carry
 
     R.G2[...] = jnp.zeros((8, WIDE), F32)
-    lax.fori_loop(0, 4, residual, 0)
+    lax.fori_loop(0, 4, residual, 0, unroll=2)
     part = jnp.where(iota((16, WIDE), 0) == 1, R.G2[0:1], 0.0)
     sums6 = jnp.concatenate([0.5 * R.PS[0:1], jnp.zeros((1, WIDE - 128), F32)], axis=1)
     keep = (iota((16, WIDE), 0) >= 2) & (iota((16, WIDE), 0) < 6)

time: 174 us -> 173 us (level)
  no operation moved by 1% of the time
where the time goes in v8:
time: 173 us
  Pallas kernels  171 us (99%)
    pallas_call x1, Pallas kernels, fused(): pl.pallas_call(body, out_shape=[jax.ShapeDtypeStruct(s, d) for s, d in OU...  166 us
    pallas_call x1, Pallas kernels, copy_out(): pl.pallas_call(body, out_shape=[jax.ShapeDtypeStruct(a.shape, a.dtype) fo...  4.84 us

profile of v8, /device:TPU:0, one launch (start us, length us, event | category | flops | bytes accessed | tf_op | source)
XLA Modules:
  0.0 172.7 jit_solution(638842983498869138)
XLA Ops:
  1.3 166.4 %block.1 = (bf16[512,768]{1,0:T(8,128)(2,1)}, f32[512,768]{1,0:T(8,128)}, f32[2,48]{1,0:T(2,128)}, f32[3,48,384]{2,1,0:T(8,128)}, f32[48,384]{1,0:T(8,128)}, /*i...) custom-call(bf16[512,768]{1,0:T(8,128)(2,1)} %refs_0_.1, ...), custom_call_target="tpu_custom_call" | custom-call | tf_op jit(solution)/shard_map/block/pallas_call | solution.py:1116
  167.7 4.8 %outputs.1 = (bf16[512,768]{1,0:T(8,128)(2,1)}, f32[512,768]{1,0:T(8,128)}, f32[2,48]{1,0:T(2,128)}, f32[3,48,384]{2,1,0:T(8,128)}, f32[48,384]{1,0:T(8,128)}, /...) custom-call(bf16[512,768]{1,0:T(8,128)(2,1)} %get-tuple-element.27.refs_0_, ...), custom_call_target="tpu_custom_call" | custom-call | tf_op jit(solution)/shard_map/outputs/pallas_call | solution.py:1146
